TPU v7x, 32 devices: a whole 2x2x4 slice. The times are simulated.
32 devices in a mesh: ax: 8 (over z, x), az: 4 (over y, core).
Axes of the slice: x: 2, y: 2, z: 4, core: 2. Of those that a mesh axis runs over, the one named last changes fastest.
Arguments:
- conserved: float32 [5, 64, 1024, 128], P(None, 'ax', 'az'), may hold values from -0.6 to 3, as said below
- panel_cells: int32 [16384], P(('ax', 'az')), may hold values from 0 to 262143
- panel_counts: int32 [32], P(('ax', 'az')), may hold values from 1 to 512, 8192 in all
- time_bins: int32 [16384, 64], P(('ax', 'az')), may hold values from 0 to 1023
- amplitudes: float32 [16384, 64], P(('ax', 'az')), may hold values from 0.5 to 2
Outputs:
- section: float32 [5, 64, 1024, 128], P(None, 'ax', 'az')
- signal: float32 [64, 1024], P(None, ('ax', 'az'))
Inputs may be any that keep to these rules, and one draw needn't show every extreme that they name: `conserved`: component 0 lies in 0.7 to 1.3, components 1 to 3 in -0.6 to 0.6, component 4 in 2.0 to 3.0. `panel_counts`: some device has exactly 512 live panel slots, each device at least one.
All inputs are finite; a program needn't handle non-finite values.
Results may differ from a plain program's by a relative error of at most 0.000076.
Values sent between devices are 32-bit elements; how exact they have to be, the bound alone decides.
No kernel may reach another device: no remote copies, remote signals or barrier semaphores. Data moves between devices by JAX's collectives and lax.ppermute only.
A program may use at most 128 MiB of HBM per device.

v0:
```python
import math

import jax
import jax.numpy as jnp
from jax import lax
from jax.sharding import PartitionSpec as P

AZIMUTH = 1024
CYCLES = 8
OBSERVERS = 64
BINS = 1024


gas_factor = 0.4
time_step = 0.02
ref_pressure = 0.95


def padded_2(value, sides, width, wrap):
    for axis, dim in sides:
        size, length = (lax.axis_size(axis), value.shape[dim])
        up = [(i, (i + 1) % size) for i in range(size if wrap else size - 1)]
        down = [(j, i) for i, j in up]
        last = lax.slice_in_dim(value, length - width, length, axis=dim)
        leading = lax.slice_in_dim(value, 0, width, axis=dim)
        before = lax.ppermute(last, axis, up)
        after = lax.ppermute(leading, axis, down)
        value = jnp.concatenate([before, value, after], axis=dim)
    return value


def primitives(conserved):
    fluid_rho_value = conserved[0]
    axial_vel = conserved[1] / fluid_rho_value
    radial_vel = conserved[2] / fluid_rho_value
    swirl_vel = conserved[3] / fluid_rho_value
    kinetic = 0.5 * (
        conserved[1] * axial_vel + conserved[2] * radial_vel + conserved[3] * swirl_vel
    )
    thermo_stress_level = gas_factor * (conserved[4] - kinetic)
    return jnp.stack([fluid_rho_value, axial_vel, radial_vel, swirl_vel, thermo_stress_level])


def flux_along(primitive, stream_heading):
    fluid_rho_value = primitive[0]
    thermo_stress_level = primitive[4]
    stream_speed = [primitive[1], primitive[2], primitive[3]]
    overall_heat_work = thermo_stress_level / gas_factor + 0.5 * fluid_rho_value * (
        stream_speed[0] * stream_speed[0]
        + stream_speed[1] * stream_speed[1]
        + stream_speed[2] * stream_speed[2]
    )
    holder_buffer = stream_speed[stream_heading]
    divided_pieces = [fluid_rho_value * holder_buffer]
    for entry_number in range(3):
        forcing_contribution = fluid_rho_value * stream_speed[entry_number] * holder_buffer
        if entry_number == stream_heading:
            forcing_contribution = forcing_contribution + thermo_stress_level
        divided_pieces.append(forcing_contribution)
    divided_pieces.append((overall_heat_work + thermo_stress_level) * holder_buffer)
    return jnp.stack(divided_pieces)


def fourth_diff(padded, along_axis, length):
    near_diff = lax.slice_in_dim(padded, 3, length + 3, axis=along_axis) - lax.slice_in_dim(
        padded, 1, length + 1, axis=along_axis
    )
    far_diff = lax.slice_in_dim(padded, 4, length + 4, axis=along_axis) - lax.slice_in_dim(
        padded, 0, length, axis=along_axis
    )
    return (8.0 * near_diff - far_diff) / 12.0


def cycle_weights(length):
    modes = jnp.arange(length // 2 + 1).astype(jnp.float32)
    cutoff = 4.0 * (jnp.arange(CYCLES).astype(jnp.float32) + 1.0)
    return jnp.exp(-((modes[None, :] / cutoff[:, None]) ** 8))


def apply_filter(line_block, cycle_index, length):
    half = length // 2 + 1
    sample = jnp.arange(length)
    modes = jnp.arange(half)
    phase = (sample[:, None] * modes[None, :] % length).astype(jnp.float32) * (
        2.0 * math.pi / length
    )
    cos_table = jnp.cos(phase)
    sin_table = jnp.sin(phase)
    factor = jnp.where((modes == 0) | (modes == length // 2), 1.0, 2.0) / length
    selector = (cycle_index[:, None] == jnp.arange(CYCLES)[None, :]).astype(jnp.float32)
    line_weight = (
        jnp.dot(selector, cycle_weights(length), precision=lax.Precision.HIGHEST) * factor[None, :]
    )
    real_part = jnp.einsum("fln,nm->flm", line_block, cos_table, precision=lax.Precision.HIGHEST)
    imag_part = jnp.einsum("fln,nm->flm", line_block, sin_table, precision=lax.Precision.HIGHEST)
    smooth = jnp.einsum(
        "flm,nm->fln", real_part * line_weight[None], cos_table, precision=lax.Precision.HIGHEST
    )
    smooth = smooth + jnp.einsum(
        "flm,nm->fln", imag_part * line_weight[None], sin_table, precision=lax.Precision.HIGHEST
    )
    return smooth


def on_device(conserved, panel_cells, panel_counts, time_bins, amplitudes):
    planes_dev = conserved.shape[1]
    sector = conserved.shape[2]
    radial_all = conserved.shape[3]
    primitive = primitives(conserved)
    radius = jnp.arange(radial_all).astype(jnp.float32) + 0.5
    dtheta = 2.0 * math.pi / AZIMUTH
    prims_x = padded_2(primitive, (("ax", 1),), 2, False)
    prims_t = padded_2(primitive, (("az", 2),), 2, True)
    padded_x = flux_along(prims_x, 0)
    padded_t = flux_along(prims_t, 2)
    radial_flux = flux_along(primitive, 1)
    padded_r = jnp.pad(radial_flux * radius, ((0, 0), (0, 0), (0, 0), (2, 2)))
    tendency = -fourth_diff(padded_x, 1, planes_dev)
    tendency = tendency - fourth_diff(padded_r, 3, radial_all) / radius
    tendency = tendency - fourth_diff(padded_t, 2, sector) / (radius * dtheta)
    fluid_rho_value = primitive[0]
    radial_vel = primitive[2]
    swirl_vel = primitive[3]
    thermo_stress_level = primitive[4]
    zeros_field = jnp.zeros_like(fluid_rho_value)
    source = jnp.stack(
        [
            zeros_field,
            zeros_field,
            (thermo_stress_level + fluid_rho_value * swirl_vel * swirl_vel) / radius,
            -fluid_rho_value * radial_vel * swirl_vel / radius,
            zeros_field,
        ]
    )
    raw_section = conserved + time_step * (tendency + source)
    inner = raw_section[..., :CYCLES]
    lines = jnp.transpose(inner, (0, 1, 3, 2)).reshape(5, planes_dev * CYCLES, sector)
    line_block = lax.all_to_all(lines, "az", split_axis=1, concat_axis=2, tiled=True)
    line_count = line_block.shape[1]
    cycle_index = (lax.axis_index("az") * line_count + jnp.arange(line_count)) % CYCLES
    smooth = apply_filter(line_block, cycle_index, AZIMUTH)
    filtered = lax.all_to_all(smooth, "az", split_axis=2, concat_axis=1, tiled=True)
    filtered = jnp.transpose(filtered.reshape(5, planes_dev, CYCLES, sector), (0, 1, 3, 2))
    section = jnp.concatenate([filtered, raw_section[..., CYCLES:]], axis=3)
    slot_count = panel_cells.shape[0]
    live = jnp.arange(slot_count) < panel_counts[0]
    sampled = jnp.where(live, thermo_stress_level.reshape(-1)[panel_cells] - ref_pressure, 0.0)
    contrib = sampled[:, None] * amplitudes
    segment = jnp.arange(OBSERVERS)[None, :] * BINS + time_bins
    partial_signal = jax.ops.segment_sum(
        contrib.reshape(-1), segment.reshape(-1), num_segments=OBSERVERS * BINS
    )
    signal = lax.psum_scatter(
        partial_signal.reshape(OBSERVERS, BINS), ("ax", "az"), scatter_dimension=1, tiled=True
    )
    return (section, signal)


def solution(mesh):
    placed = (
        P(None, "ax", "az", None),
        P(("ax", "az")),
        P(("ax", "az")),
        P(("ax", "az"), None),
        P(("ax", "az"), None),
    )
    return jax.shard_map(
        on_device,
        mesh=mesh,
        in_specs=placed,
        out_specs=(P(None, "ax", "az", None), P(None, ("ax", "az"))),
        check_vma=False,
    )
```

profile of v0, /device:TPU:0, one launch (start us, length us, event | category | flops | bytes accessed | tf_op | source)
XLA Modules:
  0.0 418.5 jit_solution(17199372925297992057)
XLA Ops:
  7.2 5.9 %copy.67 = f32[5,8,256,128]{2,3,1,0:T(8,128)} copy(f32[5,8,256,128]{3,2,1,0:T(8,128)} %param.5) | data formatting | bytes 10485760 | tf_op args[0]
  19.0 3.8 multiply_dynamic-update-slice_fusion.8
  25.1 2.5 copy.74
  27.6 2.6 copy.75
  30.2 2.6 copy.76
  32.7 2.6 copy.77
  35.3 2.6 copy.78
  38.6 4.0 fusion.46
  42.6 6.1 %gather_fusion = f32[512]{0:T(512)S(1)} fusion(f32[262144]{0:T(1024)} %fusion.46, s32[1024]{0:T(1024)S(1)} %pad_clamp_fusion), kind=kCustom, calls=%fused_computation | custom fusion | bytes 6144 | tf_op jit(solution)/shard_map/gather | solution.py:147
  50.8 172.0 %scatter_custom_fusion = f32[65536]{0:T(1024)} fusion(s32[32768]{0:T(1024)S(1)} %reshape.97, f32[32768]{0:T(1024)} %reshape.99, f32[]{:T(128)} %constant.32.clone.1), kind=kCustom, calls=%fused_computation.76 | custom fusion | flops 32768 | bytes 262656 | tf_op jit(solution)/shard_map/scatter-add | solution.py:150
  229.4 3.2 fusion.75
  232.5 5.9 %collective-permute-start = (f32[5,2,256,128]{2,3,1,0:T(8,128)}, f32[5,2,256,128]{2,3,1,0:T(8,128)}, u32[]{:S(2)}, u32[]{:S(2)}) collective-permute-start(f32[5,2,256,128]{2,3,1,0:T(8,128)} %get-tuple-element.26), channel_id=1, source_target_pairs={{0,4},{4,8},{8,12},{12,16},{16,20},{20,24},{24,28},{1,5},{5,9},{9,... | collective-permute-start | bytes 3932168 | tf_op jit(solution)/shard_map/ppermute | solution.py:26
  239.8 3.3 fusion.76
  250.3 5.7 %broadcast_multiply_fusion = f32[5,8,256,128]{2,3,1,0:T(8,128)} fusion(f32[5,8,256,128]{2,3,1,0:T(8,128)} %copy-done.5, f32[128]{0:T(128)S(1)} %convert_add_fusion), kind=kLoop, calls=%fused_computation.26 | loop fusion | flops 1310720 | bytes 10486272 | tf_op jit(solution)/shard_map/mul | solution.py:117
  260.8 6.0 %pad_maximum_fusion.1 = f32[5,8,260,128]{2,3,1,0:T(8,128)S(1)} fusion(f32[5,8,2,128]{2,3,1,0:T(8,128)} %copy.66, f32[5,8,256,128]{2,3,1,0:T(8,128)} %multiply_dynamic-update-slice_fusion.12, f32[5,8,2,128]{2,3,1,0:T(8,128)} %copy.65), kind=kLoop, calls=%fused_computation.3 | loop fusion | flops 2662400 | bytes 10649600 | tf_op jit(solution)/shard_map/concatenate | solution.py:28
  268.3 26.4 %collective-permute-done = f32[5,2,256,128]{2,3,1,0:T(8,128)} collective-permute-done((f32[5,2,256,128]{2,3,1,0:T(8,128)}, f32[5,2,256,128]{2,3,1,0:T(8,128)}, u32[]{:S(2)}, u32[]{:S(2)}) %collective-permute-start) | collective-permute-done | bytes 1310752 | tf_op jit(solution)/shard_map/ppermute | solution.py:26
  299.0 3.6 copy-done.2
  302.9 17.6 %fusion.6 = f32[5,8,256,128]{2,3,1,0:T(8,128)} fusion(f32[5,8,256,128]{2,3,1,0:T(8,128)S(1)} %bitcast.46, f32[5,8,260,128]{2,3,1,0:T(8,128)S(1)} %multiply_dynamic-update-slice_fusion, f32[5,12,256,128]{2,3,1,0:T(8,128)} %copy-done.2, f32[1,8,256,128]{2,3,1,0:T(8,128)} %get-tuple-element.19, f32[1,8,256,128]{2,3,1,0:T(8,128)S(1)} %copy-done.6, ...), kind=kLoop, calls=%fused_computation.11 | loop fusion | flops 34078720 | bytes 59769896 | tf_op jit(solution)/shard_map/add | solution.py:135
  322.5 3.6 all-to-all-start
  326.4 8.5 %all-to-all-done = f32[5,64,256]{2,0,1:T(8,128)S(1)} async-done(((f32[5,64,256]{2,0,1:T(8,128)}), f32[5,64,256]{2,0,1:T(8,128)S(1)}, u32[]{:S(2)}, u32[]{:S(2)}) %all-to-all-start) | async-done | bytes 327712 | tf_op jit(solution)/shard_map/all_to_all | solution.py:138
  335.3 10.0 %fusion.33 = f32[5,16,513]{2,1,0:T(8,128)S(1)} fusion(f32[5,16,1024]{2,1,0:T(8,128)S(1)} %all_to_all.27, f32[16,513]{1,0:T(8,128)S(1)} %convolution_multiply_fusion), kind=kOutput, calls=%fused_computation.56 | convolution fusion | flops 511694912 | bytes 524672 | tf_op jit(solution)/shard_map/fln,nm->flm/dot_general | solution.py:95
  345.3 10.1 %fusion.30 = f32[5,16,513]{2,1,0:T(8,128)S(1)} fusion(f32[5,16,1024]{2,1,0:T(8,128)S(1)} %all_to_all.27, f32[16,513]{1,0:T(8,128)S(1)} %convolution_multiply_fusion), kind=kOutput, calls=%fused_computation.55 | convolution fusion | flops 511694912 | bytes 524672 | tf_op jit(solution)/shard_map/fln,nm->flm/dot_general | solution.py:94
  355.4 9.9 %fusion.16 = f32[5,16,1024]{2,1,0:T(8,128)S(1)} fusion(f32[5,16,513]{2,1,0:T(8,128)S(1)} %fusion.33), kind=kOutput, calls=%fused_computation.30 | convolution fusion | flops 511653888 | bytes 491840 | tf_op jit(solution)/shard_map/flm,nm->fln/dot_general | solution.py:99
  365.3 10.1 %fusion.27 = f32[5,16,1024]{2,1,0:T(8,128)S(1)} fusion(f32[5,16,1024]{2,1,0:T(8,128)S(1)} %fusion.16, f32[5,16,513]{2,1,0:T(8,128)S(1)} %fusion.30), kind=kOutput, calls=%fused_computation.54 | convolution fusion | flops 511735808 | bytes 819520 | tf_op jit(solution)/shard_map/flm,nm->fln/dot_general | solution.py:96
  375.4 2.6 copy.70
  378.0 3.5 reshape.112
  381.5 3.5 all-to-all-start.1
  385.0 5.2 %slice.165 = f32[5,8,256,120]{2,3,1,0:T(8,128)} slice(f32[5,8,256,128]{2,3,1,0:T(8,128)} %fusion.6), slice={[0:5], [0:8], [0:256], [8:128]} | slice | bytes 9830400 | tf_op jit(solution)/shard_map/slice | solution.py:144
  393.7 3.5 reshape.113
  397.2 2.6 copy.82
  399.9 5.4 %pad_maximum_fusion.2 = f32[5,8,256,128]{2,3,1,0:T(8,128)} fusion(f32[5,8,256,120]{2,3,1,0:T(8,128)} %slice.165, f32[5,8,256,8]{2,3,1,0:T(8,128)S(1)} %bitcast.58), kind=kLoop, calls=%fused_computation.21 | loop fusion | flops 1310720 | bytes 10485760 | tf_op jit(solution)/shard_map/concatenate | solution.py:144
  405.3 5.9 %copy.80 = f32[5,8,256,128]{3,2,1,0:T(8,128)} copy(f32[5,8,256,128]{2,3,1,0:T(8,128)} %pad_maximum_fusion.2) | data formatting | bytes 10485760
  (89 shorter events, 42.3 us)
Async XLA Ops:
  7.2 404.0 %reduce-scatter.4.cloned.1.call-start = ((), (), s32[]{:S(2)}) async-start(), calls=%async_computation.3 | async-start | bytes 540672
  14.9 3.1 copy-start
  18.7 4.1 copy-start.3
  22.7 2.4 copy-start.5
  32.7 5.2 %copy-start.8 = (s32[512]{0:T(512)S(1)}, s32[512]{0:T(512)}, u32[]{:S(2)}) copy-start(s32[512]{0:T(512)} %param.6) | copy-start | bytes 6148
  38.6 10.1 %copy-start.7 = (f32[512,64]{0,1:T(8,128)S(1)}, f32[512,64]{0,1:T(8,128)}, u32[]{:S(2)}) copy-start(f32[512,64]{0,1:T(8,128)} %param.9) | copy-start | bytes 393220
  226.0 2.3 copy-start.4
  229.4 10.4 %copy-start.1 = (f32[5,8,256,128]{2,3,1,0:T(8,128)S(1)}, f32[5,8,256,128]{2,3,1,0:T(8,128)}, u32[]{:S(2)}) copy-start(f32[5,8,256,128]{2,3,1,0:T(8,128)} %multiply_dynamic-update-slice_fusion.12) | copy-start | bytes 15728644
  232.5 62.2 %collective-permute-start = (f32[5,2,256,128]{2,3,1,0:T(8,128)}, f32[5,2,256,128]{2,3,1,0:T(8,128)}, u32[]{:S(2)}, u32[]{:S(2)}) collective-permute-start(f32[5,2,256,128]{2,3,1,0:T(8,128)} %get-tuple-element.26), channel_id=1, source_target_pairs={{0,4},{4,8},{8,12},{12,16},{16,20},{20,24},{24,28},{1,5},{5,9},{9,... | collective-permute-start | bytes 3932168 | tf_op jit(solution)/shard_map/ppermute | solution.py:26
  238.5 56.3 %collective-permute-start.1 = (f32[5,2,256,128]{2,3,1,0:T(8,128)S(1)}, f32[5,2,256,128]{2,3,1,0:T(8,128)}, u32[]{:S(2)}, u32[]{:S(2)}) collective-permute-start(f32[5,2,256,128]{2,3,1,0:T(8,128)S(1)} %get-tuple-element.27), channel_id=1, source_target_pairs={{4,0},{8,4},{12,8},{16,12},{20,16},{24,20},{28,24},{5,1},{9,5},{13... | collective-permute-start | bytes 3932168 | tf_op jit(solution)/shard_map/ppermute | solution.py:27
  245.6 10.6 %collective-permute-start.2 = (f32[5,8,2,128]{3,1,2,0:T(8,128)S(1)}, f32[5,8,2,128]{3,1,2,0:T(8,128)S(1)}, u32[]{:S(2)}, u32[]{:S(2)}) collective-permute-start(f32[5,8,2,128]{3,1,2,0:T(8,128)S(1)} %copy.63), channel_id=1, source_target_pairs={{0,1},{1,2},{2,3},{3,0},{4,5},{5,6},{6,7},{7,4},{8,9},{9,10},{10,1... | collective-permute-start | bytes 122888 | tf_op jit(solution)/shard_map/ppermute | solution.py:26
  248.1 10.4 %collective-permute-start.3 = (f32[5,8,2,128]{3,1,2,0:T(8,128)S(1)}, f32[5,8,2,128]{3,1,2,0:T(8,128)S(1)}, u32[]{:S(2)}, u32[]{:S(2)}) collective-permute-start(f32[5,8,2,128]{3,1,2,0:T(8,128)S(1)} %copy.64), channel_id=1, source_target_pairs={{1,0},{2,1},{3,2},{0,3},{5,4},{6,5},{7,6},{4,7},{9,8},{10,9},{11,1... | collective-permute-start | bytes 122888 | tf_op jit(solution)/shard_map/ppermute | solution.py:27
  267.5 27.3 %slice-start.2 = ((s8[5242880]{0:T(1024)(128)(4,1)}), s8[4194304]{0:T(1024)(128)(4,1)S(1)}, s32[]{:S(2)}) async-start(s8[5242880]{0:T(1024)(128)(4,1)} %bitcast.47), calls=%async_computation.6 | async-start | bytes 8388608
  267.7 27.1 %slice-start.3 = ((s8[5242880]{0:T(1024)(128)(4,1)}), s8[1048576]{0:T(1024)(128)(4,1)S(1)}, s32[]{:S(2)}) async-start(s8[5242880]{0:T(1024)(128)(4,1)} %bitcast.47), calls=%async_computation.7 | async-start | bytes 2097152
  298.0 4.7 %slice-start = ((s8[5242880]{0:T(1024)(128)(4,1)}), s8[4194304]{0:T(1024)(128)(4,1)S(1)}, s32[]{:S(2)}) async-start(s8[5242880]{0:T(1024)(128)(4,1)} %bitcast.45), calls=%async_computation.4 | async-start | bytes 8388608
  298.3 4.3 %slice-start.1 = ((s8[5242880]{0:T(1024)(128)(4,1)}), s8[1048576]{0:T(1024)(128)(4,1)S(1)}, s32[]{:S(2)}) async-start(s8[5242880]{0:T(1024)(128)(4,1)} %bitcast.45), calls=%async_computation.5 | async-start | bytes 2097152
  298.3 4.6 %copy-start.6 = (f32[1,8,256,128]{2,3,1,0:T(8,128)S(1)}, f32[1,8,256,128]{2,3,1,0:T(8,128)}, u32[]{:S(2)}) copy-start(f32[1,8,256,128]{2,3,1,0:T(8,128)} %get-tuple-element.18) | copy-start | bytes 3145732
  299.0 3.6 copy-start.2
  322.5 12.4 %all-to-all-start = ((f32[5,64,256]{2,0,1:T(8,128)}), f32[5,64,256]{2,0,1:T(8,128)S(1)}, u32[]{:S(2)}, u32[]{:S(2)}) async-start(f32[5,64,256]{2,0,1:T(8,128)} %copy.68), calls=%async_computation | async-start | bytes 1048576 | tf_op jit(solution)/shard_map/all_to_all | solution.py:138
  381.5 10.2 %all-to-all-start.1 = ((f32[4,1,20480]{2,1,0:T(1,128)}), f32[4,1,20480]{2,1,0:T(1,128)S(1)}, u32[]{:S(2)}, u32[]{:S(2)}) async-start(f32[4,1,20480]{2,1,0:T(1,128)} %reshape.112), calls=%async_computation.1 | async-start | bytes 655360 | tf_op jit(solution)/shard_map/all_to_all | solution.py:142
Sparse Core Ops, SparseCore 0:
  225.0 146.7 reduce-scatter.3
where the time goes:
time: 427 us; the launch traced here: 418 us
  other arithmetic  228 us (53%)
  local copies, waits for them, and re-layouts  81.1 us (19%)
  matrix products  40.2 us (9%)
  waiting for transfers between devices  36.6 us (9%)
  starting transfers between devices  16.6 us (4%)
  between operations  15.5 us (4%)
    scatter-add x1, other arithmetic, on_device(): jax.ops.segment_sum(contrib.reshape(-1), segment.reshape(-1), num_segment...  172 us
    unnamed x34, local copies, waits for them, and re-layouts  30.6 us
    ppermute x2, waiting for transfers between devices, padded_2(): before = lax.ppermute(last, axis, up)  26.4 us
    add x1, other arithmetic, on_device(): raw_section = conserved + time_step * (tendency + source)  17.6 us
    dot_general x1, matrix products, apply_filter(): jnp.einsum('fln,nm->flm', line_block, cos_table, precision=lax.Precision....  10.1 us
    dot_general x1, matrix products, apply_filter(): jnp.einsum('flm,nm->fln', real_part * line_weight[None], cos_table, preci...  10.1 us
    dot_general x1, matrix products, apply_filter(): jnp.einsum('fln,nm->flm', line_block, sin_table, precision=lax.Precision....  9.96 us
    dot_general x1, matrix products, apply_filter(): jnp.einsum('flm,nm->fln', imag_part * line_weight[None], sin_table, preci...  9.87 us
  transfers between devices with their start and end apart: 7, of which 3 were waited for; matrix products, arithmetic and copies ran while one was open for 31% of the time, Pallas kernels for 0%

commit v1 on v0

v1 whole, which is shorter than its diff:
```python
import functools
import math

import jax
import jax.numpy as jnp
import numpy as np
from jax import lax
from jax.experimental import pallas as pl
from jax.experimental.pallas import tpu as pltpu
from jax.sharding import PartitionSpec as P

CYCLES = 8
BINS = 1024
LOW_BINS = 32
FIELDS = 5
MODES = 8 * CYCLES
COEFS = 2 * MODES
ROWS = 8

gas_factor = 0.4
time_step = 0.02
ref_pressure = 0.95
VMEM_BYTES = 48 * 1024 * 1024

HIGHEST = lax.Precision.HIGHEST


def params(**more):
    return pltpu.CompilerParams(vmem_limit_bytes=VMEM_BYTES, **more)


def cost(flops, touched):
    return pl.CostEstimate(flops=flops, bytes_accessed=touched, transcendentals=0)


def basis_table(length):
    phase = (np.arange(length)[:, None] * np.arange(MODES)[None, :] % length) * (
        2.0 * math.pi / length
    )
    return np.concatenate([np.cos(phase), np.sin(phase)], axis=1).astype(np.float32)


def mode_weights(length):
    modes = np.arange(MODES).astype(np.float64)
    cutoff = 4.0 * (np.arange(CYCLES) + 1.0)
    weight = np.exp(-((modes[None, :] / cutoff[:, None]) ** 8))
    weight = weight * np.where(modes == 0, 1.0, 2.0)[None, :] / length
    return np.tile(np.concatenate([weight, weight], axis=1), (FIELDS, 1)).astype(np.float32)


def primitives(q):
    inverse = 1.0 / q[0]
    u, v, w = q[1] * inverse, q[2] * inverse, q[3] * inverse
    p = gas_factor * (q[4] - 0.5 * (q[1] * u + q[2] * v + q[3] * w))
    return u, v, w, p


def carried(q, p, speed, heading):
    flux = [q[0] * speed, q[1] * speed, q[2] * speed, q[3] * speed, (q[4] + p) * speed]
    flux[heading] = flux[heading] + p
    return flux


def inner_lanes(fields, lane):
    packed = jnp.where(lane < CYCLES, fields[0], 0.0)
    for f in range(1, FIELDS):
        here = (lane >= CYCLES * f) & (lane < CYCLES * (f + 1))
        packed = jnp.where(here, pltpu.roll(fields[f], CYCLES * f, 1), packed)
    return packed


def edge_kernel(up, q_ref, send_ref, inner_ref):
    sector, radial = q_ref.shape[2:]
    tail = sector * CYCLES // radial
    groups = radial // CYCLES - 1
    main = sector - tail
    scale = time_step / 12.0
    lane = lax.broadcasted_iota(jnp.int32, (1, radial), 1)

    def terms(start, size):
        rows = pl.ds(start, size)
        flux = []
        for plane in range(2):
            q = [q_ref[f, plane, rows, :] for f in range(FIELDS)]
            u, _, _, p = primitives(q)
            flux.append(carried(q, p, u, 1))
        near, far = (flux[1], flux[0]) if up else (flux[0], flux[1])
        whole, part = [], []
        for f in range(FIELDS):
            wide = scale * (8.0 * near[f] - far[f])
            narrow = scale * near[f]
            whole.append(wide if up else -wide)
            part.append(-narrow if up else narrow)
        slots = (whole, part) if up else (part, whole)
        for s in range(2):
            inner_ref[s, rows, :] = inner_lanes(slots[s], lane)
        return slots

    last = terms(main, tail)

    for g in range(groups):
        slots = terms(g * tail, tail)
        shift = radial - CYCLES * (g + 1)
        for s in range(2):
            for f in range(FIELDS):
                moved = pltpu.roll(last[s][f], shift, 1)
                send_ref[f, s, pl.ds(g * tail, tail), :] = jnp.where(
                    lane < CYCLES, moved, slots[s][f]
                )


def edge_terms(conserved, up):
    fields, planes, sector, radial = conserved.shape
    main = sector - sector * CYCLES // radial
    at = planes // 2 - 1 if up else 0
    return pl.pallas_call(
        functools.partial(edge_kernel, up),
        grid=(1,),
        in_specs=[pl.BlockSpec((fields, 2, sector, radial), lambda i: (0, at, 0, 0))],
        out_specs=[
            pl.BlockSpec((fields, 2, main, radial), lambda i: (0, 0, 0, 0)),
            pl.BlockSpec((2, sector, radial), lambda i: (0, 0, 0)),
        ],
        out_shape=[
            jax.ShapeDtypeStruct((fields, 2, main, radial), jnp.float32),
            jax.ShapeDtypeStruct((2, sector, radial), jnp.float32),
        ],
        compiler_params=params(),
        cost_estimate=cost(100 * 2 * sector * radial, 4 * 4 * fields * sector * radial),
        name="edge_up" if up else "edge_down",
    )(conserved)


def small_kernel(low_ref, high_ref, up_ref, down_ref, basis_ref, *outs):
    spec_up, spec_down, first_ref, last_ref = outs
    inner = FIELDS * CYCLES
    for y_ref, s_ref in ((up_ref, spec_up), (down_ref, spec_down)):
        for s in range(2):
            full = lax.dot_general(
                y_ref[s], basis_ref[...], (((0,), (0,)), ((), ())),
                precision=HIGHEST, preferred_element_type=jnp.float32,
            )
            s_ref[s] = full[:inner]
    planes = low_ref.shape[1]
    for ref, out, start in ((low_ref, first_ref, 0), (high_ref, last_ref, ROWS - 2)):
        for k in range(planes):
            q = [ref[f, k] for f in range(FIELDS)]
            _, _, w, p = primitives(q)
            flux = carried(q, p, w, 3)
            for f in range(FIELDS):
                out[f, 2 * k : 2 * k + 2, :] = flux[f][start : start + 2]


def small_terms(conserved, inner_up, inner_down, basis):
    fields, planes, sector, radial = conserved.shape
    end = sector // ROWS - 1
    edge = (fields, planes, ROWS, radial)
    spec = jax.ShapeDtypeStruct((2, FIELDS * CYCLES, COEFS), jnp.float32)
    ring = jax.ShapeDtypeStruct((fields, 2 * planes, radial), jnp.float32)
    zero3 = lambda i: (0, 0, 0)
    whole = pl.BlockSpec((2, sector, radial), zero3)
    return pl.pallas_call(
        small_kernel,
        grid=(1,),
        in_specs=[
            pl.BlockSpec(edge, lambda i: (0, 0, 0, 0)),
            pl.BlockSpec(edge, lambda i: (0, 0, end, 0)),
            whole,
            whole,
            pl.BlockSpec((sector, COEFS), lambda i: (0, 0)),
        ],
        out_specs=[
            pl.BlockSpec(spec.shape, zero3),
            pl.BlockSpec(spec.shape, zero3),
            pl.BlockSpec(ring.shape, zero3),
            pl.BlockSpec(ring.shape, zero3),
        ],
        out_shape=[spec, spec, ring, ring],
        compiler_params=params(),
        cost_estimate=cost(6 * 8 * sector * radial * COEFS, 10 * sector * radial * 4),
        name="small_terms",
    )(conserved, conserved, inner_up, inner_down, basis)


def panel_kernel(cells_ref, count_ref, row_ref, q_ref, bins_ref, amp_ref, out_ref, held):
    slots = row_ref.shape[1]
    radial = q_ref.shape[2]
    observers = bins_ref.shape[0]
    count = count_ref[0]
    width = 8

    def fetch(i, _):
        for k in range(width):
            s = i * width + k
            at = cells_ref[s] // radial
            held[:, pl.ds(s, 1), :] = q_ref[:, pl.ds(at, 1), :]
        return 0

    lax.fori_loop(0, (count + width - 1) // width, fetch, 0)
    q = [held[f] for f in range(FIELDS)]
    p = gas_factor * (q[4] - 0.5 * (q[1] * q[1] + q[2] * q[2] + q[3] * q[3]) / q[0])
    turned = jnp.transpose(p)
    which = lax.broadcasted_iota(jnp.int32, (radial, slots), 0)
    here = which == (row_ref[...] & (radial - 1))
    sampled = jnp.sum(jnp.where(here, turned, 0.0), axis=0, keepdims=True) - ref_pressure
    slot = lax.broadcasted_iota(jnp.int32, (1, slots), 1)
    sampled = jnp.where(slot < count, sampled, 0.0)

    contrib = sampled * amp_ref[...]
    first = contrib.astype(jnp.bfloat16).astype(jnp.float32)
    second = contrib - first
    bins = bins_ref[...]
    low = bins & (LOW_BINS - 1)
    high = bins // LOW_BINS
    each = 128 // LOW_BINS
    high_count = BINS // LOW_BINS
    low_iota = lax.broadcasted_iota(jnp.int32, (LOW_BINS, slots), 0)
    high_iota = lax.broadcasted_iota(jnp.int32, (high_count, slots), 0)
    lane = lax.broadcasted_iota(jnp.int32, (high_count, 128), 1)
    for g in range(observers // each):
        left, right = [], []
        for k in range(each):
            o = g * each + k
            hit = high_iota == high[o : o + 1]
            left.append(jnp.where(hit, first[o : o + 1], 0.0).astype(jnp.bfloat16))
            left.append(jnp.where(hit, second[o : o + 1], 0.0).astype(jnp.bfloat16))
            same = low_iota == low[o : o + 1]
            right.append(jnp.where(same, 1.0, 0.0).astype(jnp.bfloat16))
        sums = lax.dot_general(
            jnp.concatenate(left, axis=0),
            jnp.concatenate(right, axis=0),
            (((1,), (1,)), ((), ())),
            preferred_element_type=jnp.float32,
        )
        total = jnp.zeros((high_count, 128), jnp.float32)
        for k in range(each):
            at = 2 * k * high_count
            both = sums[at : at + high_count] + sums[at + high_count : at + 2 * high_count]
            total = jnp.where(lane // LOW_BINS == k, both, total)
        out_ref[:, g * 128 : (g + 1) * 128] = total


def panel_sums(conserved, cells, counts, bins, amplitudes):
    fields, planes, sector, radial = conserved.shape
    slots, observers = bins.shape
    flat = conserved.reshape(fields, planes * sector, radial)
    high_count = BINS // LOW_BINS
    full = lambda *shape: pl.BlockSpec(shape, lambda i, *_: (0,) * len(shape))
    return pl.pallas_call(
        panel_kernel,
        grid_spec=pltpu.PrefetchScalarGridSpec(
            num_scalar_prefetch=2,
            grid=(1,),
            in_specs=[
                full(1, slots),
                full(fields, planes * sector, radial),
                full(observers, slots),
                full(observers, slots),
            ],
            out_specs=full(high_count, observers * LOW_BINS),
            scratch_shapes=[pltpu.VMEM((fields, slots, radial), jnp.float32)],
        ),
        out_shape=jax.ShapeDtypeStruct((high_count, observers * LOW_BINS), jnp.float32),
        compiler_params=params(),
        cost_estimate=cost(8 * observers * slots * BINS, 4 * fields * planes * sector * radial),
        name="panel_sums",
    )(cells, counts, cells.reshape(1, slots), flat, bins.T, amplitudes.T)


def section_kernel(dtheta, q_ref, before_ref, after_ref, basis_ref, out_ref, spec_ref, axial, swirl, local, inner):
    fields, _, sector, radial = q_ref.shape
    step = pl.program_id(0)
    planes = pl.num_programs(0) - 2
    scale = time_step / 12.0
    chunk = 2 * ROWS
    lane = lax.broadcasted_iota(jnp.int32, (1, radial), 1)
    radius = lane.astype(jnp.float32) + 0.5
    inverse = 1.0 / radius
    near = 8.0 * scale * inverse
    far = scale * inverse
    near_up = jnp.where(lane < radial - 1, near, 0.0)
    near_down = jnp.where(lane >= 1, near, 0.0)
    far_up = jnp.where(lane < radial - 2, far, 0.0)
    far_down = jnp.where(lane >= 2, far, 0.0)
    source = time_step * inverse

    @pl.when(step == 0)
    def _():
        axial[0:2] = jnp.zeros((2,) + axial.shape[1:], jnp.float32)
        axial[planes + 2 : planes + 4] = jnp.zeros((2,) + axial.shape[1:], jnp.float32)

    @pl.when(step < planes)
    def _():
        slot = lax.rem(step, 3)
        for f in range(FIELDS):
            swirl[slot, f, ROWS - 2 : ROWS, :] = before_ref[f, pl.ds(2 * step, 2), :]
            swirl[slot, f, ROWS + sector : ROWS + sector + 2, :] = after_ref[f, pl.ds(2 * step, 2), :]

        def body(i, _):
            start = pl.multiple_of(i * chunk, chunk)
            rows = pl.ds(start, chunk)
            q = [q_ref[f, 0, rows, :] for f in range(FIELDS)]
            u, v, w, p = primitives(q)
            along = carried(q, p, u, 1)
            around = carried(q, p, w, 3)
            outward = carried(q, p, v, 2)
            for f in range(FIELDS):
                axial[step + 2, f, rows, :] = along[f]
                swirl[slot, f, pl.ds(start + ROWS, chunk), :] = around[f]
                g = outward[f] * radius
                value = q[f] - near_up * pltpu.roll(g, radial - 1, 1)
                value = value + near_down * pltpu.roll(g, 1, 1)
                value = value + far_up * pltpu.roll(g, radial - 2, 1)
                value = value - far_down * pltpu.roll(g, 2, 1)
                if f == 2:
                    value = value + source * (p + q[3] * w)
                if f == 3:
                    value = value - source * (q[2] * w)
                local[slot, f, rows, :] = value
            return 0

        lax.fori_loop(0, sector // chunk, body, 0)

    @pl.when(step >= 2)
    def _():
        plane = step - 2
        slot = lax.rem(plane, 3)
        turn = scale * inverse / dtheta

        def body(i, _):
            start = pl.multiple_of(i * chunk, chunk)
            rows = pl.ds(start, chunk)
            result = []
            for f in range(FIELDS):
                at = lambda k: swirl[slot, f, pl.ds(start + (ROWS + k), chunk), :]
                of = lambda k: axial[plane + 2 + k, f, rows, :]
                around = 8.0 * (at(1) - at(-1)) - (at(2) - at(-2))
                along = 8.0 * (of(1) - of(-1)) - (of(2) - of(-2))
                value = local[slot, f, rows, :] - turn * around - scale * along
                out_ref[f, 0, rows, :] = value
                result.append(value)
            inner[rows, :] = inner_lanes(result, lane)
            return 0

        lax.fori_loop(0, sector // chunk, body, 0)
        full = lax.dot_general(
            inner[...], basis_ref[...], (((0,), (0,)), ((), ())),
            precision=HIGHEST, preferred_element_type=jnp.float32,
        )
        spec_ref[0] = full[: FIELDS * CYCLES]


def local_section(conserved, before, after, basis, length):
    fields, planes, sector, radial = conserved.shape
    padded = sector + 2 * ROWS
    late = lambda i: jnp.maximum(i - 2, 0)
    ring = pl.BlockSpec(before.shape, lambda i: (0, 0, 0))
    coefs = FIELDS * CYCLES
    return pl.pallas_call(
        functools.partial(section_kernel, 2.0 * math.pi / length),
        grid=(planes + 2,),
        in_specs=[
            pl.BlockSpec(
                (fields, 1, sector, radial), lambda i: (0, jnp.minimum(i, planes - 1), 0, 0)
            ),
            ring,
            ring,
            pl.BlockSpec((sector, COEFS), lambda i: (0, 0)),
        ],
        out_specs=[
            pl.BlockSpec((fields, 1, sector, radial), lambda i: (0, late(i), 0, 0)),
            pl.BlockSpec((1, coefs, COEFS), lambda i: (late(i), 0, 0)),
        ],
        out_shape=[
            jax.ShapeDtypeStruct(conserved.shape, jnp.float32),
            jax.ShapeDtypeStruct((planes, coefs, COEFS), jnp.float32),
        ],
        scratch_shapes=[
            pltpu.VMEM((planes + 4, fields, sector, radial), jnp.float32),
            pltpu.VMEM((3, fields, padded, radial), jnp.float32),
            pltpu.VMEM((3, fields, sector, radial), jnp.float32),
            pltpu.VMEM((sector, radial), jnp.float32),
        ],
        compiler_params=params(),
        cost_estimate=cost(
            600 * planes * sector * radial, 10 * 4 * fields * planes * sector * radial
        ),
        name="local_section",
    )(conserved, before, after, basis)


def smooth_kernel(raw_ref, spec_ref, weight_ref, basis_ref, out_ref, padded):
    radial = raw_ref.shape[3]
    coefs = spec_ref.shape[1]
    lane = lax.broadcasted_iota(jnp.int32, (1, radial), 1)

    @pl.when(pl.program_id(0) == 0)
    def _():
        padded[...] = jnp.zeros_like(padded)

    padded[:coefs] = spec_ref[0] * weight_ref[...]
    smooth = lax.dot_general(
        basis_ref[...], padded[...], (((1,), (1,)), ((), ())),
        precision=HIGHEST, preferred_element_type=jnp.float32,
    )
    for f in range(FIELDS):
        moved = smooth if f == 0 else pltpu.roll(smooth, radial - CYCLES * f, 1)
        out_ref[f, 0] = jnp.where(lane < CYCLES, moved, raw_ref[f, 0])


def smooth_section(raw, spec, weights, basis):
    fields, planes, sector, radial = raw.shape
    plane = pl.BlockSpec((fields, 1, sector, radial), lambda i: (0, i, 0, 0))
    return pl.pallas_call(
        smooth_kernel,
        grid=(planes,),
        in_specs=[
            plane,
            pl.BlockSpec((1,) + spec.shape[1:], lambda i: (i, 0, 0)),
            pl.BlockSpec(weights.shape, lambda i: (0, 0)),
            pl.BlockSpec(basis.shape, lambda i: (0, 0)),
        ],
        out_specs=plane,
        out_shape=jax.ShapeDtypeStruct(raw.shape, jnp.float32),
        scratch_shapes=[pltpu.VMEM((radial, COEFS), jnp.float32)],
        input_output_aliases={0: 0},
        compiler_params=params(),
        cost_estimate=cost(
            12 * planes * sector * radial * COEFS, 2 * 4 * fields * planes * sector * radial
        ),
        name="smooth_section",
    )(raw, spec, weights, basis)


def add_kernel(part_ref, low_ref, high_ref, out_ref):
    fields, _, sector, radial = part_ref.shape
    tail = sector * CYCLES // radial
    groups = radial // CYCLES - 1
    main = sector - tail
    lane = lax.broadcasted_iota(jnp.int32, (1, radial), 1)
    chosen = lane >= CYCLES

    def go(ref):
        for f in range(fields):
            out_ref[f, 0, :main, :] = part_ref[f, 0, :main, :] + jnp.where(
                chosen, ref[f, 0], 0.0
            )
            rest = jnp.zeros((tail, radial), jnp.float32)
            for g in range(groups):
                start = CYCLES * (g + 1)
                here = (lane >= start) & (lane < start + CYCLES)
                moved = pltpu.roll(ref[f, 0, g * tail : (g + 1) * tail, :], start, 1)
                rest = jnp.where(here, moved, rest)
            out_ref[f, 0, main:, :] = part_ref[f, 0, main:, :] + rest

    pl.when(pl.program_id(0) < 2)(lambda: go(low_ref))
    pl.when(pl.program_id(0) >= 2)(lambda: go(high_ref))


def add_edges(part, low, high):
    fields, planes, sector, radial = part.shape
    main = low.shape[2]
    plane = pl.BlockSpec(
        (fields, 1, sector, radial), lambda i: (0, jnp.where(i < 2, i, planes - 4 + i), 0, 0)
    )
    return pl.pallas_call(
        add_kernel,
        grid=(4,),
        in_specs=[
            plane,
            pl.BlockSpec((fields, 1, main, radial), lambda i: (0, jnp.minimum(i, 1), 0, 0)),
            pl.BlockSpec((fields, 1, main, radial), lambda i: (0, jnp.maximum(i - 2, 0), 0, 0)),
        ],
        out_specs=plane,
        out_shape=jax.ShapeDtypeStruct(part.shape, jnp.float32),
        input_output_aliases={0: 0},
        compiler_params=params(),
        cost_estimate=cost(8 * fields * sector * radial, 4 * 12 * fields * sector * radial),
        name="add_edges",
    )(part, low, high)


def shared_sums(partial, observers):
    n_ax, n_az = lax.axis_size("ax"), lax.axis_size("az")
    mine = BINS // (n_ax * n_az)
    if mine != LOW_BINS:
        partial = partial.reshape(-1, observers, LOW_BINS).transpose(0, 2, 1)
        partial = partial.reshape(n_ax * n_az, mine, observers).transpose(0, 2, 1)
    blocks = partial.reshape(n_ax, n_az, observers * mine)
    blocks = lax.all_to_all(blocks, "az", split_axis=1, concat_axis=1, tiled=True).sum(axis=1)
    return lax.all_to_all(blocks, "ax", split_axis=0, concat_axis=0, tiled=True).sum(axis=0).reshape(
        observers, mine
    )


def on_device(conserved, panel_cells, panel_counts, time_bins, amplitudes):
    fields, planes, sector, radial = conserved.shape
    n_ax, n_az = lax.axis_size("ax"), lax.axis_size("az")
    length = sector * n_az
    up = [(i, i + 1) for i in range(n_ax - 1)]
    down = [(j, i) for i, j in up]
    ahead = [(i, (i + 1) % n_az) for i in range(n_az)]
    back = [(j, i) for i, j in ahead]

    send_up, inner_up = edge_terms(conserved, True)
    low = lax.ppermute(send_up, "ax", up)
    send_down, inner_down = edge_terms(conserved, False)
    high = lax.ppermute(send_down, "ax", down)

    basis = lax.dynamic_slice_in_dim(
        jnp.asarray(basis_table(length)), lax.axis_index("az") * sector, sector, axis=0
    )
    spec_up, spec_down, first, last = small_terms(conserved, inner_up, inner_down, basis)
    before = lax.ppermute(last, "az", ahead)
    after = lax.ppermute(first, "az", back)
    spec_low = lax.ppermute(spec_up, "ax", up)
    spec_high = lax.ppermute(spec_down, "ax", down)

    partial = panel_sums(conserved, panel_cells, panel_counts, time_bins, amplitudes)
    signal = shared_sums(partial, time_bins.shape[1])

    raw, spec = local_section(conserved, before, after, basis, length)
    spec = jnp.concatenate(
        [spec[:2] + spec_low, spec[2 : planes - 2], spec[planes - 2 :] + spec_high], axis=0
    )
    bit = 1
    while bit < n_az:
        spec = spec + lax.ppermute(spec, "az", [(i, i ^ bit) for i in range(n_az)])
        bit *= 2
    part = smooth_section(raw, spec, jnp.asarray(mode_weights(length)), basis)
    section = add_edges(part, low, high)
    return (section, signal)


def solution(mesh):
    placed = (
        P(None, "ax", "az", None),
        P(("ax", "az")),
        P(("ax", "az")),
        P(("ax", "az"), None),
        P(("ax", "az"), None),
    )
    return jax.shard_map(
        on_device,
        mesh=mesh,
        in_specs=placed,
        out_specs=(P(None, "ax", "az", None), P(None, ("ax", "az"))),
        check_vma=False,
    )
```

time: 427 us -> 107 us (0.25); the launches traced: 418 us -> 106 us
  other arithmetic: 228 us -> 1.06 us
  local copies, waits for them, and re-layouts: 81.1 us -> 5.17 us
  Pallas kernels: 0 us -> 56.4 us
  matrix products: 40.2 us -> 0 us
  waiting for transfers between devices: 36.6 us -> 10.1 us
  between operations: 15.5 us -> 1.48 us
  blocking collectives: 0 us -> 12.9 us
    scatter-add x1 -> x0, other arithmetic: 172 us -> none  [on_device(): jax.ops.segment_sum(contrib.reshape(-1), segment.reshape(-1), num_segment...]
    pallas_call x0 -> x7, Pallas kernels: none -> 56.4 us  [the longest x1 31.9 us: local_section(): pl.pallas_call(functools.partial(section_kernel, 2.0 * math.pi / length),...]
    dot_general x5 -> x0, matrix products: 40.2 us -> none  [the longest x1 10.1 us: apply_filter(): jnp.einsum('fln,nm->flm', line_block, cos_table, precision=lax.Precision....]
    slice x10 -> x1, local copies, waits for them, and re-layouts: 29.4 us -> 0.01 us  [on_device(): spec[2:planes - 2]]
    unnamed x34 -> x11, local copies, waits for them, and re-layouts: 30.6 us -> 3.19 us
    ppermute x4 -> x8, waiting for transfers between devices: 26.5 us -> 6.58 us  [the longest x1 6.56 us: on_device(): spec_low = lax.ppermute(spec_up, 'ax', up)]
    add x3, other arithmetic: 18.6 us -> 0.97 us  [the longest x2 0.96 us: on_device(): spec = spec + lax.ppermute(spec, 'az', [(i, i ^ bit) for i in range(n_az)])]
    concatenate x3 -> x1, other arithmetic: 13.7 us -> 0.01 us  [on_device(): jnp.concatenate([spec[:2] + spec_low, spec[2:planes - 2], spec[planes - 2...]
  transfers between devices with their start and end apart: 7 -> 9, of which waited for: 3 -> 2; matrix products, arithmetic and copies ran while one was open for 31% -> 3% of each run, Pallas kernels for 0% -> 46%
where the time goes in v1:
time: 107 us; the launch traced here: 106 us
  Pallas kernels  56.4 us (53%)
  starting transfers between devices  19.3 us (18%)
  blocking collectives  12.9 us (12%)
  waiting for transfers between devices  10.1 us (9%)
  local copies, waits for them, and re-layouts  5.17 us (5%)
  between operations  1.48 us (1%)
    pallas_call x1, Pallas kernels, local_section(): pl.pallas_call(functools.partial(section_kernel, 2.0 * math.pi / length),...  31.9 us
    all_to_all x1, blocking collectives, shared_sums(): lax.all_to_all(blocks, 'ax', split_axis=0, concat_axis=0, tiled=True)  12.9 us
    pallas_call x1, Pallas kernels, smooth_section(): pl.pallas_call(smooth_kernel, grid=(planes,), in_specs=[plane, pl.BlockSp...  8.47 us
    ppermute x1, waiting for transfers between devices, on_device(): spec_low = lax.ppermute(spec_up, 'ax', up)  6.56 us
    pallas_call x2, Pallas kernels, edge_terms(): pl.pallas_call(functools.partial(edge_kernel, up), grid=(1,), in_specs=[p...  6.02 us
    pallas_call x1, Pallas kernels, panel_sums(): pl.pallas_call(panel_kernel, grid_spec=pltpu.PrefetchScalarGridSpec(num_s...  5 us
    ppermute x1, starting transfers between devices, on_device(): low = lax.ppermute(send_up, 'ax', up)  4.91 us
    ppermute x1, starting transfers between devices, on_device(): spec_low = lax.ppermute(spec_up, 'ax', up)  4.54 us
  transfers between devices with their start and end apart: 9, of which 2 were waited for; matrix products, arithmetic and copies ran while one was open for 3% of the time, Pallas kernels for 46%

profile of v1, /device:TPU:0, one launch (start us, length us, event | category | flops | bytes accessed | tf_op | source)
XLA Modules:
  0.0 106.3 jit_solution(15449204417388463673)
XLA Ops:
  0.6 3.0 %edge_up.1 = (f32[5,2,240,128]{3,2,1,0:T(8,128)}, f32[2,256,128]{2,1,0:T(8,128)S(1)}) custom-call(f32[5,8,256,128]{3,2,1,0:T(8,128)} %q_ref.5), custom_call_target="tpu_custom_call" | custom-call | flops 6553600 | bytes 2621440 | tf_op jit(solution)/shard_map/edge_up/pallas_call | solution.py:116
  3.7 4.9 %collective-permute-start.6 = (f32[5,2,240,128]{3,2,1,0:T(8,128)}, f32[5,2,240,128]{3,2,1,0:T(8,128)S(1)}, u32[]{:S(2)}, u32[]{:S(2)}) collective-permute-start(f32[5,2,240,128]{3,2,1,0:T(8,128)} %get-tuple-element.20), channel_id=1, source_target_pairs={{0,4},{4,8},{8,12},{12,16},{16,20},{20,24},{24,28},{1,5},{5,9},{9,... | collective-permute-start | bytes 3686408 | tf_op jit(solution)/shard_map/ppermute | solution.py:506
  8.6 3.0 %edge_down.1 = (f32[5,2,240,128]{3,2,1,0:T(8,128)}, f32[2,256,128]{2,1,0:T(8,128)S(1)}) custom-call(f32[5,8,256,128]{3,2,1,0:T(8,128)} %q_ref.5), custom_call_target="tpu_custom_call" | custom-call | flops 6553600 | bytes 2621440 | tf_op jit(solution)/shard_map/edge_down/pallas_call | solution.py:116
  11.6 1.3 %collective-permute-start.7 = (f32[5,2,240,128]{3,2,1,0:T(8,128)}, f32[5,2,240,128]{3,2,1,0:T(8,128)S(1)}, u32[]{:S(2)}, u32[]{:S(2)}) collective-permute-start(f32[5,2,240,128]{3,2,1,0:T(8,128)} %get-tuple-element.21), channel_id=1, source_target_pairs={{4,0},{8,4},{12,8},{16,12},{20,16},{24,20},{28,24},{5,1},{9,5},{13... | collective-permute-start | bytes 3686408 | tf_op jit(solution)/shard_map/ppermute | solution.py:508
  12.9 0.9 constant_dynamic-slice_fusion.basis_ref
  13.8 0.0 copy-start
  13.8 2.5 %copy-done = f32[5,8,256,128]{3,2,1,0:T(8,128)S(1)} copy-done((f32[5,8,256,128]{3,2,1,0:T(8,128)S(1)}, f32[5,8,256,128]{3,2,1,0:T(8,128)}, u32[]{:S(2)}) %copy-start) | copy-done | bytes 5242904
  16.3 0.6 small_terms.1
  16.9 0.0 copy-start.1
  16.9 0.0 copy-start.2
  16.9 0.0 copy-start.4
  16.9 0.1 collective-permute-start
  17.0 1.7 %collective-permute-start.1 = (f32[5,16,128]{2,1,0:T(8,128)S(1)}, f32[5,16,128]{2,1,0:T(8,128)S(1)}, u32[]{:S(2)}, u32[]{:S(2)}) collective-permute-start(f32[5,16,128]{2,1,0:T(8,128)S(1)} %get-tuple-element.15), channel_id=1, source_target_pairs={{1,0},{2,1},{3,2},{0,3},{5,4},{6,5},{7,6},{4,7},{9,8},{10,9},{11,1... | collective-permute-start | bytes 122888 | tf_op jit(solution)/shard_map/ppermute | solution.py:515
  18.7 4.5 %collective-permute-start.2 = (f32[2,40,128]{2,1,0:T(8,128)S(1)}, f32[2,40,128]{2,1,0:T(8,128)S(1)}, u32[]{:S(2)}, u32[]{:S(2)}) collective-permute-start(f32[2,40,128]{2,1,0:T(8,128)S(1)} %get-tuple-element.18), channel_id=1, source_target_pairs={{0,4},{4,8},{8,12},{12,16},{16,20},{20,24},{24,28},{1,5},{5,9},{9,... | collective-permute-start | bytes 122888 | tf_op jit(solution)/shard_map/ppermute | solution.py:516
  23.3 0.0 collective-permute-done.before_ref
  23.3 1.3 %collective-permute-start.3 = (f32[2,40,128]{2,1,0:T(8,128)S(1)}, f32[2,40,128]{2,1,0:T(8,128)S(1)}, u32[]{:S(2)}, u32[]{:S(2)}) collective-permute-start(f32[2,40,128]{2,1,0:T(8,128)S(1)} %get-tuple-element.19), channel_id=1, source_target_pairs={{4,0},{8,4},{12,8},{16,12},{20,16},{24,20},{28,24},{5,1},{9,5},{13... | collective-permute-start | bytes 122888 | tf_op jit(solution)/shard_map/ppermute | solution.py:517
  24.6 31.9 %local_section.1 = (f32[5,8,256,128]{3,2,1,0:T(8,128)}, f32[8,40,128]{2,1,0:T(8,128)S(1)}) custom-call(f32[5,8,256,128]{3,2,1,0:T(8,128)S(1)} %copy-done, f32[5,16,128]{2,1,0:T(8,128)S(1)} %collective-permute-done.before_ref, f32[5,16,128]{2,1,0:T(8,128)S(1)} %collective-permute-done.1.after_ref, f32[256,128]{1,0:T(8,128)S(1)} %constant_dynamic-slice_fusion.basis_ref), custom_call_target="tpu_custom_call" | custom-call | flops 157286400 | bytes 52428800 | tf_op jit(solution)/shard_map/local_section/pallas_call | solution.py:359
  56.5 6.6 %collective-permute-done.2 = f32[2,40,128]{2,1,0:T(8,128)S(1)} collective-permute-done((f32[2,40,128]{2,1,0:T(8,128)S(1)}, f32[2,40,128]{2,1,0:T(8,128)S(1)}, u32[]{:S(2)}, u32[]{:S(2)}) %collective-permute-start.2) | collective-permute-done | bytes 40992 | tf_op jit(solution)/shard_map/ppermute | solution.py:516
  63.1 0.1 collective-permute-start.4
  63.9 5.0 %panel_sums.1 = f32[32,2048]{1,0:T(8,128)S(1)} custom-call(s32[512]{0:T(512)S(1)} %copy-done.4, s32[1]{0:T(128)S(6)} %copy.16.count_ref, s32[1,512]{1,0:T(1,128)S(1)} %bitcast.7, f32[5,2048,128]{2,1,0:T(8,128)S(1)} %bitcast.4, s32[64,512]{1,0:T(8,128)S(1)} %bitcast.5, f32[64,512]{1,0:T(8,128)S(1)} %bitcast.6), custom_call_target="tpu_custom_call" | custom-call | flops 268435456 | bytes 5242880 | tf_op jit(solution)/shard_map/panel_sums/pallas_call | solution.py:249
  68.9 0.1 reshape.20
  68.9 0.9 copy.12
  69.8 3.4 %all-to-all-start = ((f32[8,4,2048]{2,0,1:T(8,128)}), f32[8,4,2048]{2,0,1:T(8,128)S(1)}, u32[]{:S(2)}, u32[]{:S(2)}) async-start(f32[8,4,2048]{2,0,1:T(8,128)} %copy.12), calls=%async_computation | async-start | bytes 524288 | tf_op jit(solution)/shard_map/all_to_all | solution.py:490
  73.2 0.9 fusion
  74.2 2.0 %collective-permute-start.5 = (f32[8,40,128]{2,1,0:T(8,128)S(1)}, f32[8,40,128]{2,1,0:T(8,128)S(1)}, u32[]{:S(2)}, u32[]{:S(2)}) collective-permute-start(f32[8,40,128]{2,1,0:T(8,128)S(1)} %fusion), channel_id=1, source_target_pairs={{0,2},{1,3},{2,0},{3,1},{4,6},{5,7},{6,4},{7,5},{8,10},{9,11},{10,... | collective-permute-start | bytes 491528 | tf_op jit(solution)/shard_map/ppermute | solution.py:528
  76.2 3.5 %all-to-all-done = f32[8,4,2048]{2,0,1:T(8,128)S(1)} async-done(((f32[8,4,2048]{2,0,1:T(8,128)}), f32[8,4,2048]{2,0,1:T(8,128)S(1)}, u32[]{:S(2)}, u32[]{:S(2)}) %all-to-all-start) | async-done | bytes 262176 | tf_op jit(solution)/shard_map/all_to_all | solution.py:490
  79.8 12.9 %all_to_all.14 = f32[8,1,2048]{2,1,0:T(1,128)S(1)} all-to-all(f32[8,1,2048]{2,1,0:T(1,128)S(1)} %all_to_all.10), channel_id=1, replica_groups=mesh['ax'=8,'az'=4] {'ax'}, dimensions={0} | all-to-all | bytes 131072 | tf_op jit(solution)/shard_map/all_to_all | solution.py:491
  92.6 0.1 reduce_sum.19
  92.7 0.1 reshape.21
  92.8 0.7 copy.13
  93.5 8.5 %smooth_section.1.part_ref = f32[5,8,256,128]{3,2,1,0:T(8,128)} custom-call(f32[5,8,256,128]{3,2,1,0:T(8,128)} %get-tuple-element.16.raw_ref, f32[8,40,128]{2,1,0:T(8,128)S(1)} %add.19.spec_ref, f32[40,128]{1,0:T(8,128)S(1)} %copy-done.3, f32[256,128]{1,0:T(8,128)S(1)} %constant_dynamic-slice_fusion.basis_ref), custom_call_target="tpu_custom_call", output_to_operand_aliasing={{}: (0, {})} | custom-call | flops 402653184 | bytes 10485760 | tf_op jit(solution)/shard_map/smooth_section/pallas_call | solution.py:414
  102.0 4.4 %add_edges.1 = f32[5,8,256,128]{3,2,1,0:T(8,128)} custom-call(f32[5,8,256,128]{3,2,1,0:T(8,128)} %smooth_section.1.part_ref, f32[5,2,240,128]{3,2,1,0:T(8,128)S(1)} %collective-permute-done.6.low_ref, f32[5,2,240,128]{3,2,1,0:T(8,128)S(1)} %collective-permute-done.7.high_ref), custom_call_target="tpu_custom_call", output_to_operand_aliasing={{}: (0, {})} | custom-call | flops 1310720 | bytes 7864320 | tf_op jit(solution)/shard_map/add_edges/pallas_call | solution.py:466
  (17 shorter events, 0.1 us)
Async XLA Ops:
  3.7 98.3 %collective-permute-start.6 = (f32[5,2,240,128]{3,2,1,0:T(8,128)}, f32[5,2,240,128]{3,2,1,0:T(8,128)S(1)}, u32[]{:S(2)}, u32[]{:S(2)}) collective-permute-start(f32[5,2,240,128]{3,2,1,0:T(8,128)} %get-tuple-element.20), channel_id=1, source_target_pairs={{0,4},{4,8},{8,12},{12,16},{16,20},{20,24},{24,28},{1,5},{5,9},{9,... | collective-permute-start | bytes 3686408 | tf_op jit(solution)/shard_map/ppermute | solution.py:506
  11.6 90.4 %collective-permute-start.7 = (f32[5,2,240,128]{3,2,1,0:T(8,128)}, f32[5,2,240,128]{3,2,1,0:T(8,128)S(1)}, u32[]{:S(2)}, u32[]{:S(2)}) collective-permute-start(f32[5,2,240,128]{3,2,1,0:T(8,128)} %get-tuple-element.21), channel_id=1, source_target_pairs={{4,0},{8,4},{12,8},{16,12},{20,16},{24,20},{28,24},{5,1},{9,5},{13... | collective-permute-start | bytes 3686408 | tf_op jit(solution)/shard_map/ppermute | solution.py:508
  13.8 2.5 %copy-start = (f32[5,8,256,128]{3,2,1,0:T(8,128)S(1)}, f32[5,8,256,128]{3,2,1,0:T(8,128)}, u32[]{:S(2)}) copy-start(f32[5,8,256,128]{3,2,1,0:T(8,128)} %q_ref.5) | copy-start | bytes 15728644
  16.9 46.9 %copy-start.1 = (s32[512,64]{0,1:T(8,128)S(1)}, s32[512,64]{0,1:T(8,128)}, u32[]{:S(2)}) copy-start(s32[512,64]{0,1:T(8,128)} %param.10) | copy-start | bytes 393220
  16.9 46.9 %copy-start.2 = (f32[512,64]{0,1:T(8,128)S(1)}, f32[512,64]{0,1:T(8,128)}, u32[]{:S(2)}) copy-start(f32[512,64]{0,1:T(8,128)} %param.11) | copy-start | bytes 393220
  16.9 46.9 %copy-start.4 = (s32[512]{0:T(512)S(1)}, s32[512]{0:T(512)}, u32[]{:S(2)}) copy-start(s32[512]{0:T(512)} %cells_ref.1) | copy-start | bytes 6148
  16.9 6.3 %collective-permute-start = (f32[5,16,128]{2,1,0:T(8,128)S(1)}, f32[5,16,128]{2,1,0:T(8,128)S(1)}, u32[]{:S(2)}, u32[]{:S(2)}) collective-permute-start(f32[5,16,128]{2,1,0:T(8,128)S(1)} %get-tuple-element.14), channel_id=1, source_target_pairs={{0,1},{1,2},{2,3},{3,0},{4,5},{5,6},{6,7},{7,4},{8,9},{9,10},{10,1... | collective-permute-start | bytes 122888 | tf_op jit(solution)/shard_map/ppermute | solution.py:514
  17.0 7.6 %collective-permute-start.1 = (f32[5,16,128]{2,1,0:T(8,128)S(1)}, f32[5,16,128]{2,1,0:T(8,128)S(1)}, u32[]{:S(2)}, u32[]{:S(2)}) collective-permute-start(f32[5,16,128]{2,1,0:T(8,128)S(1)} %get-tuple-element.15), channel_id=1, source_target_pairs={{1,0},{2,1},{3,2},{0,3},{5,4},{6,5},{7,6},{4,7},{9,8},{10,9},{11,1... | collective-permute-start | bytes 122888 | tf_op jit(solution)/shard_map/ppermute | solution.py:515
  18.7 44.3 %collective-permute-start.2 = (f32[2,40,128]{2,1,0:T(8,128)S(1)}, f32[2,40,128]{2,1,0:T(8,128)S(1)}, u32[]{:S(2)}, u32[]{:S(2)}) collective-permute-start(f32[2,40,128]{2,1,0:T(8,128)S(1)} %get-tuple-element.18), channel_id=1, source_target_pairs={{0,4},{4,8},{8,12},{12,16},{16,20},{20,24},{24,28},{1,5},{5,9},{9,... | collective-permute-start | bytes 122888 | tf_op jit(solution)/shard_map/ppermute | solution.py:516
  23.3 39.8 %collective-permute-start.3 = (f32[2,40,128]{2,1,0:T(8,128)S(1)}, f32[2,40,128]{2,1,0:T(8,128)S(1)}, u32[]{:S(2)}, u32[]{:S(2)}) collective-permute-start(f32[2,40,128]{2,1,0:T(8,128)S(1)} %get-tuple-element.19), channel_id=1, source_target_pairs={{4,0},{8,4},{12,8},{16,12},{20,16},{24,20},{28,24},{5,1},{9,5},{13... | collective-permute-start | bytes 122888 | tf_op jit(solution)/shard_map/ppermute | solution.py:517
  56.5 37.0 %copy-start.3 = (f32[40,128]{1,0:T(8,128)S(1)}, f32[40,128]{1,0:T(8,128)}, u32[]{:S(2)}) copy-start(f32[40,128]{1,0:T(8,128)} %constant.17.clone.weight_ref) | copy-start | bytes 61444
  63.1 10.1 %collective-permute-start.4 = (f32[8,40,128]{2,1,0:T(8,128)S(1)}, f32[8,40,128]{2,1,0:T(8,128)}, u32[]{:S(2)}, u32[]{:S(2)}) collective-permute-start(f32[8,40,128]{2,1,0:T(8,128)S(1)} %pad_maximum_fusion), channel_id=1, source_target_pairs={{0,1},{1,0},{2,3},{3,2},{4,5},{5,4},{6,7},{7,6},{8,9},{9,8},{10,11... | collective-permute-start | bytes 491528 | tf_op jit(solution)/shard_map/ppermute | solution.py:528
  69.8 9.9 %all-to-all-start = ((f32[8,4,2048]{2,0,1:T(8,128)}), f32[8,4,2048]{2,0,1:T(8,128)S(1)}, u32[]{:S(2)}, u32[]{:S(2)}) async-start(f32[8,4,2048]{2,0,1:T(8,128)} %copy.12), calls=%async_computation | async-start | bytes 524288 | tf_op jit(solution)/shard_map/all_to_all | solution.py:490
  74.2 19.3 %collective-permute-start.5 = (f32[8,40,128]{2,1,0:T(8,128)S(1)}, f32[8,40,128]{2,1,0:T(8,128)S(1)}, u32[]{:S(2)}, u32[]{:S(2)}) collective-permute-start(f32[8,40,128]{2,1,0:T(8,128)S(1)} %fusion), channel_id=1, source_target_pairs={{0,2},{1,3},{2,0},{3,1},{4,6},{5,7},{6,4},{7,5},{8,10},{9,11},{10,... | collective-permute-start | bytes 491528 | tf_op jit(solution)/shard_map/ppermute | solution.py:528

commit v2 on v1

v2 whole, which is shorter than its diff:
```python
import functools
import math

import jax
import jax.numpy as jnp
import numpy as np
from jax import lax
from jax.experimental import pallas as pl
from jax.experimental.pallas import tpu as pltpu
from jax.sharding import PartitionSpec as P

CYCLES = 8
BINS = 1024
LOW_BINS = 32
FIELDS = 5
MODES = 8 * CYCLES
COEFS = 2 * MODES
ROWS = 8

gas_factor = 0.4
time_step = 0.02
ref_pressure = 0.95
VMEM_BYTES = 48 * 1024 * 1024

HIGHEST = lax.Precision.HIGHEST


def params(**more):
    return pltpu.CompilerParams(vmem_limit_bytes=VMEM_BYTES, **more)


def cost(flops, touched):
    return pl.CostEstimate(flops=flops, bytes_accessed=touched, transcendentals=0)


def basis_table(length):
    phase = (np.arange(length)[:, None] * np.arange(MODES)[None, :] % length) * (
        2.0 * math.pi / length
    )
    return np.concatenate([np.cos(phase), np.sin(phase)], axis=1).astype(np.float32)


def mode_weights(length):
    modes = np.arange(MODES).astype(np.float64)
    cutoff = 4.0 * (np.arange(CYCLES) + 1.0)
    weight = np.exp(-((modes[None, :] / cutoff[:, None]) ** 8))
    weight = weight * np.where(modes == 0, 1.0, 2.0)[None, :] / length
    return np.concatenate([weight, weight], axis=1).astype(np.float32)


def primitives(q):
    inverse = 1.0 / q[0]
    u, v, w = q[1] * inverse, q[2] * inverse, q[3] * inverse
    p = gas_factor * (q[4] - 0.5 * (q[1] * u + q[2] * v + q[3] * w))
    return u, v, w, p


def carried(q, p, speed, heading):
    flux = [q[0] * speed, q[1] * speed, q[2] * speed, q[3] * speed, (q[4] + p) * speed]
    flux[heading] = flux[heading] + p
    return flux


def swirl_rows(ref, low):
    for k in range(ref.shape[1]):
        q = [ref[f, k] for f in range(FIELDS)]
        _, _, w, p = primitives(q)
        flux = carried(q, p, w, 3)
        yield k, [jnp.where(low, f[:2], f[ROWS - 2 :]) for f in flux]


def edge_kernel(az_ref, q_ref, rim_ref, up_ref, down_ref, early_ref):
    sector, radial = q_ref.shape[2:]
    groups = radial // CYCLES - 1
    tail = sector * CYCLES // radial
    scale = time_step / 12.0
    lane = lax.broadcasted_iota(jnp.int32, (1, radial), 1)

    def go(up, send):
        def terms(start):
            rows = pl.ds(start, tail)
            flux = []
            for plane in range(2):
                q = [q_ref[f, plane, rows, :] for f in range(FIELDS)]
                u, _, _, p = primitives(q)
                flux.append(carried(q, p, u, 1))
            near, far = (flux[1], flux[0]) if up else (flux[0], flux[1])
            whole, part = [], []
            for f in range(FIELDS):
                wide = scale * (8.0 * near[f] - far[f])
                narrow = scale * near[f]
                whole.append(wide if up else -wide)
                part.append(-narrow if up else narrow)
            return (whole, part) if up else (part, whole)

        last = terms(groups * tail)
        for g in range(groups):
            slots = terms(g * tail)
            shift = radial - CYCLES * (g + 1)
            for s in range(2):
                for f in range(FIELDS):
                    moved = pltpu.roll(last[s][f], shift, 1)
                    send[f, s, pl.ds(g * tail, tail), :] = jnp.where(
                        lane < CYCLES, moved, slots[s][f]
                    )

    @pl.when(pl.program_id(0) == 0)
    def _():
        go(True, up_ref)
        for k, flux in swirl_rows(rim_ref, lax.rem(az_ref[0], 2) == 1):
            for f in range(FIELDS):
                early_ref[f, 2 * k : 2 * k + 2, :] = flux[f]

    pl.when(pl.program_id(0) == 1)(lambda: go(False, down_ref))


def edge_terms(conserved, az):
    fields, planes, sector, radial = conserved.shape
    out = jax.ShapeDtypeStruct((fields, 2, sector - sector * CYCLES // radial, radial), jnp.float32)
    early = jax.ShapeDtypeStruct((fields, 2 * planes, radial), jnp.float32)
    last = sector // ROWS - 1
    wide = pl.BlockSpec(out.shape, lambda i, *_: (0, 0, 0, 0))
    return pl.pallas_call(
        edge_kernel,
        grid_spec=pltpu.PrefetchScalarGridSpec(
            num_scalar_prefetch=1,
            grid=(2,),
            in_specs=[
                pl.BlockSpec(
                    (fields, 2, sector, radial), lambda i, az: (0, (planes // 2 - 1) * (1 - i), 0, 0)
                ),
                pl.BlockSpec(
                    (fields, planes, ROWS, radial),
                    lambda i, az: (0, 0, last * (1 - lax.rem(az[0], 2)), 0),
                ),
            ],
            out_specs=[wide, wide, pl.BlockSpec(early.shape, lambda i, *_: (0, 0, 0))],
        ),
        out_shape=[out, out, early],
        compiler_params=params(),
        cost_estimate=cost(400 * sector * radial, 4 * 8 * fields * sector * radial),
        name="edge_terms",
    )(az, conserved, conserved)


def here_specs(table, sector):
    return pl.BlockSpec((sector, COEFS), lambda i, az, *_: (az[0], 0))


def inner_kernel(dtheta, *refs):
    az_ref, q_ref, rim_ref, before_ref, here_ref, after_ref, _ = refs[:7]
    message_ref, later_ref, local, swirl, outside = refs[7:]
    fields, planes, sector, radial = q_ref.shape
    group = 2 * CYCLES
    scale = time_step / 12.0
    chunk = min(sector, 8 * ROWS)
    lane = lax.broadcasted_iota(jnp.int32, (1, radial), 1)
    cycle = lane & (group - 1)
    plane = lane // group
    radius = cycle.astype(jnp.float32) + 0.5
    inverse = 1.0 / radius
    near = 8.0 * scale * inverse
    far = scale * inverse
    near_down = jnp.where(cycle >= 1, near, 0.0)
    far_down = jnp.where(cycle >= 2, far, 0.0)
    source = time_step * inverse
    turn = scale * inverse / dtheta

    def split(there, value):
        return jnp.where(there, value, 0.0), jnp.where(there, 0.0, value)

    behind, behind_out = split(plane >= 1, 8.0 * scale)
    behind2, behind2_out = split(plane >= 2, scale)
    ahead, ahead_out = split(plane < planes - 1, 8.0 * scale)
    ahead2, ahead2_out = split(plane < planes - 2, scale)

    zeros = jnp.zeros((FIELDS, 2 * ROWS, radial), jnp.float32)
    swirl[:, : 2 * ROWS, :] = zeros
    swirl[:, 2 * ROWS + sector :, :] = zeros
    local[:, :ROWS, :] = zeros[:, :ROWS]
    local[:, ROWS + sector :, :] = zeros[:, :ROWS]

    def body(i, _):
        start = pl.multiple_of(i * chunk, chunk)
        rows = pl.ds(start, chunk)
        q = []
        for f in range(FIELDS):
            packed = q_ref[f, 0, rows, :]
            for k in range(1, planes):
                moved = pltpu.roll(q_ref[f, k, rows, :], group * k, 1)
                packed = jnp.where(plane == k, moved, packed)
            q.append(packed)
        u, v, w, p = primitives(q)
        along = carried(q, p, u, 1)
        around = carried(q, p, w, 3)
        outward = carried(q, p, v, 2)
        for f in range(FIELDS):
            swirl[f, pl.ds(start + 2 * ROWS, chunk), :] = around[f]
            g = outward[f] * radius
            value = q[f] - near * pltpu.roll(g, radial - 1, 1)
            value = value + near_down * pltpu.roll(g, 1, 1)
            value = value + far * pltpu.roll(g, radial - 2, 1)
            value = value - far_down * pltpu.roll(g, 2, 1)
            if f == 2:
                value = value + source * (p + q[3] * w)
            if f == 3:
                value = value - source * (q[2] * w)
            up1 = pltpu.roll(along[f], group, 1)
            up2 = pltpu.roll(along[f], 2 * group, 1)
            down1 = pltpu.roll(along[f], radial - group, 1)
            down2 = pltpu.roll(along[f], radial - 2 * group, 1)
            value = value + behind * up1 - behind2 * up2 - ahead * down1 + ahead2 * down2
            local[f, pl.ds(start + ROWS, chunk), :] = value
            outside[f, rows, :] = (
                behind_out * up1 - behind2_out * up2 - ahead_out * down1 + ahead2_out * down2
            )
        return 0

    lax.fori_loop(0, sector // chunk, body, 0)

    def rest(start, size):
        for f in range(FIELDS):
            at = lambda k: swirl[f, pl.ds(start + (ROWS + k), size), :]
            around = 8.0 * (at(1) - at(-1)) - (at(2) - at(-2))
            rows = pl.ds(start, size)
            local[f, rows, :] = local[f, rows, :] - turn * around

    rest(0, ROWS)
    rest(ROWS + sector, ROWS)

    def body2(i, _):
        rest(pl.multiple_of(i * chunk, chunk) + ROWS, chunk)
        return 0

    lax.fori_loop(0, sector // chunk, body2, 0)

    basis = jnp.concatenate([before_ref[...], here_ref[...], after_ref[...]], axis=0)

    def transform(rows, table):
        return lax.dot_general(
            rows, table, (((0,), (0,)), ((), ())),
            precision=HIGHEST, preferred_element_type=jnp.float32,
        )

    for f in range(FIELDS):
        own = transform(local[f], basis)
        for k in range(planes):
            message_ref[f, k * CYCLES : (k + 1) * CYCLES, :] = own[k * group : k * group + CYCLES]
        other = transform(outside[f], here_ref[...])
        for s, k in enumerate((0, 1, planes - 2, planes - 1)):
            at = (planes + s) * CYCLES
            message_ref[f, at : at + CYCLES, :] = other[k * group : k * group + CYCLES]

    for k, flux in swirl_rows(rim_ref, lax.rem(az_ref[0], 2) == 0):
        for f in range(FIELDS):
            later_ref[f, 2 * k : 2 * k + 2, :] = flux[f]


def inner_terms(conserved, az, table, after):
    fields, planes, sector, radial = conserved.shape
    length = table.shape[0]
    message = (fields, (planes + 4) * CYCLES, COEFS)
    later = (fields, 2 * planes, radial)
    full = lambda *shape: pl.BlockSpec(shape, lambda i, *_: (0,) * len(shape))
    tiles = sector // ROWS
    wrap = lambda k: lax.rem(k + length // ROWS, length // ROWS)
    return pl.pallas_call(
        functools.partial(inner_kernel, 2.0 * math.pi / length),
        grid_spec=pltpu.PrefetchScalarGridSpec(
            num_scalar_prefetch=1,
            grid=(1,),
            in_specs=[
                full(*conserved.shape),
                pl.BlockSpec(
                    (fields, planes, ROWS, radial),
                    lambda i, az: (0, 0, (tiles - 1) * lax.rem(az[0], 2), 0),
                ),
                pl.BlockSpec((ROWS, COEFS), lambda i, az: (wrap(az[0] * tiles - 1), 0)),
                here_specs(table, sector),
                pl.BlockSpec((ROWS, COEFS), lambda i, az: (wrap((az[0] + 1) * tiles), 0)),
                pl.BlockSpec(memory_space=pl.ANY),
            ],
            out_specs=[full(*message), full(*later)],
            scratch_shapes=[
                pltpu.VMEM((fields, sector + 2 * ROWS, radial), jnp.float32),
                pltpu.VMEM((fields, sector + 4 * ROWS, radial), jnp.float32),
                pltpu.VMEM((fields, sector, radial), jnp.float32),
            ],
        ),
        out_shape=[
            jax.ShapeDtypeStruct(message, jnp.float32),
            jax.ShapeDtypeStruct(later, jnp.float32),
        ],
        compiler_params=params(),
        cost_estimate=cost(60 * sector * radial * COEFS, 4 * fields * planes * sector * radial),
        name="inner_terms",
    )(az, conserved, conserved, table, table, table, after)


def panel_kernel(cells_ref, count_ref, row_ref, q_ref, bins_ref, amp_ref, _, out_ref, held):
    slots = row_ref.shape[1]
    radial = q_ref.shape[2]
    observers = bins_ref.shape[0]
    count = count_ref[0]
    width = 8

    def fetch(i, _):
        for k in range(width):
            s = i * width + k
            at = cells_ref[s] // radial
            held[:, pl.ds(s, 1), :] = q_ref[:, pl.ds(at, 1), :]
        return 0

    lax.fori_loop(0, (count + width - 1) // width, fetch, 0)
    q = [held[f] for f in range(FIELDS)]
    p = gas_factor * (q[4] - 0.5 * (q[1] * q[1] + q[2] * q[2] + q[3] * q[3]) / q[0])
    turned = jnp.transpose(p)
    which = lax.broadcasted_iota(jnp.int32, (radial, slots), 0)
    here = which == (row_ref[...] & (radial - 1))
    sampled = jnp.sum(jnp.where(here, turned, 0.0), axis=0, keepdims=True) - ref_pressure
    slot = lax.broadcasted_iota(jnp.int32, (1, slots), 1)
    sampled = jnp.where(slot < count, sampled, 0.0)

    contrib = sampled * amp_ref[...]
    first = contrib.astype(jnp.bfloat16).astype(jnp.float32)
    second = contrib - first
    bins = bins_ref[...]
    low = bins & (LOW_BINS - 1)
    high = bins // LOW_BINS
    each = 128 // LOW_BINS
    high_count = BINS // LOW_BINS
    low_iota = lax.broadcasted_iota(jnp.int32, (LOW_BINS, slots), 0)
    high_iota = lax.broadcasted_iota(jnp.int32, (high_count, slots), 0)
    lane = lax.broadcasted_iota(jnp.int32, (high_count, 128), 1)
    for g in range(observers // each):
        left, right = [], []
        for k in range(each):
            o = g * each + k
            hit = high_iota == high[o : o + 1]
            left.append(jnp.where(hit, first[o : o + 1], 0.0).astype(jnp.bfloat16))
            left.append(jnp.where(hit, second[o : o + 1], 0.0).astype(jnp.bfloat16))
            same = low_iota == low[o : o + 1]
            right.append(jnp.where(same, 1.0, 0.0).astype(jnp.bfloat16))
        sums = lax.dot_general(
            jnp.concatenate(left, axis=0),
            jnp.concatenate(right, axis=0),
            (((1,), (1,)), ((), ())),
            preferred_element_type=jnp.float32,
        )
        total = jnp.zeros((high_count, 128), jnp.float32)
        for k in range(each):
            at = 2 * k * high_count
            both = sums[at : at + high_count] + sums[at + high_count : at + 2 * high_count]
            total = jnp.where(lane // LOW_BINS == k, both, total)
        out_ref[:, g, :] = total


def panel_sums(conserved, cells, counts, bins, amplitudes, after):
    fields, planes, sector, radial = conserved.shape
    slots, observers = bins.shape
    flat = conserved.reshape(fields, planes * sector, radial)
    high_count = BINS // LOW_BINS
    full = lambda *shape: pl.BlockSpec(shape, lambda i, *_: (0,) * len(shape))
    return pl.pallas_call(
        panel_kernel,
        grid_spec=pltpu.PrefetchScalarGridSpec(
            num_scalar_prefetch=2,
            grid=(1,),
            in_specs=[
                full(1, slots),
                full(fields, planes * sector, radial),
                full(observers, slots),
                full(observers, slots),
                pl.BlockSpec(memory_space=pl.ANY),
            ],
            out_specs=full(high_count, observers * LOW_BINS // 128, 128),
            scratch_shapes=[pltpu.VMEM((fields, slots, radial), jnp.float32)],
        ),
        out_shape=jax.ShapeDtypeStruct(
            (high_count, observers * LOW_BINS // 128, 128), jnp.float32
        ),
        compiler_params=params(),
        cost_estimate=cost(8 * observers * slots * BINS, 4 * fields * planes * sector * radial),
        name="panel_sums",
    )(cells, counts, cells.reshape(1, slots), flat, bins.T, amplitudes.T, after)


def section_kernel(dtheta, *refs):
    az_ref, q_ref, mine_ref, theirs_ref, early_ref, late_ref, weight_ref, basis_ref = refs[:8]
    out_ref, axial, swirl, local, spec, smooth = refs[8:]
    fields, _, sector, radial = q_ref.shape
    step = pl.program_id(0)
    planes = pl.num_programs(0) - 2
    scale = time_step / 12.0
    chunk = min(sector, 16 * ROWS)
    lane = lax.broadcasted_iota(jnp.int32, (1, radial), 1)
    radius = lane.astype(jnp.float32) + 0.5
    inverse = 1.0 / radius
    near = 8.0 * scale * inverse
    far = scale * inverse
    near_up = jnp.where(lane < radial - 1, near, 0.0)
    near_down = jnp.where(lane >= 1, near, 0.0)
    far_up = jnp.where(lane < radial - 2, far, 0.0)
    far_down = jnp.where(lane >= 2, far, 0.0)
    source = time_step * inverse
    odd = lax.rem(az_ref[0], 2) == 1
    static_planes = axial.shape[0] - 4

    @pl.when(step == 0)
    def _():
        axial[0:2] = jnp.zeros((2,) + axial.shape[1:], jnp.float32)
        axial[planes + 2 : planes + 4] = jnp.zeros((2,) + axial.shape[1:], jnp.float32)
        spec[...] = jnp.zeros_like(spec)
        for k in range(static_planes):
            for f in range(FIELDS):
                rows = slice(k * CYCLES, (k + 1) * CYCLES)
                value = mine_ref[f, rows, :] + theirs_ref[f, rows, :]
                spec[k, f * CYCLES : (f + 1) * CYCLES, :] = value * weight_ref[...]

    @pl.when(step < planes)
    def _():
        slot = lax.rem(step, 3)
        for f in range(FIELDS):
            early = early_ref[f, pl.ds(2 * step, 2), :]
            late = late_ref[f, pl.ds(2 * step, 2), :]
            swirl[slot, f, ROWS - 2 : ROWS, :] = jnp.where(odd, early, late)
            swirl[slot, f, ROWS + sector : ROWS + sector + 2, :] = jnp.where(odd, late, early)

        def body(i, _):
            start = pl.multiple_of(i * chunk, chunk)
            rows = pl.ds(start, chunk)
            q = [q_ref[f, 0, rows, :] for f in range(FIELDS)]
            u, v, w, p = primitives(q)
            along = carried(q, p, u, 1)
            around = carried(q, p, w, 3)
            outward = carried(q, p, v, 2)
            for f in range(FIELDS):
                axial[step + 2, f, rows, :] = along[f]
                swirl[slot, f, pl.ds(start + ROWS, chunk), :] = around[f]
                g = outward[f] * radius
                value = q[f] - near_up * pltpu.roll(g, radial - 1, 1)
                value = value + near_down * pltpu.roll(g, 1, 1)
                value = value + far_up * pltpu.roll(g, radial - 2, 1)
                value = value - far_down * pltpu.roll(g, 2, 1)
                if f == 2:
                    value = value + source * (p + q[3] * w)
                if f == 3:
                    value = value - source * (q[2] * w)
                local[slot, f, rows, :] = value
            return 0

        lax.fori_loop(0, sector // chunk, body, 0)

    @pl.when(step >= 2)
    def _():
        plane = step - 2
        slot = lax.rem(plane, 3)
        turn = scale * inverse / dtheta
        smooth[...] = lax.dot_general(
            basis_ref[...], spec[plane], (((1,), (1,)), ((), ())),
            precision=HIGHEST, preferred_element_type=jnp.float32,
        )

        def body(i, _):
            start = pl.multiple_of(i * chunk, chunk)
            rows = pl.ds(start, chunk)
            for f in range(FIELDS):
                at = lambda k: swirl[slot, f, pl.ds(start + (ROWS + k), chunk), :]
                of = lambda k: axial[plane + 2 + k, f, rows, :]
                around = 8.0 * (at(1) - at(-1)) - (at(2) - at(-2))
                along = 8.0 * (of(1) - of(-1)) - (of(2) - of(-2))
                value = local[slot, f, rows, :] - turn * around - scale * along
                moved = smooth[rows, :]
                if f > 0:
                    moved = pltpu.roll(moved, radial - CYCLES * f, 1)
                out_ref[f, 0, rows, :] = jnp.where(lane < CYCLES, moved, value)
            return 0

        lax.fori_loop(0, sector // chunk, body, 0)


def local_section(conserved, az, mine, theirs, early, late, weights, table):
    fields, planes, sector, radial = conserved.shape
    length = table.shape[0]
    two_back = lambda i: jnp.maximum(i - 2, 0)
    ring = (fields, 2 * planes, radial)
    last = late.shape[1] // ring[1] - 1
    full = lambda a: pl.BlockSpec(a.shape, lambda i, *_: (0,) * a.ndim)
    plane = (fields, 1, sector, radial)
    return pl.pallas_call(
        functools.partial(section_kernel, 2.0 * math.pi / length),
        grid_spec=pltpu.PrefetchScalarGridSpec(
            num_scalar_prefetch=1,
            grid=(planes + 2,),
            in_specs=[
                pl.BlockSpec(plane, lambda i, *_: (0, jnp.minimum(i, planes - 1), 0, 0)),
                full(mine),
                full(theirs),
                full(early),
                pl.BlockSpec(ring, lambda i, *_: (0, last, 0)),
                full(weights),
                here_specs(table, sector),
            ],
            out_specs=pl.BlockSpec(plane, lambda i, *_: (0, two_back(i), 0, 0)),
            scratch_shapes=[
                pltpu.VMEM((planes + 4, fields, sector, radial), jnp.float32),
                pltpu.VMEM((3, fields, sector + 2 * ROWS, radial), jnp.float32),
                pltpu.VMEM((3, fields, sector, radial), jnp.float32),
                pltpu.VMEM((planes, radial, COEFS), jnp.float32),
                pltpu.VMEM((sector, radial), jnp.float32),
            ],
        ),
        out_shape=jax.ShapeDtypeStruct(conserved.shape, jnp.float32),
        compiler_params=params(),
        cost_estimate=cost(
            600 * planes * sector * radial, 10 * 4 * fields * planes * sector * radial
        ),
        name="local_section",
    )(az, conserved, mine, theirs, early, late, weights, table)


def add_kernel(az_ref, part_ref, low_ref, high_ref, spec_low, spec_high, weight_ref, basis_ref, sums_ref, *outs):
    out_ref, signal_ref, padded, turned = outs
    step = pl.program_id(0)
    fields, _, sector, radial = part_ref.shape
    groups = radial // CYCLES - 1
    tail = sector // (groups + 1)
    main = groups * tail
    lane = lax.broadcasted_iota(jnp.int32, (1, radial), 1)
    wide = lane >= CYCLES

    @pl.when(step == 0)
    def _():
        padded[...] = jnp.zeros_like(padded)
        observers, _ = turned.shape
        bins = signal_ref.shape[0]
        total = jnp.sum(sums_ref[...], axis=0)
        for o in range(observers):
            row, at = o * bins // 128, o * bins % 128
            piece = total[row : row + 1]
            turned[o : o + 1, :] = pltpu.roll(piece, 128 - at, 1) if at else piece
        signal_ref[...] = jnp.transpose(turned[...])[:bins]

    def go(ref, spec_ref, slot):
        for f in range(fields):
            rows = slice(slot * CYCLES, (slot + 1) * CYCLES)
            padded[f * CYCLES : (f + 1) * CYCLES, :] = spec_ref[f, rows, :] * weight_ref[...]
        smooth = lax.dot_general(
            basis_ref[...], padded[...], (((1,), (1,)), ((), ())),
            precision=HIGHEST, preferred_element_type=jnp.float32,
        )
        for f in range(fields):
            inner = smooth if f == 0 else pltpu.roll(smooth, radial - CYCLES * f, 1)
            out_ref[f, 0, :main, :] = part_ref[f, 0, :main, :] + jnp.where(
                wide, ref[f, 0], inner[:main]
            )
            rest = inner[main:]
            for g in range(groups):
                moved = pltpu.roll(ref[f, 0, g * tail : (g + 1) * tail, :], CYCLES * (g + 1), 1)
                rest = jnp.where(lane // CYCLES == g + 1, moved, rest)
            out_ref[f, 0, main:, :] = part_ref[f, 0, main:, :] + rest

    for k in range(2):
        pl.when(step == k)(lambda k=k: go(low_ref, spec_low, k))
        pl.when(step == 2 + k)(lambda k=k: go(high_ref, spec_high, k))


def add_edges(section, az, low, high, spec_low, spec_high, weights, table, sums, observers):
    fields, planes, sector, radial = section.shape
    main = low.shape[2]
    bins = sums.shape[1] * sums.shape[2] // observers
    full = lambda a: pl.BlockSpec(a.shape, lambda i, *_: (0,) * a.ndim)
    plane = pl.BlockSpec(
        (fields, 1, sector, radial), lambda i, *_: (0, jnp.where(i < 2, i, planes - 4 + i), 0, 0)
    )
    return pl.pallas_call(
        add_kernel,
        grid_spec=pltpu.PrefetchScalarGridSpec(
            num_scalar_prefetch=1,
            grid=(4,),
            in_specs=[
                plane,
                pl.BlockSpec((fields, 1, main, radial), lambda i, *_: (0, jnp.minimum(i, 1), 0, 0)),
                pl.BlockSpec((fields, 1, main, radial), lambda i, *_: (0, jnp.maximum(i - 2, 0), 0, 0)),
                full(spec_low),
                full(spec_high),
                full(weights),
                here_specs(table, sector),
                full(sums),
            ],
            out_specs=[plane, pl.BlockSpec((bins, observers), lambda i, *_: (0, 0))],
            scratch_shapes=[
                pltpu.VMEM((radial, COEFS), jnp.float32),
                pltpu.VMEM((observers, 128), jnp.float32),
            ],
        ),
        out_shape=[
            jax.ShapeDtypeStruct(section.shape, jnp.float32),
            jax.ShapeDtypeStruct((bins, observers), jnp.float32),
        ],
        input_output_aliases={1: 0},
        compiler_params=params(),
        cost_estimate=cost(8 * fields * sector * radial, 4 * 12 * fields * sector * radial),
        name="add_edges",
    )(az, section, low, high, spec_low, spec_high, weights, table, sums)


def exchanged_sums(partial, observers):
    devices = lax.axis_size("ax") * lax.axis_size("az")
    mine = BINS // devices
    if mine != LOW_BINS:
        partial = partial.reshape(-1, observers, LOW_BINS).transpose(0, 2, 1)
        partial = partial.reshape(devices, mine, observers).transpose(0, 2, 1)
        partial = partial.reshape(devices, observers * mine // 128, 128)
    return lax.all_to_all(partial, ("ax", "az"), split_axis=0, concat_axis=0, tiled=True)


def on_device(conserved, panel_cells, panel_counts, time_bins, amplitudes):
    fields, planes, sector, radial = conserved.shape
    observers = time_bins.shape[1]
    n_ax, n_az = lax.axis_size("ax"), lax.axis_size("az")
    length = sector * n_az
    up = [(i, i + 1) for i in range(n_ax - 1)]
    down = [(j, i) for i, j in up]
    az = lax.axis_index("az").astype(jnp.int32).reshape(1)
    table = jnp.asarray(basis_table(length))
    weights = jnp.asarray(mode_weights(length))

    pair = [(i, i ^ 1) for i in range(n_az)]
    send_up, send_down, early = edge_terms(conserved, az)
    early = lax.ppermute(early, "az", pair)
    low = lax.ppermute(send_up, "ax", up)
    high = lax.ppermute(send_down, "ax", down)

    partial = panel_sums(conserved, panel_cells, panel_counts, time_bins, amplitudes, early)
    sums = exchanged_sums(partial, observers)

    message, later = inner_terms(conserved, az, table, partial)
    edge = (planes + 4) * CYCLES
    mine = jnp.concatenate([message + lax.ppermute(message, "az", pair), later], axis=1)
    pairs = [(i, (i + 1) % n_az) for i in range(1, n_az, 2)]
    theirs = lax.ppermute(mine, "az", pairs + [(j, i) for i, j in pairs])
    late = theirs
    shift = 4
    while shift < n_az:
        mine = mine + theirs
        theirs = lax.ppermute(mine, "az", [(i, (i + shift) % n_az) for i in range(n_az)])
        shift *= 2
    outside = mine[:, planes * CYCLES : edge] + theirs[:, planes * CYCLES : edge]
    spec_low = lax.ppermute(outside[:, : 2 * CYCLES], "ax", up)
    spec_high = lax.ppermute(outside[:, 2 * CYCLES :], "ax", down)

    section = local_section(conserved, az, mine, theirs, early, late, weights, table)
    section, signal = add_edges(
        section, az, low, high, spec_low, spec_high, weights, table, sums, observers
    )
    return (section, signal.T)


def solution(mesh):
    placed = (
        P(None, "ax", "az", None),
        P(("ax", "az")),
        P(("ax", "az")),
        P(("ax", "az"), None),
        P(("ax", "az"), None),
    )
    return jax.shard_map(
        on_device,
        mesh=mesh,
        in_specs=placed,
        out_specs=(P(None, "ax", "az", None), P(None, ("ax", "az"))),
        check_vma=False,
    )
```

time: 107 us -> 74.5 us (0.70)
  Pallas kernels: 56.4 us -> 35.1 us
  blocking collectives: 12.9 us -> 0 us
  starting transfers between devices: 19.3 us -> 24.1 us
  waiting for transfers between devices: 10.1 us -> 7.51 us
  local copies, waits for them, and re-layouts: 5.17 us -> 4.1 us
    pallas_call x1, Pallas kernels: 31.9 us -> 15.7 us  [local_section(): pl.pallas_call(functools.partial(section_kernel, 2.0 * math.pi / length),...]
    all_to_all x1 -> x0, blocking collectives: 12.9 us -> none  [shared_sums(): lax.all_to_all(blocks, 'ax', split_axis=0, concat_axis=0, tiled=True)]
    all_to_all x1, starting transfers between devices: 3.4 us -> 7.94 us  [exchanged_sums(): lax.all_to_all(partial, ('ax', 'az'), split_axis=0, concat_axis=0, tiled=...]
    ppermute x6 -> x5, waiting for transfers between devices: 6.58 us -> 2.1 us  [the longest x1 1.5 us: on_device(): lax.ppermute(message, 'az', pair)]
    pallas_call x5 -> x3, Pallas kernels: 19.5 us -> 16 us  [the longest x1 7.11 us: inner_terms(): pl.pallas_call(functools.partial(inner_kernel, 2.0 * math.pi / length), g...]
    all_to_all x1, waiting for transfers between devices: 3.48 us -> 5.41 us  [exchanged_sums(): lax.all_to_all(partial, ('ax', 'az'), split_axis=0, concat_axis=0, tiled=...]
    pallas_call x1, Pallas kernels: 5 us -> 3.38 us  [panel_sums(): pl.pallas_call(panel_kernel, grid_spec=pltpu.PrefetchScalarGridSpec(num_s...]
    ppermute x6 -> x5, starting transfers between devices: 9.74 us -> 10.4 us  [the longest x1 6.78 us: on_device(): spec_low = lax.ppermute(outside[:, :2 * CYCLES], 'ax', up)]
  transfers between devices with their start and end apart: 9 -> 8, of which waited for: 2 -> 3; matrix products, arithmetic and copies ran while one was open for 3% -> 2% of each run, Pallas kernels for 46% -> 36%
where the time goes in v2:
time: 74.5 us; the launch traced here: 73.2 us
  Pallas kernels  35.1 us (47%)
  starting transfers between devices  24.1 us (32%)
  waiting for transfers between devices  7.51 us (10%)
  local copies, waits for them, and re-layouts  4.1 us (6%)
  between operations  1.47 us (2%)
  other arithmetic  0.97 us (1%)
    pallas_call x1, Pallas kernels, local_section(): pl.pallas_call(functools.partial(section_kernel, 2.0 * math.pi / length),...  15.7 us
    all_to_all x1, starting transfers between devices, exchanged_sums(): lax.all_to_all(partial, ('ax', 'az'), split_axis=0, concat_axis=0, tiled=...  7.94 us
    pallas_call x1, Pallas kernels, inner_terms(): pl.pallas_call(functools.partial(inner_kernel, 2.0 * math.pi / length), g...  7.11 us
    ppermute x1, starting transfers between devices, on_device(): spec_low = lax.ppermute(outside[:, :2 * CYCLES], 'ax', up)  6.78 us
    all_to_all x1, waiting for transfers between devices, exchanged_sums(): lax.all_to_all(partial, ('ax', 'az'), split_axis=0, concat_axis=0, tiled=...  5.41 us
    pallas_call x1, Pallas kernels, add_edges(): pl.pallas_call(add_kernel, grid_spec=pltpu.PrefetchScalarGridSpec(num_sca...  5.06 us
    ppermute x1, starting transfers between devices, on_device(): low = lax.ppermute(send_up, 'ax', up)  4.46 us
    pallas_call x1, Pallas kernels, edge_terms(): pl.pallas_call(edge_kernel, grid_spec=pltpu.PrefetchScalarGridSpec(num_sc...  3.79 us
  transfers between devices with their start and end apart: 8, of which 3 were waited for; matrix products, arithmetic and copies ran while one was open for 2% of the time, Pallas kernels for 36%

profile of v2, /device:TPU:0, one launch (start us, length us, event | category | flops | bytes accessed | tf_op | source)
XLA Modules:
  0.0 73.2 jit_solution(6409083861335935846)
XLA Ops:
  0.6 0.0 slice-start
  0.6 0.0 slice-start.1
  0.7 3.8 %edge_terms.1 = (f32[5,2,240,128]{3,2,1,0:T(8,128)}, f32[5,2,240,128]{3,2,1,0:T(8,128)}, f32[5,16,128]{2,1,0:T(8,128)S(1)}) custom-call(s32[1]{0:T(128)} %bitcast.az_ref.refs_0_, f32[5,8,256,128]{3,2,1,0:T(8,128)} %refs_1_.3, f32[5,8,256,128]{3,2,1,0:T(8,128)} %refs_1_.3), custom_call_target="tpu_custom_call" | custom-call | flops 13107200 | bytes 5242880 | tf_op jit(solution)/shard_map/edge_terms/pallas_call | solution.py:123
  4.5 0.5 collective-permute-start
  4.9 4.5 %collective-permute-start.3 = (f32[5,2,240,128]{3,2,1,0:T(8,128)}, f32[5,2,240,128]{3,2,1,0:T(8,128)S(1)}, u32[]{:S(2)}, u32[]{:S(2)}) collective-permute-start(f32[5,2,240,128]{3,2,1,0:T(8,128)} %get-tuple-element.12), channel_id=1, source_target_pairs={{0,4},{4,8},{8,12},{12,16},{16,20},{20,24},{24,28},{1,5},{5,9},{9,... | collective-permute-start | bytes 3686408 | tf_op jit(solution)/shard_map/ppermute | solution.py:632
  9.4 1.3 %collective-permute-start.4 = (f32[5,2,240,128]{3,2,1,0:T(8,128)}, f32[5,2,240,128]{3,2,1,0:T(8,128)S(1)}, u32[]{:S(2)}, u32[]{:S(2)}) collective-permute-start(f32[5,2,240,128]{3,2,1,0:T(8,128)} %get-tuple-element.13), channel_id=1, source_target_pairs={{4,0},{8,4},{12,8},{16,12},{20,16},{24,20},{28,24},{5,1},{9,5},{13... | collective-permute-start | bytes 3686408 | tf_op jit(solution)/shard_map/ppermute | solution.py:633
  11.3 0.0 collective-permute-done._.refs_4_
  11.4 0.0 copy-start
  11.4 3.4 %panel_sums.1.refs_6_ = f32[32,16,128]{2,1,0:T(8,128)} custom-call(s32[512]{0:T(512)S(1)} %copy-done.7, s32[1]{0:T(128)S(6)} %copy.11.count_ref, s32[1,512]{1,0:T(1,128)S(1)} %bitcast.11, f32[5,2048,128]{2,1,0:T(8,128)S(1)} %bitcast.8, s32[64,512]{1,0:T(8,128)S(1)} %bitcast.9, f32[64,512]{1,0:T(8,128)S(1)} %bitcast.10, ...), custom_call_target="tpu_custom_call" | custom-call | flops 268435456 | bytes 5242880 | tf_op jit(solution)/shard_map/panel_sums/pallas_call | solution.py:364
  14.8 0.6 copy-done.1
  15.4 7.1 %inner_terms.1 = (f32[5,96,128]{2,1,0:T(8,128)S(1)}, f32[5,16,128]{2,1,0:T(8,128)S(1)}) custom-call(s32[1]{0:T(128)} %bitcast.az_ref.refs_0_, f32[5,8,256,128]{3,2,1,0:T(8,128)} %refs_1_.3, f32[5,8,256,128]{3,2,1,0:T(8,128)} %refs_1_.3, f32[1024,128]{1,0:T(8,128)S(1)} %copy-done, f32[1024,128]{1,0:T(8,128)S(1)} %copy-done, f32[1024,128]{1,0:T(8,128)S(1)} %copy-done, ...), custom_call_target="tpu_custom_call" | custom-call | flops 251658240 | bytes 5242880 | tf_op jit(solution)/shard_map/inner_terms/pallas_call | solution.py:267
  22.5 0.1 collective-permute-start.1
  22.6 1.5 %collective-permute-done.1 = f32[5,96,128]{2,1,0:T(8,128)S(1)} collective-permute-done((f32[5,96,128]{2,1,0:T(8,128)S(1)}, f32[5,96,128]{2,1,0:T(8,128)S(1)}, u32[]{:S(2)}, u32[]{:S(2)}) %collective-permute-start.1) | collective-permute-done | bytes 245792 | tf_op jit(solution)/shard_map/ppermute | solution.py:640
  24.2 0.0 copy-start.8
  24.2 0.7 copy-done.8
  24.9 1.8 %collective-permute-start.2 = (f32[5,112,128]{2,1,0:T(8,128)S(1)}, f32[5,112,128]{2,1,0:T(8,128)S(1)}, u32[]{:S(2)}, u32[]{:S(2)}) collective-permute-start(f32[5,112,128]{2,1,0:T(8,128)S(1)} %pad_maximum_fusion.refs_2_), channel_id=1, source_target_pairs={{1,2},{3,0},{2,1},{0,3},{5,6},{7,4},{6,5},{4,7},{9,10},{11,8},{10,... | collective-permute-start | bytes 860168 | tf_op jit(solution)/shard_map/ppermute | solution.py:642
  26.7 7.9 %all-to-all-start = ((f32[32,16,128]{2,1,0:T(8,128)}), f32[32,16,128]{2,1,0:T(8,128)}, u32[]{:S(2)}, u32[]{:S(2)}) async-start(f32[32,16,128]{2,1,0:T(8,128)} %panel_sums.1.refs_6_), calls=%async_computation | async-start | bytes 524288 | tf_op jit(solution)/shard_map/all_to_all | solution.py:615
  34.6 0.0 collective-permute-done.2.refs_3_.refs_5_
  34.6 0.9 %slice_add_fusion = f32[5,32,128]{2,1,0:T(8,128)S(1)} fusion(f32[5,112,128]{2,1,0:T(8,128)S(1)} %collective-permute-done.2.refs_3_.refs_5_, f32[5,96,128]{2,1,0:T(8,128)} %copy-done.8), kind=kLoop, calls=%fused_computation.1 | loop fusion | flops 20480 | bytes 245760 | tf_op jit(solution)/shard_map/add | solution.py:649
  35.5 0.6 fusion
  36.2 1.3 %collective-permute-start.6 = (f32[5,16,128]{2,1,0:T(8,128)}, f32[5,16,128]{2,1,0:T(8,128)}, u32[]{:S(2)}, u32[]{:S(2)}) collective-permute-start(f32[5,16,128]{2,1,0:T(8,128)} %get-tuple-element.16), channel_id=1, source_target_pairs={{4,0},{8,4},{12,8},{16,12},{20,16},{24,20},{28,24},{5,1},{9,5},{13... | collective-permute-start | bytes 122888 | tf_op jit(solution)/shard_map/ppermute | solution.py:651
  37.5 6.8 %collective-permute-start.5 = (f32[5,16,128]{2,1,0:T(8,128)}, f32[5,16,128]{2,1,0:T(8,128)}, u32[]{:S(2)}, u32[]{:S(2)}) collective-permute-start(f32[5,16,128]{2,1,0:T(8,128)} %get-tuple-element.17), channel_id=1, source_target_pairs={{0,4},{4,8},{8,12},{12,16},{16,20},{20,24},{24,28},{1,5},{5,9},{9,... | collective-permute-start | bytes 122888 | tf_op jit(solution)/shard_map/ppermute | solution.py:650
  44.3 0.8 %copy-done.2 = f32[5,16,128]{2,1,0:T(8,128)S(1)} copy-done((f32[5,16,128]{2,1,0:T(8,128)S(1)}, f32[5,16,128]{2,1,0:T(8,128)}, u32[]{:S(2)}) %copy-start.2) | copy-done | bytes 40984
  45.0 0.7 copy-done.5
  45.7 15.7 %local_section.1.part_ref = f32[5,8,256,128]{3,2,1,0:T(8,128)} custom-call(s32[1]{0:T(128)} %bitcast.az_ref.refs_0_, f32[5,8,256,128]{3,2,1,0:T(8,128)} %refs_1_.3, f32[5,112,128]{2,1,0:T(8,128)S(1)} %pad_maximum_fusion.refs_2_, f32[5,112,128]{2,1,0:T(8,128)S(1)} %collective-permute-done.2.refs_3_.refs_5_, f32[5,16,128]{2,1,0:T(8,128)S(1)} %copy-done.2, ...), custom_call_target="tpu_custom_call" | custom-call | flops 157286400 | bytes 52428800 | tf_op jit(solution)/shard_map/local_section/pallas_call | solution.py:490
  61.5 5.4 %all-to-all-done.sums_ref = f32[32,16,128]{2,1,0:T(8,128)} async-done(((f32[32,16,128]{2,1,0:T(8,128)}), f32[32,16,128]{2,1,0:T(8,128)}, u32[]{:S(2)}, u32[]{:S(2)}) %all-to-all-start) | async-done | bytes 262176 | tf_op jit(solution)/shard_map/all_to_all | solution.py:615
  66.9 0.0 collective-permute-done.6.spec_high
  66.9 0.6 collective-permute-done.5.spec_low
  67.5 0.0 collective-permute-done.3.low_ref
  67.5 0.0 collective-permute-done.4.high_ref
  67.5 0.7 copy-done.6
  68.2 5.1 %add_edges.1 = (f32[5,8,256,128]{3,2,1,0:T(8,128)}, f32[32,64]{1,0:T(8,128)}) custom-call(s32[1]{0:T(128)} %bitcast.az_ref.refs_0_, f32[5,8,256,128]{3,2,1,0:T(8,128)} %local_section.1.part_ref, f32[5,2,240,128]{3,2,1,0:T(8,128)S(1)} %collective-permute-done.3.low_ref, ...), custom_call_target="tpu_custom_call", output_to_operand_aliasing={{0}: (1, {})} | custom-call | flops 1310720 | bytes 7864320 | tf_op jit(solution)/shard_map/add_edges/pallas_call | solution.py:576
  (16 shorter events, 0.1 us)
Async XLA Ops:
  0.6 10.7 %slice-start = ((s8[5242880]{0:T(1024)(128)(4,1)}), s8[4194304]{0:T(1024)(128)(4,1)S(1)}, s32[]{:S(2)}) async-start(s8[5242880]{0:T(1024)(128)(4,1)} %bitcast.6), calls=%async_computation.1 | async-start | bytes 8388608
  0.6 10.7 %slice-start.1 = ((s8[5242880]{0:T(1024)(128)(4,1)}), s8[1048576]{0:T(1024)(128)(4,1)S(1)}, s32[]{:S(2)}) async-start(s8[5242880]{0:T(1024)(128)(4,1)} %bitcast.6), calls=%async_computation.2 | async-start | bytes 2097152
  0.7 10.7 %copy-start.3 = (s32[512,64]{0,1:T(8,128)S(1)}, s32[512,64]{0,1:T(8,128)}, u32[]{:S(2)}) copy-start(s32[512,64]{0,1:T(8,128)} %param.10) | copy-start | bytes 393220
  0.7 10.7 %copy-start.4 = (f32[512,64]{0,1:T(8,128)S(1)}, f32[512,64]{0,1:T(8,128)}, u32[]{:S(2)}) copy-start(f32[512,64]{0,1:T(8,128)} %param.11) | copy-start | bytes 393220
  0.7 10.7 %copy-start.7 = (s32[512]{0:T(512)S(1)}, s32[512]{0:T(512)}, u32[]{:S(2)}) copy-start(s32[512]{0:T(512)} %cells_ref.1) | copy-start | bytes 6148
  4.5 6.9 %collective-permute-start = (f32[5,16,128]{2,1,0:T(8,128)S(1)}, f32[5,16,128]{2,1,0:T(8,128)S(1)}, u32[]{:S(2)}, u32[]{:S(2)}) collective-permute-start(f32[5,16,128]{2,1,0:T(8,128)S(1)} %get-tuple-element.9), channel_id=1, source_target_pairs={{0,1},{1,0},{2,3},{3,2},{4,5},{5,4},{6,7},{7,6},{8,9},{9,8},{10,11... | collective-permute-start | bytes 122888 | tf_op jit(solution)/shard_map/ppermute | solution.py:631
  4.9 62.5 %collective-permute-start.3 = (f32[5,2,240,128]{3,2,1,0:T(8,128)}, f32[5,2,240,128]{3,2,1,0:T(8,128)S(1)}, u32[]{:S(2)}, u32[]{:S(2)}) collective-permute-start(f32[5,2,240,128]{3,2,1,0:T(8,128)} %get-tuple-element.12), channel_id=1, source_target_pairs={{0,4},{4,8},{8,12},{12,16},{16,20},{20,24},{24,28},{1,5},{5,9},{9,... | collective-permute-start | bytes 3686408 | tf_op jit(solution)/shard_map/ppermute | solution.py:632
  9.4 58.1 %collective-permute-start.4 = (f32[5,2,240,128]{3,2,1,0:T(8,128)}, f32[5,2,240,128]{3,2,1,0:T(8,128)S(1)}, u32[]{:S(2)}, u32[]{:S(2)}) collective-permute-start(f32[5,2,240,128]{3,2,1,0:T(8,128)} %get-tuple-element.13), channel_id=1, source_target_pairs={{4,0},{8,4},{12,8},{16,12},{20,16},{24,20},{28,24},{5,1},{9,5},{13... | collective-permute-start | bytes 3686408 | tf_op jit(solution)/shard_map/ppermute | solution.py:633
  11.4 4.0 %copy-start = (f32[1024,128]{1,0:T(8,128)S(1)}, f32[1024,128]{1,0:T(8,128)}, u32[]{:S(2)}) copy-start(f32[1024,128]{1,0:T(8,128)} %constant.8.clone.refs_3_.refs_4_.refs_5_.refs_7_.basis_ref) | copy-start | bytes 1572868
  14.8 0.6 copy-start.1
  22.5 1.6 %collective-permute-start.1 = (f32[5,96,128]{2,1,0:T(8,128)S(1)}, f32[5,96,128]{2,1,0:T(8,128)S(1)}, u32[]{:S(2)}, u32[]{:S(2)}) collective-permute-start(f32[5,96,128]{2,1,0:T(8,128)S(1)} %get-tuple-element.10), channel_id=1, source_target_pairs={{0,1},{1,0},{2,3},{3,2},{4,5},{5,4},{6,7},{7,6},{8,9},{9,8},{10,11... | collective-permute-start | bytes 737288 | tf_op jit(solution)/shard_map/ppermute | solution.py:640
  24.2 0.7 copy-start.8
  24.9 9.8 %collective-permute-start.2 = (f32[5,112,128]{2,1,0:T(8,128)S(1)}, f32[5,112,128]{2,1,0:T(8,128)S(1)}, u32[]{:S(2)}, u32[]{:S(2)}) collective-permute-start(f32[5,112,128]{2,1,0:T(8,128)S(1)} %pad_maximum_fusion.refs_2_), channel_id=1, source_target_pairs={{1,2},{3,0},{2,1},{0,3},{5,6},{7,4},{6,5},{4,7},{9,10},{11,8},{10,... | collective-permute-start | bytes 860168 | tf_op jit(solution)/shard_map/ppermute | solution.py:642
  26.7 40.2 %all-to-all-start = ((f32[32,16,128]{2,1,0:T(8,128)}), f32[32,16,128]{2,1,0:T(8,128)}, u32[]{:S(2)}, u32[]{:S(2)}) async-start(f32[32,16,128]{2,1,0:T(8,128)} %panel_sums.1.refs_6_), calls=%async_computation | async-start | bytes 524288 | tf_op jit(solution)/shard_map/all_to_all | solution.py:615
  36.2 30.7 %collective-permute-start.6 = (f32[5,16,128]{2,1,0:T(8,128)}, f32[5,16,128]{2,1,0:T(8,128)}, u32[]{:S(2)}, u32[]{:S(2)}) collective-permute-start(f32[5,16,128]{2,1,0:T(8,128)} %get-tuple-element.16), channel_id=1, source_target_pairs={{4,0},{8,4},{12,8},{16,12},{20,16},{24,20},{28,24},{5,1},{9,5},{13... | collective-permute-start | bytes 122888 | tf_op jit(solution)/shard_map/ppermute | solution.py:651
  37.5 30.0 %collective-permute-start.5 = (f32[5,16,128]{2,1,0:T(8,128)}, f32[5,16,128]{2,1,0:T(8,128)}, u32[]{:S(2)}, u32[]{:S(2)}) collective-permute-start(f32[5,16,128]{2,1,0:T(8,128)} %get-tuple-element.17), channel_id=1, source_target_pairs={{0,4},{4,8},{8,12},{12,16},{16,20},{20,24},{24,28},{1,5},{5,9},{9,... | collective-permute-start | bytes 122888 | tf_op jit(solution)/shard_map/ppermute | solution.py:650
  44.2 0.8 %copy-start.2 = (f32[5,16,128]{2,1,0:T(8,128)S(1)}, f32[5,16,128]{2,1,0:T(8,128)}, u32[]{:S(2)}) copy-start(f32[5,16,128]{2,1,0:T(8,128)} %copy-done.1) | copy-start | bytes 122884
  45.0 0.7 copy-start.5
  67.5 0.7 copy-start.6

commit v3 on v2

--- a/solution.py
+++ b/solution.py
@@ -143,17 +143,13 @@
     )(az, conserved, conserved)
 
 
-def here_specs(table, sector):
-    return pl.BlockSpec((sector, COEFS), lambda i, az, *_: (az[0], 0))
-
-
 def inner_kernel(dtheta, *refs):
-    az_ref, q_ref, rim_ref, before_ref, here_ref, after_ref, _ = refs[:7]
-    message_ref, later_ref, local, swirl, outside = refs[7:]
+    az_ref, q_ref, rim_ref, basis_ref, _ = refs[:5]
+    message_ref, later_ref, local, swirl, outside = refs[5:]
     fields, planes, sector, radial = q_ref.shape
     group = 2 * CYCLES
     scale = time_step / 12.0
-    chunk = min(sector, 8 * ROWS)
+    chunk = min(sector, 32 * ROWS)
     lane = lax.broadcasted_iota(jnp.int32, (1, radial), 1)
     cycle = lane & (group - 1)
     plane = lane // group
@@ -234,8 +230,6 @@
 
     lax.fori_loop(0, sector // chunk, body2, 0)
 
-    basis = jnp.concatenate([before_ref[...], here_ref[...], after_ref[...]], axis=0)
-
     def transform(rows, table):
         return lax.dot_general(
             rows, table, (((0,), (0,)), ((), ())),
@@ -243,10 +237,10 @@
         )
 
     for f in range(FIELDS):
-        own = transform(local[f], basis)
+        own = transform(local[f], basis_ref[: sector + 2 * ROWS, :])
         for k in range(planes):
             message_ref[f, k * CYCLES : (k + 1) * CYCLES, :] = own[k * group : k * group + CYCLES]
-        other = transform(outside[f], here_ref[...])
+        other = transform(outside[f], basis_ref[ROWS : ROWS + sector, :])
         for s, k in enumerate((0, 1, planes - 2, planes - 1)):
             at = (planes + s) * CYCLES
             message_ref[f, at : at + CYCLES, :] = other[k * group : k * group + CYCLES]
@@ -256,14 +250,12 @@
             later_ref[f, 2 * k : 2 * k + 2, :] = flux[f]
 
 
-def inner_terms(conserved, az, table, after):
+def inner_terms(conserved, az, basis, length, after):
     fields, planes, sector, radial = conserved.shape
-    length = table.shape[0]
     message = (fields, (planes + 4) * CYCLES, COEFS)
     later = (fields, 2 * planes, radial)
     full = lambda *shape: pl.BlockSpec(shape, lambda i, *_: (0,) * len(shape))
     tiles = sector // ROWS
-    wrap = lambda k: lax.rem(k + length // ROWS, length // ROWS)
     return pl.pallas_call(
         functools.partial(inner_kernel, 2.0 * math.pi / length),
         grid_spec=pltpu.PrefetchScalarGridSpec(
@@ -275,9 +267,7 @@
                     (fields, planes, ROWS, radial),
                     lambda i, az: (0, 0, (tiles - 1) * lax.rem(az[0], 2), 0),
                 ),
-                pl.BlockSpec((ROWS, COEFS), lambda i, az: (wrap(az[0] * tiles - 1), 0)),
-                here_specs(table, sector),
-                pl.BlockSpec((ROWS, COEFS), lambda i, az: (wrap((az[0] + 1) * tiles), 0)),
+                full(*basis.shape),
                 pl.BlockSpec(memory_space=pl.ANY),
             ],
             out_specs=[full(*message), full(*later)],
@@ -294,10 +284,10 @@
         compiler_params=params(),
         cost_estimate=cost(60 * sector * radial * COEFS, 4 * fields * planes * sector * radial),
         name="inner_terms",
-    )(az, conserved, conserved, table, table, table, after)
-
-
-def panel_kernel(cells_ref, count_ref, row_ref, q_ref, bins_ref, amp_ref, _, out_ref, held):
+    )(az, conserved, conserved, basis, after)
+
+
+def panel_kernel(n_ax, n_az, cells_ref, count_ref, row_ref, q_ref, bins_ref, amp_ref, _, out_ref, held):
     slots = row_ref.shape[1]
     radial = q_ref.shape[2]
     observers = bins_ref.shape[0]
@@ -327,6 +317,8 @@
     bins = bins_ref[...]
     low = bins & (LOW_BINS - 1)
     high = bins // LOW_BINS
+    if n_ax * n_az * LOW_BINS == BINS:
+        high = (high % n_az) * n_ax + high // n_az
     each = 128 // LOW_BINS
     high_count = BINS // LOW_BINS
     low_iota = lax.broadcasted_iota(jnp.int32, (LOW_BINS, slots), 0)
@@ -362,7 +354,7 @@
     high_count = BINS // LOW_BINS
     full = lambda *shape: pl.BlockSpec(shape, lambda i, *_: (0,) * len(shape))
     return pl.pallas_call(
-        panel_kernel,
+        functools.partial(panel_kernel, lax.axis_size("ax"), lax.axis_size("az")),
         grid_spec=pltpu.PrefetchScalarGridSpec(
             num_scalar_prefetch=2,
             grid=(1,),
@@ -386,13 +378,13 @@
 
 
 def section_kernel(dtheta, *refs):
-    az_ref, q_ref, mine_ref, theirs_ref, early_ref, late_ref, weight_ref, basis_ref = refs[:8]
-    out_ref, axial, swirl, local, spec, smooth = refs[8:]
+    az_ref, q_ref, mine_ref, theirs_ref, early_ref, late_ref, basis_ref = refs[:7]
+    out_ref, axial, swirl, local, spec, smooth = refs[7:]
     fields, _, sector, radial = q_ref.shape
     step = pl.program_id(0)
     planes = pl.num_programs(0) - 2
     scale = time_step / 12.0
-    chunk = min(sector, 16 * ROWS)
+    chunk = min(sector, 32 * ROWS)
     lane = lax.broadcasted_iota(jnp.int32, (1, radial), 1)
     radius = lane.astype(jnp.float32) + 0.5
     inverse = 1.0 / radius
@@ -415,7 +407,7 @@
             for f in range(FIELDS):
                 rows = slice(k * CYCLES, (k + 1) * CYCLES)
                 value = mine_ref[f, rows, :] + theirs_ref[f, rows, :]
-                spec[k, f * CYCLES : (f + 1) * CYCLES, :] = value * weight_ref[...]
+                spec[k, f * CYCLES : (f + 1) * CYCLES, :] = value * basis_ref[sector + 2 * ROWS :, :]
 
     @pl.when(step < planes)
     def _():
@@ -457,7 +449,7 @@
         slot = lax.rem(plane, 3)
         turn = scale * inverse / dtheta
         smooth[...] = lax.dot_general(
-            basis_ref[...], spec[plane], (((1,), (1,)), ((), ())),
+            basis_ref[ROWS : ROWS + sector, :], spec[plane], (((1,), (1,)), ((), ())),
             precision=HIGHEST, preferred_element_type=jnp.float32,
         )
 
@@ -479,9 +471,8 @@
         lax.fori_loop(0, sector // chunk, body, 0)
 
 
-def local_section(conserved, az, mine, theirs, early, late, weights, table):
+def local_section(conserved, az, mine, theirs, early, late, basis, length):
     fields, planes, sector, radial = conserved.shape
-    length = table.shape[0]
     two_back = lambda i: jnp.maximum(i - 2, 0)
     ring = (fields, 2 * planes, radial)
     last = late.shape[1] // ring[1] - 1
@@ -498,8 +489,7 @@
                 full(theirs),
                 full(early),
                 pl.BlockSpec(ring, lambda i, *_: (0, last, 0)),
-                full(weights),
-                here_specs(table, sector),
+                full(basis),
             ],
             out_specs=pl.BlockSpec(plane, lambda i, *_: (0, two_back(i), 0, 0)),
             scratch_shapes=[
@@ -516,10 +506,10 @@
             600 * planes * sector * radial, 10 * 4 * fields * planes * sector * radial
         ),
         name="local_section",
-    )(az, conserved, mine, theirs, early, late, weights, table)
-
-
-def add_kernel(az_ref, part_ref, low_ref, high_ref, spec_low, spec_high, weight_ref, basis_ref, sums_ref, *outs):
+    )(az, conserved, mine, theirs, early, late, basis)
+
+
+def add_kernel(part_ref, low_ref, high_ref, spec_low, spec_high, basis_ref, sums_ref, *outs):
     out_ref, signal_ref, padded, turned = outs
     step = pl.program_id(0)
     fields, _, sector, radial = part_ref.shape
@@ -541,12 +531,14 @@
             turned[o : o + 1, :] = pltpu.roll(piece, 128 - at, 1) if at else piece
         signal_ref[...] = jnp.transpose(turned[...])[:bins]
 
+    weight = basis_ref[sector + 2 * ROWS :, :]
+
     def go(ref, spec_ref, slot):
         for f in range(fields):
             rows = slice(slot * CYCLES, (slot + 1) * CYCLES)
-            padded[f * CYCLES : (f + 1) * CYCLES, :] = spec_ref[f, rows, :] * weight_ref[...]
+            padded[f * CYCLES : (f + 1) * CYCLES, :] = spec_ref[f, rows, :] * weight
         smooth = lax.dot_general(
-            basis_ref[...], padded[...], (((1,), (1,)), ((), ())),
+            basis_ref[ROWS : ROWS + sector, :], padded[...], (((1,), (1,)), ((), ())),
             precision=HIGHEST, preferred_element_type=jnp.float32,
         )
         for f in range(fields):
@@ -565,7 +557,7 @@
         pl.when(step == 2 + k)(lambda k=k: go(high_ref, spec_high, k))
 
 
-def add_edges(section, az, low, high, spec_low, spec_high, weights, table, sums, observers):
+def add_edges(section, low, high, spec_low, spec_high, basis, sums, observers):
     fields, planes, sector, radial = section.shape
     main = low.shape[2]
     bins = sums.shape[1] * sums.shape[2] // observers
@@ -576,7 +568,7 @@
     return pl.pallas_call(
         add_kernel,
         grid_spec=pltpu.PrefetchScalarGridSpec(
-            num_scalar_prefetch=1,
+            num_scalar_prefetch=0,
             grid=(4,),
             in_specs=[
                 plane,
@@ -584,8 +576,7 @@
                 pl.BlockSpec((fields, 1, main, radial), lambda i, *_: (0, jnp.maximum(i - 2, 0), 0, 0)),
                 full(spec_low),
                 full(spec_high),
-                full(weights),
-                here_specs(table, sector),
+                full(basis),
                 full(sums),
             ],
             out_specs=[plane, pl.BlockSpec((bins, observers), lambda i, *_: (0, 0))],
@@ -598,21 +589,22 @@
             jax.ShapeDtypeStruct(section.shape, jnp.float32),
             jax.ShapeDtypeStruct((bins, observers), jnp.float32),
         ],
-        input_output_aliases={1: 0},
+        input_output_aliases={0: 0},
         compiler_params=params(),
         cost_estimate=cost(8 * fields * sector * radial, 4 * 12 * fields * sector * radial),
         name="add_edges",
-    )(az, section, low, high, spec_low, spec_high, weights, table, sums)
+    )(section, low, high, spec_low, spec_high, basis, sums)
 
 
 def exchanged_sums(partial, observers):
-    devices = lax.axis_size("ax") * lax.axis_size("az")
-    mine = BINS // devices
+    n_ax, n_az = lax.axis_size("ax"), lax.axis_size("az")
+    mine = BINS // (n_ax * n_az)
     if mine != LOW_BINS:
         partial = partial.reshape(-1, observers, LOW_BINS).transpose(0, 2, 1)
-        partial = partial.reshape(devices, mine, observers).transpose(0, 2, 1)
-        partial = partial.reshape(devices, observers * mine // 128, 128)
-    return lax.all_to_all(partial, ("ax", "az"), split_axis=0, concat_axis=0, tiled=True)
+        partial = partial.reshape(n_ax, n_az, mine, observers).transpose(1, 0, 3, 2)
+    blocks = partial.reshape(n_az, n_ax, observers * mine // 128, 128)
+    blocks = lax.all_to_all(blocks, "az", split_axis=0, concat_axis=0, tiled=True).sum(axis=0)
+    return lax.all_to_all(blocks, "ax", split_axis=0, concat_axis=0, tiled=True)
 
 
 def on_device(conserved, panel_cells, panel_counts, time_bins, amplitudes):
@@ -623,8 +615,10 @@
     up = [(i, i + 1) for i in range(n_ax - 1)]
     down = [(j, i) for i, j in up]
     az = lax.axis_index("az").astype(jnp.int32).reshape(1)
-    table = jnp.asarray(basis_table(length))
-    weights = jnp.asarray(mode_weights(length))
+    table = basis_table(length)
+    table = jnp.asarray(np.concatenate([table[-ROWS:], table, table[:ROWS]], axis=0))
+    basis = lax.dynamic_slice_in_dim(table, az[0] * sector, sector + 2 * ROWS, axis=0)
+    basis = jnp.concatenate([basis, jnp.asarray(mode_weights(length))], axis=0)
 
     pair = [(i, i ^ 1) for i in range(n_az)]
     send_up, send_down, early = edge_terms(conserved, az)
@@ -635,7 +629,7 @@
     partial = panel_sums(conserved, panel_cells, panel_counts, time_bins, amplitudes, early)
     sums = exchanged_sums(partial, observers)
 
-    message, later = inner_terms(conserved, az, table, partial)
+    message, later = inner_terms(conserved, az, basis, length, partial)
     edge = (planes + 4) * CYCLES
     mine = jnp.concatenate([message + lax.ppermute(message, "az", pair), later], axis=1)
     pairs = [(i, (i + 1) % n_az) for i in range(1, n_az, 2)]
@@ -650,9 +644,9 @@
     spec_low = lax.ppermute(outside[:, : 2 * CYCLES], "ax", up)
     spec_high = lax.ppermute(outside[:, 2 * CYCLES :], "ax", down)
 
-    section = local_section(conserved, az, mine, theirs, early, late, weights, table)
+    section = local_section(pltpu.with_memory_space_constraint(conserved, pltpu.HBM), az, mine, theirs, early, late, basis, length)
     section, signal = add_edges(
-        section, az, low, high, spec_low, spec_high, weights, table, sums, observers
+        section, low, high, spec_low, spec_high, basis, sums, observers
     )
     return (section, signal.T)
 

time: 74.5 us -> 71.9 us (0.965)
  blocking collectives: 0 us -> 12 us
  waiting for transfers between devices: 7.51 us -> 1.16 us
  starting transfers between devices: 24.1 us -> 19.5 us
  Pallas kernels: 35.1 us -> 31.5 us
    all_to_all x0 -> x1, blocking collectives: none -> 12 us  [exchanged_sums(): lax.all_to_all(blocks, 'az', split_axis=0, concat_axis=0, tiled=True)]
    all_to_all x1, waiting for transfers between devices: 5.41 us -> 0.01 us  [exchanged_sums(): return lax.all_to_all(blocks, 'ax', split_axis=0, concat_axis=0, tiled=True)]
    pallas_call x1, Pallas kernels: 7.11 us -> 4.22 us  [inner_terms(): pl.pallas_call(functools.partial(inner_kernel, 2.0 * math.pi / length), g...]
    ppermute x1, starting transfers between devices: 6.78 us -> 4.55 us  [on_device(): spec_low = lax.ppermute(outside[:, :2 * CYCLES], 'ax', up)]
    ppermute x1, starting transfers between devices: 1.82 us -> 0.07 us  [on_device(): theirs = lax.ppermute(mine, 'az', pairs + [(j, i) for i, j in pairs])]
    pallas_call x1, Pallas kernels: 15.7 us -> 14.1 us  [local_section(): pl.pallas_call(functools.partial(section_kernel, 2.0 * math.pi / length),...]
    reduce_sum x0 -> x1, other arithmetic: none -> 1.6 us  [exchanged_sums(): lax.all_to_all(blocks, 'az', split_axis=0, concat_axis=0, tiled=True)]
    all_to_all x1, starting transfers between devices: 7.94 us -> 6.41 us  [exchanged_sums(): return lax.all_to_all(blocks, 'ax', split_axis=0, concat_axis=0, tiled=True)]
  transfers between devices with their start and end apart: 8 -> 8, of which waited for: 3 -> 1; matrix products, arithmetic and copies ran while one was open for 2% -> 4% of each run, Pallas kernels for 36% -> 32%
where the time goes in v3:
time: 71.9 us; the launch traced here: 70.8 us
  Pallas kernels  31.5 us (44%)
  starting transfers between devices  19.5 us (27%)
  blocking collectives  12 us (17%)
  local copies, waits for them, and re-layouts  3.44 us (5%)
  other arithmetic  1.68 us (2%)
  between operations  1.49 us (2%)
  waiting for transfers between devices  1.16 us (2%)
    pallas_call x1, Pallas kernels, local_section(): pl.pallas_call(functools.partial(section_kernel, 2.0 * math.pi / length),...  14.1 us
    all_to_all x1, blocking collectives, exchanged_sums(): lax.all_to_all(blocks, 'az', split_axis=0, concat_axis=0, tiled=True)  12 us
    all_to_all x1, starting transfers between devices, exchanged_sums(): return lax.all_to_all(blocks, 'ax', split_axis=0, concat_axis=0, tiled=True)  6.41 us
    pallas_call x1, Pallas kernels, add_edges(): pl.pallas_call(add_kernel, grid_spec=pltpu.PrefetchScalarGridSpec(num_sca...  5.14 us
    ppermute x1, starting transfers between devices, on_device(): spec_low = lax.ppermute(outside[:, :2 * CYCLES], 'ax', up)  4.55 us
    ppermute x1, starting transfers between devices, on_device(): low = lax.ppermute(send_up, 'ax', up)  4.46 us
    pallas_call x1, Pallas kernels, panel_sums(): pl.pallas_call(functools.partial(panel_kernel, lax.axis_size('ax'), lax.a...  4.28 us
    pallas_call x1, Pallas kernels, inner_terms(): pl.pallas_call(functools.partial(inner_kernel, 2.0 * math.pi / length), g...  4.22 us
  transfers between devices with their start and end apart: 8, of which 1 were waited for; matrix products, arithmetic and copies ran while one was open for 4% of the time, Pallas kernels for 32%

profile of v3, /device:TPU:0, one launch (start us, length us, event | category | flops | bytes accessed | tf_op | source)
XLA Modules:
  0.0 70.8 jit_solution(16605411825677936250)
XLA Ops:
  0.6 0.0 copy-start.5
  0.6 0.0 copy-start.2
  0.7 0.0 copy-start.3
  0.7 0.0 copy-start.4
  0.7 3.8 %edge_terms.1 = (f32[5,2,240,128]{3,2,1,0:T(8,128)}, f32[5,2,240,128]{3,2,1,0:T(8,128)}, f32[5,16,128]{2,1,0:T(8,128)S(1)}) custom-call(s32[1]{0:T(128)} %bitcast.az_ref.refs_0_, f32[5,8,256,128]{3,2,1,0:T(8,128)} %refs_1_.3, f32[5,8,256,128]{3,2,1,0:T(8,128)} %refs_1_.3), custom_call_target="tpu_custom_call" | custom-call | flops 13107200 | bytes 5242880 | tf_op jit(solution)/shard_map/edge_terms/pallas_call | solution.py:123
  4.4 0.5 collective-permute-start
  4.9 4.5 %collective-permute-start.3 = (f32[5,2,240,128]{3,2,1,0:T(8,128)}, f32[5,2,240,128]{3,2,1,0:T(8,128)S(1)}, u32[]{:S(2)}, u32[]{:S(2)}) collective-permute-start(f32[5,2,240,128]{3,2,1,0:T(8,128)} %get-tuple-element.12), channel_id=1, source_target_pairs={{0,4},{4,8},{8,12},{12,16},{16,20},{20,24},{24,28},{1,5},{5,9},{9,... | collective-permute-start | bytes 3686408 | tf_op jit(solution)/shard_map/ppermute | solution.py:626
  9.4 1.3 %collective-permute-start.4 = (f32[5,2,240,128]{3,2,1,0:T(8,128)}, f32[5,2,240,128]{3,2,1,0:T(8,128)S(1)}, u32[]{:S(2)}, u32[]{:S(2)}) collective-permute-start(f32[5,2,240,128]{3,2,1,0:T(8,128)} %get-tuple-element.13), channel_id=1, source_target_pairs={{4,0},{8,4},{12,8},{16,12},{20,16},{24,20},{28,24},{5,1},{9,5},{13... | collective-permute-start | bytes 3686408 | tf_op jit(solution)/shard_map/ppermute | solution.py:627
  10.7 0.9 %constant_dynamic-slice_fusion = f32[272,128]{1,0:T(8,128)S(1)} fusion(f32[1040,128]{1,0:T(8,128)} %constant.16.clone, s32[]{:T(128)S(6)} %select_n.3), kind=kLoop, calls=%fused_computation.3 | loop fusion | bytes 278532 | tf_op jit(solution)/shard_map/dynamic_slice | solution.py:620
  11.6 0.0 copy-done.5
  12.3 0.0 collective-permute-done._.refs_4_
  12.3 0.0 copy-done.2
  12.3 0.0 copy-start
  12.3 2.5 %copy-done = f32[5,8,256,128]{3,2,1,0:T(8,128)S(1)} copy-done((f32[5,8,256,128]{3,2,1,0:T(8,128)S(1)}, f32[5,8,256,128]{3,2,1,0:T(8,128)}, u32[]{:S(2)}) %copy-start) | copy-done | bytes 5242904
  14.8 4.3 %panel_sums.1.refs_4_ = f32[32,16,128]{2,1,0:T(8,128)S(1)} custom-call(s32[512]{0:T(512)S(1)} %copy-done.4, s32[1]{0:T(128)S(6)} %copy.11.count_ref, s32[1,512]{1,0:T(1,128)S(1)} %bitcast.11, f32[5,2048,128]{2,1,0:T(8,128)S(1)} %bitcast.7, s32[64,512]{1,0:T(8,128)S(1)} %bitcast.9, f32[64,512]{1,0:T(8,128)S(1)} %bitcast.10, ...), custom_call_target="tpu_custom_call" | custom-call | flops 268435456 | bytes 5242880 | tf_op jit(solution)/shard_map/panel_sums/pallas_call | solution.py:356
  19.1 4.2 %inner_terms.1 = (f32[5,96,128]{2,1,0:T(8,128)S(1)}, f32[5,16,128]{2,1,0:T(8,128)S(1)}) custom-call(s32[1]{0:T(128)} %bitcast.az_ref.refs_0_, f32[5,8,256,128]{3,2,1,0:T(8,128)S(1)} %copy-done.1, f32[5,8,256,128]{3,2,1,0:T(8,128)S(1)} %copy-done.1, f32[280,128]{1,0:T(8,128)S(1)} %pad_maximum_fusion.1.refs_3_.refs_6_.basis_ref, ...), custom_call_target="tpu_custom_call" | custom-call | flops 251658240 | bytes 5242880 | tf_op jit(solution)/shard_map/inner_terms/pallas_call | solution.py:259
  23.3 1.0 %collective-permute-start.1 = (f32[5,96,128]{2,1,0:T(8,128)S(1)}, f32[5,96,128]{2,1,0:T(8,128)S(1)}, u32[]{:S(2)}, u32[]{:S(2)}) collective-permute-start(f32[5,96,128]{2,1,0:T(8,128)S(1)} %get-tuple-element.10), channel_id=1, source_target_pairs={{0,1},{1,0},{2,3},{3,2},{4,5},{5,4},{6,7},{7,6},{8,9},{9,8},{10,11... | collective-permute-start | bytes 737288 | tf_op jit(solution)/shard_map/ppermute | solution.py:634
  24.3 1.1 %collective-permute-done.1 = f32[5,96,128]{2,1,0:T(8,128)S(1)} collective-permute-done((f32[5,96,128]{2,1,0:T(8,128)S(1)}, f32[5,96,128]{2,1,0:T(8,128)S(1)}, u32[]{:S(2)}, u32[]{:S(2)}) %collective-permute-start.1) | collective-permute-done | bytes 245792 | tf_op jit(solution)/shard_map/ppermute | solution.py:634
  25.5 0.1 collective-permute-start.2
  25.6 12.0 %all_to_all.10 = f32[4,8,16,128]{3,2,1,0:T(8,128)} all-to-all(f32[4,8,16,128]{3,2,1,0:T(8,128)S(1)} %bitcast.8), channel_id=1, replica_groups=mesh['ax'=8,'az'=4] {'az'}, dimensions={0} | all-to-all | bytes 524288 | tf_op jit(solution)/shard_map/all_to_all | solution.py:606
  37.7 1.6 %reduce_sum.9 = f32[8,16,128]{2,1,0:T(8,128)} reduce(f32[4,8,16,128]{3,2,1,0:T(8,128)} %all_to_all.10, f32[]{:T(128)} %constant.6.clone.1), dimensions={0}, to_apply=%region_0.0 | reduce | flops 49152 | bytes 327684 | tf_op jit(solution)/shard_map/reduce_sum | solution.py:606
  39.3 6.4 %all-to-all-start.1 = ((f32[8,16,128]{2,1,0:T(8,128)}), f32[8,16,128]{2,1,0:T(8,128)S(1)}, u32[]{:S(2)}, u32[]{:S(2)}) async-start(f32[8,16,128]{2,1,0:T(8,128)} %reduce_sum.9), calls=%async_computation.1 | async-start | bytes 131072 | tf_op jit(solution)/shard_map/all_to_all | solution.py:607
  45.7 0.0 collective-permute-done.2.refs_3_.refs_5_
  45.7 1.3 %collective-permute-start.6 = (f32[5,16,128]{2,1,0:T(8,128)S(1)}, f32[5,16,128]{2,1,0:T(8,128)S(1)}, u32[]{:S(2)}, u32[]{:S(2)}) collective-permute-start(f32[5,16,128]{2,1,0:T(8,128)S(1)} %get-tuple-element.16), channel_id=1, source_target_pairs={{4,0},{8,4},{12,8},{16,12},{20,16},{24,20},{28,24},{5,1},{9,5},{13... | collective-permute-start | bytes 122888 | tf_op jit(solution)/shard_map/ppermute | solution.py:645
  47.0 4.5 %collective-permute-start.5 = (f32[5,16,128]{2,1,0:T(8,128)S(1)}, f32[5,16,128]{2,1,0:T(8,128)S(1)}, u32[]{:S(2)}, u32[]{:S(2)}) collective-permute-start(f32[5,16,128]{2,1,0:T(8,128)S(1)} %get-tuple-element.17), channel_id=1, source_target_pairs={{0,4},{4,8},{8,12},{12,16},{16,20},{20,24},{24,28},{1,5},{5,9},{9,... | collective-permute-start | bytes 122888 | tf_op jit(solution)/shard_map/ppermute | solution.py:644
  51.6 14.1 %local_section.1.part_ref = f32[5,8,256,128]{3,2,1,0:T(8,128)} custom-call(s32[1]{0:T(128)} %bitcast.az_ref.refs_0_, f32[5,8,256,128]{3,2,1,0:T(8,128)} %refs_1_.3, f32[5,112,128]{2,1,0:T(8,128)S(1)} %pad_maximum_fusion.refs_2_, f32[5,112,128]{2,1,0:T(8,128)S(1)} %collective-permute-done.2.refs_3_.refs_5_, f32[5,16,128]{2,1,0:T(8,128)S(1)} %collective-permute-done._.refs_4_, ...), custom_call_target="tpu_custom_call" | custom-call | flops 157286400 | bytes 52428800 | tf_op jit(solution)/shard_map/local_section/pallas_call | solution.py:481
  65.6 0.0 all-to-all-done.1.sums_ref
  65.7 0.0 collective-permute-done.6.spec_high
  65.7 0.0 collective-permute-done.5.spec_low
  65.7 0.0 collective-permute-done.3.low_ref
  65.7 0.0 collective-permute-done.4.high_ref
  65.7 5.1 %add_edges.1 = (f32[5,8,256,128]{3,2,1,0:T(8,128)}, f32[32,64]{1,0:T(8,128)}) custom-call(f32[5,8,256,128]{3,2,1,0:T(8,128)} %local_section.1.part_ref, f32[5,2,240,128]{3,2,1,0:T(8,128)S(1)} %collective-permute-done.3.low_ref, f32[5,2,240,128]{3,2,1,0:T(8,128)S(1)} %collective-permute-done.4.high_ref, ...), custom_call_target="tpu_custom_call", output_to_operand_aliasing={{0}: (0, {})} | custom-call | flops 1310720 | bytes 7864320 | tf_op jit(solution)/shard_map/add_edges/pallas_call | solution.py:568
  (9 shorter events, 0.1 us)
Async XLA Ops:
  0.6 11.0 %copy-start.5 = (f32[8,128]{1,0:T(8,128)S(1)}, f32[8,128]{1,0:T(8,128)}, u32[]{:S(2)}) copy-start(f32[8,128]{1,0:T(8,128)} %constant.17.clone) | copy-start | bytes 12292
  0.6 11.6 %copy-start.2 = (s32[512,64]{0,1:T(8,128)S(1)}, s32[512,64]{0,1:T(8,128)}, u32[]{:S(2)}) copy-start(s32[512,64]{0,1:T(8,128)} %param.10) | copy-start | bytes 393220
  0.7 11.6 %copy-start.3 = (f32[512,64]{0,1:T(8,128)S(1)}, f32[512,64]{0,1:T(8,128)}, u32[]{:S(2)}) copy-start(f32[512,64]{0,1:T(8,128)} %param.11) | copy-start | bytes 393220
  0.7 11.6 %copy-start.4 = (s32[512]{0:T(512)S(1)}, s32[512]{0:T(512)}, u32[]{:S(2)}) copy-start(s32[512]{0:T(512)} %cells_ref.1) | copy-start | bytes 6148
  4.4 7.8 %collective-permute-start = (f32[5,16,128]{2,1,0:T(8,128)S(1)}, f32[5,16,128]{2,1,0:T(8,128)S(1)}, u32[]{:S(2)}, u32[]{:S(2)}) collective-permute-start(f32[5,16,128]{2,1,0:T(8,128)S(1)} %get-tuple-element.9), channel_id=1, source_target_pairs={{0,1},{1,0},{2,3},{3,2},{4,5},{5,4},{6,7},{7,6},{8,9},{9,8},{10,11... | collective-permute-start | bytes 122888 | tf_op jit(solution)/shard_map/ppermute | solution.py:625
  4.9 60.8 %collective-permute-start.3 = (f32[5,2,240,128]{3,2,1,0:T(8,128)}, f32[5,2,240,128]{3,2,1,0:T(8,128)S(1)}, u32[]{:S(2)}, u32[]{:S(2)}) collective-permute-start(f32[5,2,240,128]{3,2,1,0:T(8,128)} %get-tuple-element.12), channel_id=1, source_target_pairs={{0,4},{4,8},{8,12},{12,16},{16,20},{20,24},{24,28},{1,5},{5,9},{9,... | collective-permute-start | bytes 3686408 | tf_op jit(solution)/shard_map/ppermute | solution.py:626
  9.4 56.3 %collective-permute-start.4 = (f32[5,2,240,128]{3,2,1,0:T(8,128)}, f32[5,2,240,128]{3,2,1,0:T(8,128)S(1)}, u32[]{:S(2)}, u32[]{:S(2)}) collective-permute-start(f32[5,2,240,128]{3,2,1,0:T(8,128)} %get-tuple-element.13), channel_id=1, source_target_pairs={{4,0},{8,4},{12,8},{16,12},{20,16},{24,20},{28,24},{5,1},{9,5},{13... | collective-permute-start | bytes 3686408 | tf_op jit(solution)/shard_map/ppermute | solution.py:627
  12.3 2.5 %copy-start = (f32[5,8,256,128]{3,2,1,0:T(8,128)S(1)}, f32[5,8,256,128]{3,2,1,0:T(8,128)}, u32[]{:S(2)}) copy-start(f32[5,8,256,128]{3,2,1,0:T(8,128)} %refs_1_.3) | copy-start | bytes 15728644
  14.8 4.3 %copy-start.1 = (f32[5,8,256,128]{3,2,1,0:T(8,128)S(1)}, f32[5,8,256,128]{3,2,1,0:T(8,128)}, u32[]{:S(2)}) copy-start(f32[5,8,256,128]{3,2,1,0:T(8,128)} %refs_1_.3) | copy-start | bytes 15728644
  23.3 2.1 %collective-permute-start.1 = (f32[5,96,128]{2,1,0:T(8,128)S(1)}, f32[5,96,128]{2,1,0:T(8,128)S(1)}, u32[]{:S(2)}, u32[]{:S(2)}) collective-permute-start(f32[5,96,128]{2,1,0:T(8,128)S(1)} %get-tuple-element.10), channel_id=1, source_target_pairs={{0,1},{1,0},{2,3},{3,2},{4,5},{5,4},{6,7},{7,6},{8,9},{9,8},{10,11... | collective-permute-start | bytes 737288 | tf_op jit(solution)/shard_map/ppermute | solution.py:634
  25.5 20.1 %collective-permute-start.2 = (f32[5,112,128]{2,1,0:T(8,128)S(1)}, f32[5,112,128]{2,1,0:T(8,128)S(1)}, u32[]{:S(2)}, u32[]{:S(2)}) collective-permute-start(f32[5,112,128]{2,1,0:T(8,128)S(1)} %pad_maximum_fusion.refs_2_), channel_id=1, source_target_pairs={{1,2},{3,0},{2,1},{0,3},{5,6},{7,4},{6,5},{4,7},{9,10},{11,8},{10,... | collective-permute-start | bytes 860168 | tf_op jit(solution)/shard_map/ppermute | solution.py:636
  39.3 26.4 %all-to-all-start.1 = ((f32[8,16,128]{2,1,0:T(8,128)}), f32[8,16,128]{2,1,0:T(8,128)S(1)}, u32[]{:S(2)}, u32[]{:S(2)}) async-start(f32[8,16,128]{2,1,0:T(8,128)} %reduce_sum.9), calls=%async_computation.1 | async-start | bytes 131072 | tf_op jit(solution)/shard_map/all_to_all | solution.py:607
  45.7 19.9 %collective-permute-start.6 = (f32[5,16,128]{2,1,0:T(8,128)S(1)}, f32[5,16,128]{2,1,0:T(8,128)S(1)}, u32[]{:S(2)}, u32[]{:S(2)}) collective-permute-start(f32[5,16,128]{2,1,0:T(8,128)S(1)} %get-tuple-element.16), channel_id=1, source_target_pairs={{4,0},{8,4},{12,8},{16,12},{20,16},{24,20},{28,24},{5,1},{9,5},{13... | collective-permute-start | bytes 122888 | tf_op jit(solution)/shard_map/ppermute | solution.py:645
  47.0 18.6 %collective-permute-start.5 = (f32[5,16,128]{2,1,0:T(8,128)S(1)}, f32[5,16,128]{2,1,0:T(8,128)S(1)}, u32[]{:S(2)}, u32[]{:S(2)}) collective-permute-start(f32[5,16,128]{2,1,0:T(8,128)S(1)} %get-tuple-element.17), channel_id=1, source_target_pairs={{0,4},{4,8},{8,12},{12,16},{16,20},{20,24},{24,28},{1,5},{5,9},{9,... | collective-permute-start | bytes 122888 | tf_op jit(solution)/shard_map/ppermute | solution.py:644

commit v4 on v3

--- a/solution.py
+++ b/solution.py
@@ -626,11 +626,11 @@
     low = lax.ppermute(send_up, "ax", up)
     high = lax.ppermute(send_down, "ax", down)
 
-    partial = panel_sums(conserved, panel_cells, panel_counts, time_bins, amplitudes, early)
+    message, later = inner_terms(conserved, az, basis, length, early)
+    edge = (planes + 4) * CYCLES
+    partial = panel_sums(conserved, panel_cells, panel_counts, time_bins, amplitudes, message)
     sums = exchanged_sums(partial, observers)
 
-    message, later = inner_terms(conserved, az, basis, length, partial)
-    edge = (planes + 4) * CYCLES
     mine = jnp.concatenate([message + lax.ppermute(message, "az", pair), later], axis=1)
     pairs = [(i, (i + 1) % n_az) for i in range(1, n_az, 2)]
     theirs = lax.ppermute(mine, "az", pairs + [(j, i) for i, j in pairs])

time: 71.9 us -> 71.5 us (level)
  waiting for transfers between devices: 1.16 us -> 3.24 us
  Pallas kernels: 31.5 us -> 29.5 us
  blocking collectives: 12 us -> 10.4 us
  starting transfers between devices: 19.5 us -> 20.5 us
    pallas_call x1, Pallas kernels: 4.28 us -> 2.44 us  [panel_sums(): pl.pallas_call(functools.partial(panel_kernel, lax.axis_size('ax'), lax.a...]
    all_to_all x1, blocking collectives: 12 us -> 10.4 us  [exchanged_sums(): lax.all_to_all(blocks, 'az', split_axis=0, concat_axis=0, tiled=True)]
    all_to_all x1, waiting for transfers between devices: 0.01 us -> 1.45 us  [exchanged_sums(): return lax.all_to_all(blocks, 'ax', split_axis=0, concat_axis=0, tiled=True)]
    ppermute x1, starting transfers between devices: 0.07 us -> 1.42 us  [on_device(): theirs = lax.ppermute(mine, 'az', pairs + [(j, i) for i, j in pairs])]
  transfers between devices with their start and end apart: 8 -> 8, of which waited for: 1 -> 3; matrix products, arithmetic and copies ran while one was open for 4% -> 4% of each run, Pallas kernels for 32% -> 30%
where the time goes in v4:
time: 71.5 us; the launch traced here: 70.2 us
  Pallas kernels  29.5 us (41%)
  starting transfers between devices  20.5 us (29%)
  blocking collectives  10.4 us (15%)
  local copies, waits for them, and re-layouts  3.44 us (5%)
  waiting for transfers between devices  3.24 us (5%)
  other arithmetic  1.68 us (2%)
  between operations  1.47 us (2%)
    pallas_call x1, Pallas kernels, local_section(): pl.pallas_call(functools.partial(section_kernel, 2.0 * math.pi / length),...  14.1 us
    all_to_all x1, blocking collectives, exchanged_sums(): lax.all_to_all(blocks, 'az', split_axis=0, concat_axis=0, tiled=True)  10.4 us
    all_to_all x1, starting transfers between devices, exchanged_sums(): return lax.all_to_all(blocks, 'ax', split_axis=0, concat_axis=0, tiled=True)  6.73 us
    pallas_call x1, Pallas kernels, add_edges(): pl.pallas_call(add_kernel, grid_spec=pltpu.PrefetchScalarGridSpec(num_sca...  5.12 us
    ppermute x1, starting transfers between devices, on_device(): spec_low = lax.ppermute(outside[:, :2 * CYCLES], 'ax', up)  4.55 us
    ppermute x1, starting transfers between devices, on_device(): low = lax.ppermute(send_up, 'ax', up)  4.46 us
    pallas_call x1, Pallas kernels, inner_terms(): pl.pallas_call(functools.partial(inner_kernel, 2.0 * math.pi / length), g...  4.22 us
    pallas_call x1, Pallas kernels, edge_terms(): pl.pallas_call(edge_kernel, grid_spec=pltpu.PrefetchScalarGridSpec(num_sc...  3.67 us
  transfers between devices with their start and end apart: 8, of which 3 were waited for; matrix products, arithmetic and copies ran while one was open for 4% of the time, Pallas kernels for 30%

profile of v4, /device:TPU:0, one launch (start us, length us, event | category | flops | bytes accessed | tf_op | source)
XLA Modules:
  0.0 70.2 jit_solution(1658424397750858856)
XLA Ops:
  0.6 0.0 copy-start.5
  0.6 3.7 %edge_terms.1 = (f32[5,2,240,128]{3,2,1,0:T(8,128)}, f32[5,2,240,128]{3,2,1,0:T(8,128)}, f32[5,16,128]{2,1,0:T(8,128)S(1)}) custom-call(s32[1]{0:T(128)} %bitcast.az_ref.refs_0_, f32[5,8,256,128]{3,2,1,0:T(8,128)} %refs_1_.3, f32[5,8,256,128]{3,2,1,0:T(8,128)} %refs_1_.3), custom_call_target="tpu_custom_call" | custom-call | flops 13107200 | bytes 5242880 | tf_op jit(solution)/shard_map/edge_terms/pallas_call | solution.py:123
  4.3 0.5 collective-permute-start
  4.8 4.5 %collective-permute-start.3 = (f32[5,2,240,128]{3,2,1,0:T(8,128)}, f32[5,2,240,128]{3,2,1,0:T(8,128)S(1)}, u32[]{:S(2)}, u32[]{:S(2)}) collective-permute-start(f32[5,2,240,128]{3,2,1,0:T(8,128)} %get-tuple-element.12), channel_id=1, source_target_pairs={{0,4},{4,8},{8,12},{12,16},{16,20},{20,24},{24,28},{1,5},{5,9},{9,... | collective-permute-start | bytes 3686408 | tf_op jit(solution)/shard_map/ppermute | solution.py:626
  9.2 1.3 %collective-permute-start.4 = (f32[5,2,240,128]{3,2,1,0:T(8,128)}, f32[5,2,240,128]{3,2,1,0:T(8,128)S(1)}, u32[]{:S(2)}, u32[]{:S(2)}) collective-permute-start(f32[5,2,240,128]{3,2,1,0:T(8,128)} %get-tuple-element.13), channel_id=1, source_target_pairs={{4,0},{8,4},{12,8},{16,12},{20,16},{24,20},{28,24},{5,1},{9,5},{13... | collective-permute-start | bytes 3686408 | tf_op jit(solution)/shard_map/ppermute | solution.py:627
  10.5 0.9 %constant_dynamic-slice_fusion = f32[272,128]{1,0:T(8,128)S(1)} fusion(f32[1040,128]{1,0:T(8,128)} %constant.16.clone, s32[]{:T(128)S(6)} %select_n.3), kind=kLoop, calls=%fused_computation.3 | loop fusion | bytes 278532 | tf_op jit(solution)/shard_map/dynamic_slice | solution.py:620
  11.5 0.0 copy-done.5
  11.5 0.0 collective-permute-done.refs_4_
  11.5 0.0 copy-start
  11.5 2.5 %copy-done = f32[5,8,256,128]{3,2,1,0:T(8,128)S(1)} copy-done((f32[5,8,256,128]{3,2,1,0:T(8,128)S(1)}, f32[5,8,256,128]{3,2,1,0:T(8,128)}, u32[]{:S(2)}) %copy-start) | copy-done | bytes 5242904
  14.0 4.2 %inner_terms.1 = (f32[5,96,128]{2,1,0:T(8,128)S(1)}, f32[5,16,128]{2,1,0:T(8,128)S(1)}) custom-call(s32[1]{0:T(128)} %bitcast.az_ref.refs_0_, f32[5,8,256,128]{3,2,1,0:T(8,128)S(1)} %copy-done, f32[5,8,256,128]{3,2,1,0:T(8,128)S(1)} %copy-done, f32[280,128]{1,0:T(8,128)S(1)} %pad_maximum_fusion.1.refs_3_.refs_6_.basis_ref, ...), custom_call_target="tpu_custom_call" | custom-call | flops 251658240 | bytes 5242880 | tf_op jit(solution)/shard_map/inner_terms/pallas_call | solution.py:259
  18.2 0.0 copy-start.2
  18.2 0.0 copy-start.3
  18.2 0.0 copy-start.4
  18.3 0.3 collective-permute-start.1
  18.6 1.3 %collective-permute-done.1 = f32[5,96,128]{2,1,0:T(8,128)S(1)} collective-permute-done((f32[5,96,128]{2,1,0:T(8,128)S(1)}, f32[5,96,128]{2,1,0:T(8,128)S(1)}, u32[]{:S(2)}, u32[]{:S(2)}) %collective-permute-start.1) | collective-permute-done | bytes 245792 | tf_op jit(solution)/shard_map/ppermute | solution.py:634
  19.9 1.4 %collective-permute-start.2 = (f32[5,112,128]{2,1,0:T(8,128)S(1)}, f32[5,112,128]{2,1,0:T(8,128)S(1)}, u32[]{:S(2)}, u32[]{:S(2)}) collective-permute-start(f32[5,112,128]{2,1,0:T(8,128)S(1)} %pad_maximum_fusion.refs_2_), channel_id=1, source_target_pairs={{1,2},{3,0},{2,1},{0,3},{5,6},{7,4},{6,5},{4,7},{9,10},{11,8},{10,... | collective-permute-start | bytes 860168 | tf_op jit(solution)/shard_map/ppermute | solution.py:636
  22.0 0.0 copy-done.1
  22.0 2.4 %panel_sums.1 = f32[32,16,128]{2,1,0:T(8,128)S(1)} custom-call(s32[512]{0:T(512)S(1)} %copy-done.4, s32[1]{0:T(128)S(6)} %copy.11.count_ref, s32[1,512]{1,0:T(1,128)S(1)} %bitcast.11, f32[5,2048,128]{2,1,0:T(8,128)S(1)} %bitcast.7, s32[64,512]{1,0:T(8,128)S(1)} %bitcast.9, f32[64,512]{1,0:T(8,128)S(1)} %bitcast.10, f32[5,96,128]{2,1,0:T(8,128)S(1)} %get-tuple-element.10._), custom_call_target="tpu_custom_call" | custom-call | flops 268435456 | bytes 5242880 | tf_op jit(solution)/shard_map/panel_sums/pallas_call | solution.py:356
  24.5 10.4 %all_to_all.10 = f32[4,8,16,128]{3,2,1,0:T(8,128)} all-to-all(f32[4,8,16,128]{3,2,1,0:T(8,128)S(1)} %bitcast.8), channel_id=1, replica_groups=mesh['ax'=8,'az'=4] {'az'}, dimensions={0} | all-to-all | bytes 524288 | tf_op jit(solution)/shard_map/all_to_all | solution.py:606
  34.8 1.6 %reduce_sum.9 = f32[8,16,128]{2,1,0:T(8,128)} reduce(f32[4,8,16,128]{3,2,1,0:T(8,128)} %all_to_all.10, f32[]{:T(128)} %constant.6.clone.1), dimensions={0}, to_apply=%region_0.0 | reduce | flops 49152 | bytes 327684 | tf_op jit(solution)/shard_map/reduce_sum | solution.py:606
  36.4 6.7 %all-to-all-start.1 = ((f32[8,16,128]{2,1,0:T(8,128)}), f32[8,16,128]{2,1,0:T(8,128)S(1)}, u32[]{:S(2)}, u32[]{:S(2)}) async-start(f32[8,16,128]{2,1,0:T(8,128)} %reduce_sum.9), calls=%async_computation.1 | async-start | bytes 131072 | tf_op jit(solution)/shard_map/all_to_all | solution.py:607
  43.2 0.0 collective-permute-done.2.refs_3_.refs_5_
  43.2 1.3 %collective-permute-start.6 = (f32[5,16,128]{2,1,0:T(8,128)S(1)}, f32[5,16,128]{2,1,0:T(8,128)S(1)}, u32[]{:S(2)}, u32[]{:S(2)}) collective-permute-start(f32[5,16,128]{2,1,0:T(8,128)S(1)} %get-tuple-element.16), channel_id=1, source_target_pairs={{4,0},{8,4},{12,8},{16,12},{20,16},{24,20},{28,24},{5,1},{9,5},{13... | collective-permute-start | bytes 122888 | tf_op jit(solution)/shard_map/ppermute | solution.py:645
  44.5 4.5 %collective-permute-start.5 = (f32[5,16,128]{2,1,0:T(8,128)S(1)}, f32[5,16,128]{2,1,0:T(8,128)S(1)}, u32[]{:S(2)}, u32[]{:S(2)}) collective-permute-start(f32[5,16,128]{2,1,0:T(8,128)S(1)} %get-tuple-element.17), channel_id=1, source_target_pairs={{0,4},{4,8},{8,12},{12,16},{16,20},{20,24},{24,28},{1,5},{5,9},{9,... | collective-permute-start | bytes 122888 | tf_op jit(solution)/shard_map/ppermute | solution.py:644
  49.1 14.1 %local_section.1.part_ref = f32[5,8,256,128]{3,2,1,0:T(8,128)} custom-call(s32[1]{0:T(128)} %bitcast.az_ref.refs_0_, f32[5,8,256,128]{3,2,1,0:T(8,128)} %refs_1_.3, f32[5,112,128]{2,1,0:T(8,128)S(1)} %pad_maximum_fusion.refs_2_, f32[5,112,128]{2,1,0:T(8,128)S(1)} %collective-permute-done.2.refs_3_.refs_5_, f32[5,16,128]{2,1,0:T(8,128)S(1)} %collective-permute-done.refs_4_, ...), custom_call_target="tpu_custom_call" | custom-call | flops 157286400 | bytes 52428800 | tf_op jit(solution)/shard_map/local_section/pallas_call | solution.py:481
  63.1 1.5 %all-to-all-done.1.sums_ref = f32[8,16,128]{2,1,0:T(8,128)S(1)} async-done(((f32[8,16,128]{2,1,0:T(8,128)}), f32[8,16,128]{2,1,0:T(8,128)S(1)}, u32[]{:S(2)}, u32[]{:S(2)}) %all-to-all-start.1) | async-done | bytes 65568 | tf_op jit(solution)/shard_map/all_to_all | solution.py:607
  64.6 0.0 collective-permute-done.6.spec_high
  64.6 0.5 collective-permute-done.5.spec_low
  65.1 0.0 collective-permute-done.3.low_ref
  65.1 0.0 collective-permute-done.4.high_ref
  65.1 5.1 %add_edges.1 = (f32[5,8,256,128]{3,2,1,0:T(8,128)}, f32[32,64]{1,0:T(8,128)}) custom-call(f32[5,8,256,128]{3,2,1,0:T(8,128)} %local_section.1.part_ref, f32[5,2,240,128]{3,2,1,0:T(8,128)S(1)} %collective-permute-done.3.low_ref, f32[5,2,240,128]{3,2,1,0:T(8,128)S(1)} %collective-permute-done.4.high_ref, ...), custom_call_target="tpu_custom_call", output_to_operand_aliasing={{0}: (0, {})} | custom-call | flops 1310720 | bytes 7864320 | tf_op jit(solution)/shard_map/add_edges/pallas_call | solution.py:568
  (9 shorter events, 0.1 us)
Async XLA Ops:
  0.6 10.8 %copy-start.5 = (f32[8,128]{1,0:T(8,128)S(1)}, f32[8,128]{1,0:T(8,128)}, u32[]{:S(2)}) copy-start(f32[8,128]{1,0:T(8,128)} %constant.17.clone) | copy-start | bytes 12292
  4.3 7.2 %collective-permute-start = (f32[5,16,128]{2,1,0:T(8,128)S(1)}, f32[5,16,128]{2,1,0:T(8,128)S(1)}, u32[]{:S(2)}, u32[]{:S(2)}) collective-permute-start(f32[5,16,128]{2,1,0:T(8,128)S(1)} %get-tuple-element.9), channel_id=1, source_target_pairs={{0,1},{1,0},{2,3},{3,2},{4,5},{5,4},{6,7},{7,6},{8,9},{9,8},{10,11... | collective-permute-start | bytes 122888 | tf_op jit(solution)/shard_map/ppermute | solution.py:625
  4.8 60.3 %collective-permute-start.3 = (f32[5,2,240,128]{3,2,1,0:T(8,128)}, f32[5,2,240,128]{3,2,1,0:T(8,128)S(1)}, u32[]{:S(2)}, u32[]{:S(2)}) collective-permute-start(f32[5,2,240,128]{3,2,1,0:T(8,128)} %get-tuple-element.12), channel_id=1, source_target_pairs={{0,4},{4,8},{8,12},{12,16},{16,20},{20,24},{24,28},{1,5},{5,9},{9,... | collective-permute-start | bytes 3686408 | tf_op jit(solution)/shard_map/ppermute | solution.py:626
  9.2 55.9 %collective-permute-start.4 = (f32[5,2,240,128]{3,2,1,0:T(8,128)}, f32[5,2,240,128]{3,2,1,0:T(8,128)S(1)}, u32[]{:S(2)}, u32[]{:S(2)}) collective-permute-start(f32[5,2,240,128]{3,2,1,0:T(8,128)} %get-tuple-element.13), channel_id=1, source_target_pairs={{4,0},{8,4},{12,8},{16,12},{20,16},{24,20},{28,24},{5,1},{9,5},{13... | collective-permute-start | bytes 3686408 | tf_op jit(solution)/shard_map/ppermute | solution.py:627
  11.5 2.5 %copy-start = (f32[5,8,256,128]{3,2,1,0:T(8,128)S(1)}, f32[5,8,256,128]{3,2,1,0:T(8,128)}, u32[]{:S(2)}) copy-start(f32[5,8,256,128]{3,2,1,0:T(8,128)} %refs_1_.3) | copy-start | bytes 15728644
  14.0 8.0 %copy-start.1 = (f32[5,8,256,128]{3,2,1,0:T(8,128)S(1)}, f32[5,8,256,128]{3,2,1,0:T(8,128)}, u32[]{:S(2)}) copy-start(f32[5,8,256,128]{3,2,1,0:T(8,128)} %refs_1_.3) | copy-start | bytes 15728644
  18.2 3.8 %copy-start.2 = (s32[512,64]{0,1:T(8,128)S(1)}, s32[512,64]{0,1:T(8,128)}, u32[]{:S(2)}) copy-start(s32[512,64]{0,1:T(8,128)} %param.10) | copy-start | bytes 393220
  18.2 3.8 %copy-start.3 = (f32[512,64]{0,1:T(8,128)S(1)}, f32[512,64]{0,1:T(8,128)}, u32[]{:S(2)}) copy-start(f32[512,64]{0,1:T(8,128)} %param.11) | copy-start | bytes 393220
  18.2 3.8 %copy-start.4 = (s32[512]{0:T(512)S(1)}, s32[512]{0:T(512)}, u32[]{:S(2)}) copy-start(s32[512]{0:T(512)} %cells_ref.1) | copy-start | bytes 6148
  18.3 1.6 %collective-permute-start.1 = (f32[5,96,128]{2,1,0:T(8,128)S(1)}, f32[5,96,128]{2,1,0:T(8,128)S(1)}, u32[]{:S(2)}, u32[]{:S(2)}) collective-permute-start(f32[5,96,128]{2,1,0:T(8,128)S(1)} %get-tuple-element.10._), channel_id=1, source_target_pairs={{0,1},{1,0},{2,3},{3,2},{4,5},{5,4},{6,7},{7,6},{8,9},{9,8},{10,11... | collective-permute-start | bytes 737288 | tf_op jit(solution)/shard_map/ppermute | solution.py:634
  19.9 23.3 %collective-permute-start.2 = (f32[5,112,128]{2,1,0:T(8,128)S(1)}, f32[5,112,128]{2,1,0:T(8,128)S(1)}, u32[]{:S(2)}, u32[]{:S(2)}) collective-permute-start(f32[5,112,128]{2,1,0:T(8,128)S(1)} %pad_maximum_fusion.refs_2_), channel_id=1, source_target_pairs={{1,2},{3,0},{2,1},{0,3},{5,6},{7,4},{6,5},{4,7},{9,10},{11,8},{10,... | collective-permute-start | bytes 860168 | tf_op jit(solution)/shard_map/ppermute | solution.py:636
  36.4 28.2 %all-to-all-start.1 = ((f32[8,16,128]{2,1,0:T(8,128)}), f32[8,16,128]{2,1,0:T(8,128)S(1)}, u32[]{:S(2)}, u32[]{:S(2)}) async-start(f32[8,16,128]{2,1,0:T(8,128)} %reduce_sum.9), calls=%async_computation.1 | async-start | bytes 131072 | tf_op jit(solution)/shard_map/all_to_all | solution.py:607
  43.2 21.4 %collective-permute-start.6 = (f32[5,16,128]{2,1,0:T(8,128)S(1)}, f32[5,16,128]{2,1,0:T(8,128)S(1)}, u32[]{:S(2)}, u32[]{:S(2)}) collective-permute-start(f32[5,16,128]{2,1,0:T(8,128)S(1)} %get-tuple-element.16), channel_id=1, source_target_pairs={{4,0},{8,4},{12,8},{16,12},{20,16},{24,20},{28,24},{5,1},{9,5},{13... | collective-permute-start | bytes 122888 | tf_op jit(solution)/shard_map/ppermute | solution.py:645
  44.5 20.6 %collective-permute-start.5 = (f32[5,16,128]{2,1,0:T(8,128)S(1)}, f32[5,16,128]{2,1,0:T(8,128)S(1)}, u32[]{:S(2)}, u32[]{:S(2)}) collective-permute-start(f32[5,16,128]{2,1,0:T(8,128)S(1)} %get-tuple-element.17), channel_id=1, source_target_pairs={{0,4},{4,8},{8,12},{12,16},{16,20},{20,24},{24,28},{1,5},{5,9},{9,... | collective-permute-start | bytes 122888 | tf_op jit(solution)/shard_map/ppermute | solution.py:644

commit v5 on v4

--- a/solution.py
+++ b/solution.py
@@ -69,14 +69,14 @@
         yield k, [jnp.where(low, f[:2], f[ROWS - 2 :]) for f in flux]
 
 
-def edge_kernel(az_ref, q_ref, rim_ref, up_ref, down_ref, early_ref):
-    sector, radial = q_ref.shape[2:]
+def edge_kernel(az_ref, top_ref, bottom_ref, rim_ref, up_ref, down_ref, early_ref):
+    sector, radial = top_ref.shape[2:]
     groups = radial // CYCLES - 1
     tail = sector * CYCLES // radial
     scale = time_step / 12.0
     lane = lax.broadcasted_iota(jnp.int32, (1, radial), 1)
 
-    def go(up, send):
+    def go(up, q_ref, send):
         def terms(start):
             rows = pl.ds(start, tail)
             flux = []
@@ -104,14 +104,11 @@
                         lane < CYCLES, moved, slots[s][f]
                     )
 
-    @pl.when(pl.program_id(0) == 0)
-    def _():
-        go(True, up_ref)
-        for k, flux in swirl_rows(rim_ref, lax.rem(az_ref[0], 2) == 1):
-            for f in range(FIELDS):
-                early_ref[f, 2 * k : 2 * k + 2, :] = flux[f]
-
-    pl.when(pl.program_id(0) == 1)(lambda: go(False, down_ref))
+    go(True, top_ref, up_ref)
+    go(False, bottom_ref, down_ref)
+    for k, flux in swirl_rows(rim_ref, lax.rem(az_ref[0], 2) == 1):
+        for f in range(FIELDS):
+            early_ref[f, 2 * k : 2 * k + 2, :] = flux[f]
 
 
 def edge_terms(conserved, az):
@@ -124,11 +121,10 @@
         edge_kernel,
         grid_spec=pltpu.PrefetchScalarGridSpec(
             num_scalar_prefetch=1,
-            grid=(2,),
+            grid=(1,),
             in_specs=[
-                pl.BlockSpec(
-                    (fields, 2, sector, radial), lambda i, az: (0, (planes // 2 - 1) * (1 - i), 0, 0)
-                ),
+                pl.BlockSpec((fields, 2, sector, radial), lambda i, az: (0, planes // 2 - 1, 0, 0)),
+                pl.BlockSpec((fields, 2, sector, radial), lambda i, az: (0, 0, 0, 0)),
                 pl.BlockSpec(
                     (fields, planes, ROWS, radial),
                     lambda i, az: (0, 0, last * (1 - lax.rem(az[0], 2)), 0),
@@ -140,7 +136,7 @@
         compiler_params=params(),
         cost_estimate=cost(400 * sector * radial, 4 * 8 * fields * sector * radial),
         name="edge_terms",
-    )(az, conserved, conserved)
+    )(az, conserved, conserved, conserved)
 
 
 def inner_kernel(dtheta, *refs):
@@ -543,37 +539,36 @@
         )
         for f in range(fields):
             inner = smooth if f == 0 else pltpu.roll(smooth, radial - CYCLES * f, 1)
-            out_ref[f, 0, :main, :] = part_ref[f, 0, :main, :] + jnp.where(
-                wide, ref[f, 0], inner[:main]
+            out_ref[f, slot, :main, :] = part_ref[f, slot, :main, :] + jnp.where(
+                wide, ref[f, slot], inner[:main]
             )
             rest = inner[main:]
             for g in range(groups):
-                moved = pltpu.roll(ref[f, 0, g * tail : (g + 1) * tail, :], CYCLES * (g + 1), 1)
+                moved = pltpu.roll(ref[f, slot, g * tail : (g + 1) * tail, :], CYCLES * (g + 1), 1)
                 rest = jnp.where(lane // CYCLES == g + 1, moved, rest)
-            out_ref[f, 0, main:, :] = part_ref[f, 0, main:, :] + rest
+            out_ref[f, slot, main:, :] = part_ref[f, slot, main:, :] + rest
 
     for k in range(2):
-        pl.when(step == k)(lambda k=k: go(low_ref, spec_low, k))
-        pl.when(step == 2 + k)(lambda k=k: go(high_ref, spec_high, k))
+        pl.when(step == 0)(lambda k=k: go(low_ref, spec_low, k))
+        pl.when(step == 1)(lambda k=k: go(high_ref, spec_high, k))
 
 
 def add_edges(section, low, high, spec_low, spec_high, basis, sums, observers):
     fields, planes, sector, radial = section.shape
-    main = low.shape[2]
     bins = sums.shape[1] * sums.shape[2] // observers
     full = lambda a: pl.BlockSpec(a.shape, lambda i, *_: (0,) * a.ndim)
     plane = pl.BlockSpec(
-        (fields, 1, sector, radial), lambda i, *_: (0, jnp.where(i < 2, i, planes - 4 + i), 0, 0)
+        (fields, 2, sector, radial), lambda i, *_: (0, (planes // 2 - 1) * i, 0, 0)
     )
     return pl.pallas_call(
         add_kernel,
         grid_spec=pltpu.PrefetchScalarGridSpec(
             num_scalar_prefetch=0,
-            grid=(4,),
+            grid=(2,),
             in_specs=[
                 plane,
-                pl.BlockSpec((fields, 1, main, radial), lambda i, *_: (0, jnp.minimum(i, 1), 0, 0)),
-                pl.BlockSpec((fields, 1, main, radial), lambda i, *_: (0, jnp.maximum(i - 2, 0), 0, 0)),
+                full(low),
+                full(high),
                 full(spec_low),
                 full(spec_high),
                 full(basis),

time: 71.5 us -> 70.9 us (level)
  waiting for transfers between devices: 3.24 us -> 1.74 us
  Pallas kernels: 29.5 us -> 30.9 us
  blocking collectives: 10.4 us -> 9.1 us
  starting transfers between devices: 20.5 us -> 21.3 us
    pallas_call x1, Pallas kernels: 2.44 us -> 4.38 us  [panel_sums(): pl.pallas_call(functools.partial(panel_kernel, lax.axis_size('ax'), lax.a...]
    all_to_all x1, waiting for transfers between devices: 1.45 us -> 0.01 us  [exchanged_sums(): return lax.all_to_all(blocks, 'ax', split_axis=0, concat_axis=0, tiled=True)]
    all_to_all x1, blocking collectives: 10.4 us -> 9.1 us  [exchanged_sums(): lax.all_to_all(blocks, 'az', split_axis=0, concat_axis=0, tiled=True)]
    all_to_all x1, starting transfers between devices: 6.73 us -> 7.58 us  [exchanged_sums(): return lax.all_to_all(blocks, 'ax', split_axis=0, concat_axis=0, tiled=True)]
  transfers between devices with their start and end apart: 8 -> 8, of which waited for: 3 -> 2; matrix products, arithmetic and copies ran while one was open for 4% -> 4% of each run, Pallas kernels for 30% -> 33%
where the time goes in v5:
time: 70.9 us; the launch traced here: 69.7 us
  Pallas kernels  30.9 us (44%)
  starting transfers between devices  21.3 us (30%)
  blocking collectives  9.1 us (13%)
  local copies, waits for them, and re-layouts  3.44 us (5%)
  waiting for transfers between devices  1.74 us (2%)
  other arithmetic  1.68 us (2%)
  between operations  1.47 us (2%)
    pallas_call x1, Pallas kernels, local_section(): pl.pallas_call(functools.partial(section_kernel, 2.0 * math.pi / length),...  14.1 us
    all_to_all x1, blocking collectives, exchanged_sums(): lax.all_to_all(blocks, 'az', split_axis=0, concat_axis=0, tiled=True)  9.1 us
    all_to_all x1, starting transfers between devices, exchanged_sums(): return lax.all_to_all(blocks, 'ax', split_axis=0, concat_axis=0, tiled=True)  7.58 us
    pallas_call x1, Pallas kernels, add_edges(): pl.pallas_call(add_kernel, grid_spec=pltpu.PrefetchScalarGridSpec(num_sca...  4.59 us
    ppermute x1, starting transfers between devices, on_device(): spec_low = lax.ppermute(outside[:, :2 * CYCLES], 'ax', up)  4.55 us
    ppermute x1, starting transfers between devices, on_device(): low = lax.ppermute(send_up, 'ax', up)  4.46 us
    pallas_call x1, Pallas kernels, panel_sums(): pl.pallas_call(functools.partial(panel_kernel, lax.axis_size('ax'), lax.a...  4.38 us
    pallas_call x1, Pallas kernels, inner_terms(): pl.pallas_call(functools.partial(inner_kernel, 2.0 * math.pi / length), g...  4.22 us
  transfers between devices with their start and end apart: 8, of which 2 were waited for; matrix products, arithmetic and copies ran while one was open for 4% of the time, Pallas kernels for 33%

profile of v5, /device:TPU:0, one launch (start us, length us, event | category | flops | bytes accessed | tf_op | source)
XLA Modules:
  0.0 69.7 jit_solution(15410882195663253544)
XLA Ops:
  0.6 0.0 copy-start.5
  0.6 3.6 %edge_terms.1 = (f32[5,2,240,128]{3,2,1,0:T(8,128)}, f32[5,2,240,128]{3,2,1,0:T(8,128)}, f32[5,16,128]{2,1,0:T(8,128)S(1)}) custom-call(s32[1]{0:T(128)} %bitcast.az_ref.refs_0_, f32[5,8,256,128]{3,2,1,0:T(8,128)} %refs_1_.3, f32[5,8,256,128]{3,2,1,0:T(8,128)} %refs_1_.3, f32[5,8,256,128]{3,2,1,0:T(8,128)} %refs_1_.3), custom_call_target="tpu_custom_call" | custom-call | flops 13107200 | bytes 5242880 | tf_op jit(solution)/shard_map/edge_terms/pallas_call | solution.py:120
  4.3 0.5 collective-permute-start
  4.7 4.5 %collective-permute-start.3 = (f32[5,2,240,128]{3,2,1,0:T(8,128)}, f32[5,2,240,128]{3,2,1,0:T(8,128)S(1)}, u32[]{:S(2)}, u32[]{:S(2)}) collective-permute-start(f32[5,2,240,128]{3,2,1,0:T(8,128)} %get-tuple-element.12), channel_id=1, source_target_pairs={{0,4},{4,8},{8,12},{12,16},{16,20},{20,24},{24,28},{1,5},{5,9},{9,... | collective-permute-start | bytes 3686408 | tf_op jit(solution)/shard_map/ppermute | solution.py:621
  9.2 1.3 %collective-permute-start.4 = (f32[5,2,240,128]{3,2,1,0:T(8,128)}, f32[5,2,240,128]{3,2,1,0:T(8,128)S(1)}, u32[]{:S(2)}, u32[]{:S(2)}) collective-permute-start(f32[5,2,240,128]{3,2,1,0:T(8,128)} %get-tuple-element.13), channel_id=1, source_target_pairs={{4,0},{8,4},{12,8},{16,12},{20,16},{24,20},{28,24},{5,1},{9,5},{13... | collective-permute-start | bytes 3686408 | tf_op jit(solution)/shard_map/ppermute | solution.py:622
  10.5 0.9 %constant_dynamic-slice_fusion = f32[272,128]{1,0:T(8,128)S(1)} fusion(f32[1040,128]{1,0:T(8,128)} %constant.16.clone, s32[]{:T(128)S(6)} %select_n.3), kind=kLoop, calls=%fused_computation.3 | loop fusion | bytes 278532 | tf_op jit(solution)/shard_map/dynamic_slice | solution.py:615
  11.4 0.0 copy-done.5
  11.5 0.0 collective-permute-done.refs_4_
  11.5 0.0 copy-start
  11.5 2.5 %copy-done = f32[5,8,256,128]{3,2,1,0:T(8,128)S(1)} copy-done((f32[5,8,256,128]{3,2,1,0:T(8,128)S(1)}, f32[5,8,256,128]{3,2,1,0:T(8,128)}, u32[]{:S(2)}) %copy-start) | copy-done | bytes 5242904
  14.0 4.2 %inner_terms.1 = (f32[5,96,128]{2,1,0:T(8,128)S(1)}, f32[5,16,128]{2,1,0:T(8,128)S(1)}) custom-call(s32[1]{0:T(128)} %bitcast.az_ref.refs_0_, f32[5,8,256,128]{3,2,1,0:T(8,128)S(1)} %copy-done, f32[5,8,256,128]{3,2,1,0:T(8,128)S(1)} %copy-done, f32[280,128]{1,0:T(8,128)S(1)} %pad_maximum_fusion.1.refs_3_.refs_6_.basis_ref, ...), custom_call_target="tpu_custom_call" | custom-call | flops 251658240 | bytes 5242880 | tf_op jit(solution)/shard_map/inner_terms/pallas_call | solution.py:255
  18.2 0.0 copy-start.2
  18.2 0.0 copy-start.3
  18.2 0.0 copy-start.4
  18.2 0.3 collective-permute-start.1
  18.5 1.3 %collective-permute-done.1 = f32[5,96,128]{2,1,0:T(8,128)S(1)} collective-permute-done((f32[5,96,128]{2,1,0:T(8,128)S(1)}, f32[5,96,128]{2,1,0:T(8,128)S(1)}, u32[]{:S(2)}, u32[]{:S(2)}) %collective-permute-start.1) | collective-permute-done | bytes 245792 | tf_op jit(solution)/shard_map/ppermute | solution.py:629
  19.9 1.4 %collective-permute-start.2 = (f32[5,112,128]{2,1,0:T(8,128)S(1)}, f32[5,112,128]{2,1,0:T(8,128)S(1)}, u32[]{:S(2)}, u32[]{:S(2)}) collective-permute-start(f32[5,112,128]{2,1,0:T(8,128)S(1)} %pad_maximum_fusion.refs_2_), channel_id=1, source_target_pairs={{1,2},{3,0},{2,1},{0,3},{5,6},{7,4},{6,5},{4,7},{9,10},{11,8},{10,... | collective-permute-start | bytes 860168 | tf_op jit(solution)/shard_map/ppermute | solution.py:631
  21.9 0.0 copy-done.1
  22.0 4.4 %panel_sums.1 = f32[32,16,128]{2,1,0:T(8,128)S(1)} custom-call(s32[512]{0:T(512)S(1)} %copy-done.4, s32[1]{0:T(128)S(6)} %copy.11.count_ref, s32[1,512]{1,0:T(1,128)S(1)} %bitcast.11, f32[5,2048,128]{2,1,0:T(8,128)S(1)} %bitcast.7, s32[64,512]{1,0:T(8,128)S(1)} %bitcast.9, f32[64,512]{1,0:T(8,128)S(1)} %bitcast.10, f32[5,96,128]{2,1,0:T(8,128)S(1)} %get-tuple-element.10._), custom_call_target="tpu_custom_call" | custom-call | flops 268435456 | bytes 5242880 | tf_op jit(solution)/shard_map/panel_sums/pallas_call | solution.py:352
  26.4 9.1 %all_to_all.10 = f32[4,8,16,128]{3,2,1,0:T(8,128)} all-to-all(f32[4,8,16,128]{3,2,1,0:T(8,128)S(1)} %bitcast.8), channel_id=1, replica_groups=mesh['ax'=8,'az'=4] {'az'}, dimensions={0} | all-to-all | bytes 524288 | tf_op jit(solution)/shard_map/all_to_all | solution.py:601
  35.5 1.6 %reduce_sum.9 = f32[8,16,128]{2,1,0:T(8,128)} reduce(f32[4,8,16,128]{3,2,1,0:T(8,128)} %all_to_all.10, f32[]{:T(128)} %constant.6.clone.1), dimensions={0}, to_apply=%region_0.0 | reduce | flops 49152 | bytes 327684 | tf_op jit(solution)/shard_map/reduce_sum | solution.py:601
  37.1 7.6 %all-to-all-start.1 = ((f32[8,16,128]{2,1,0:T(8,128)}), f32[8,16,128]{2,1,0:T(8,128)S(1)}, u32[]{:S(2)}, u32[]{:S(2)}) async-start(f32[8,16,128]{2,1,0:T(8,128)} %reduce_sum.9), calls=%async_computation.1 | async-start | bytes 131072 | tf_op jit(solution)/shard_map/all_to_all | solution.py:602
  44.6 0.0 collective-permute-done.2.refs_3_.refs_5_
  44.7 1.3 %collective-permute-start.6 = (f32[5,16,128]{2,1,0:T(8,128)S(1)}, f32[5,16,128]{2,1,0:T(8,128)S(1)}, u32[]{:S(2)}, u32[]{:S(2)}) collective-permute-start(f32[5,16,128]{2,1,0:T(8,128)S(1)} %get-tuple-element.16), channel_id=1, source_target_pairs={{4,0},{8,4},{12,8},{16,12},{20,16},{24,20},{28,24},{5,1},{9,5},{13... | collective-permute-start | bytes 122888 | tf_op jit(solution)/shard_map/ppermute | solution.py:640
  46.0 4.5 %collective-permute-start.5 = (f32[5,16,128]{2,1,0:T(8,128)S(1)}, f32[5,16,128]{2,1,0:T(8,128)S(1)}, u32[]{:S(2)}, u32[]{:S(2)}) collective-permute-start(f32[5,16,128]{2,1,0:T(8,128)S(1)} %get-tuple-element.17), channel_id=1, source_target_pairs={{0,4},{4,8},{8,12},{12,16},{16,20},{20,24},{24,28},{1,5},{5,9},{9,... | collective-permute-start | bytes 122888 | tf_op jit(solution)/shard_map/ppermute | solution.py:639
  50.5 14.1 %local_section.1.part_ref = f32[5,8,256,128]{3,2,1,0:T(8,128)} custom-call(s32[1]{0:T(128)} %bitcast.az_ref.refs_0_, f32[5,8,256,128]{3,2,1,0:T(8,128)} %refs_1_.3, f32[5,112,128]{2,1,0:T(8,128)S(1)} %pad_maximum_fusion.refs_2_, f32[5,112,128]{2,1,0:T(8,128)S(1)} %collective-permute-done.2.refs_3_.refs_5_, f32[5,16,128]{2,1,0:T(8,128)S(1)} %collective-permute-done.refs_4_, ...), custom_call_target="tpu_custom_call" | custom-call | flops 157286400 | bytes 52428800 | tf_op jit(solution)/shard_map/local_section/pallas_call | solution.py:477
  64.6 0.0 all-to-all-done.1.sums_ref
  64.6 0.0 collective-permute-done.6.spec_high
  64.6 0.4 collective-permute-done.5.spec_low
  65.1 0.0 collective-permute-done.3.low_ref
  65.1 0.0 collective-permute-done.4.high_ref
  65.1 4.6 %add_edges.1 = (f32[5,8,256,128]{3,2,1,0:T(8,128)}, f32[32,64]{1,0:T(8,128)}) custom-call(f32[5,8,256,128]{3,2,1,0:T(8,128)} %local_section.1.part_ref, f32[5,2,240,128]{3,2,1,0:T(8,128)S(1)} %collective-permute-done.3.low_ref, f32[5,2,240,128]{3,2,1,0:T(8,128)S(1)} %collective-permute-done.4.high_ref, ...), custom_call_target="tpu_custom_call", output_to_operand_aliasing={{0}: (0, {})} | custom-call | flops 1310720 | bytes 7864320 | tf_op jit(solution)/shard_map/add_edges/pallas_call | solution.py:563
  (9 shorter events, 0.1 us)
Async XLA Ops:
  0.6 10.8 %copy-start.5 = (f32[8,128]{1,0:T(8,128)S(1)}, f32[8,128]{1,0:T(8,128)}, u32[]{:S(2)}) copy-start(f32[8,128]{1,0:T(8,128)} %constant.17.clone) | copy-start | bytes 12292
  4.3 7.2 %collective-permute-start = (f32[5,16,128]{2,1,0:T(8,128)S(1)}, f32[5,16,128]{2,1,0:T(8,128)S(1)}, u32[]{:S(2)}, u32[]{:S(2)}) collective-permute-start(f32[5,16,128]{2,1,0:T(8,128)S(1)} %get-tuple-element.9), channel_id=1, source_target_pairs={{0,1},{1,0},{2,3},{3,2},{4,5},{5,4},{6,7},{7,6},{8,9},{9,8},{10,11... | collective-permute-start | bytes 122888 | tf_op jit(solution)/shard_map/ppermute | solution.py:620
  4.7 60.3 %collective-permute-start.3 = (f32[5,2,240,128]{3,2,1,0:T(8,128)}, f32[5,2,240,128]{3,2,1,0:T(8,128)S(1)}, u32[]{:S(2)}, u32[]{:S(2)}) collective-permute-start(f32[5,2,240,128]{3,2,1,0:T(8,128)} %get-tuple-element.12), channel_id=1, source_target_pairs={{0,4},{4,8},{8,12},{12,16},{16,20},{20,24},{24,28},{1,5},{5,9},{9,... | collective-permute-start | bytes 3686408 | tf_op jit(solution)/shard_map/ppermute | solution.py:621
  9.2 55.9 %collective-permute-start.4 = (f32[5,2,240,128]{3,2,1,0:T(8,128)}, f32[5,2,240,128]{3,2,1,0:T(8,128)S(1)}, u32[]{:S(2)}, u32[]{:S(2)}) collective-permute-start(f32[5,2,240,128]{3,2,1,0:T(8,128)} %get-tuple-element.13), channel_id=1, source_target_pairs={{4,0},{8,4},{12,8},{16,12},{20,16},{24,20},{28,24},{5,1},{9,5},{13... | collective-permute-start | bytes 3686408 | tf_op jit(solution)/shard_map/ppermute | solution.py:622
  11.5 2.5 %copy-start = (f32[5,8,256,128]{3,2,1,0:T(8,128)S(1)}, f32[5,8,256,128]{3,2,1,0:T(8,128)}, u32[]{:S(2)}) copy-start(f32[5,8,256,128]{3,2,1,0:T(8,128)} %refs_1_.3) | copy-start | bytes 15728644
  14.0 8.0 %copy-start.1 = (f32[5,8,256,128]{3,2,1,0:T(8,128)S(1)}, f32[5,8,256,128]{3,2,1,0:T(8,128)}, u32[]{:S(2)}) copy-start(f32[5,8,256,128]{3,2,1,0:T(8,128)} %refs_1_.3) | copy-start | bytes 15728644
  18.2 3.8 %copy-start.2 = (s32[512,64]{0,1:T(8,128)S(1)}, s32[512,64]{0,1:T(8,128)}, u32[]{:S(2)}) copy-start(s32[512,64]{0,1:T(8,128)} %param.10) | copy-start | bytes 393220
  18.2 3.8 %copy-start.3 = (f32[512,64]{0,1:T(8,128)S(1)}, f32[512,64]{0,1:T(8,128)}, u32[]{:S(2)}) copy-start(f32[512,64]{0,1:T(8,128)} %param.11) | copy-start | bytes 393220
  18.2 3.7 %copy-start.4 = (s32[512]{0:T(512)S(1)}, s32[512]{0:T(512)}, u32[]{:S(2)}) copy-start(s32[512]{0:T(512)} %cells_ref.1) | copy-start | bytes 6148
  18.2 1.6 %collective-permute-start.1 = (f32[5,96,128]{2,1,0:T(8,128)S(1)}, f32[5,96,128]{2,1,0:T(8,128)S(1)}, u32[]{:S(2)}, u32[]{:S(2)}) collective-permute-start(f32[5,96,128]{2,1,0:T(8,128)S(1)} %get-tuple-element.10._), channel_id=1, source_target_pairs={{0,1},{1,0},{2,3},{3,2},{4,5},{5,4},{6,7},{7,6},{8,9},{9,8},{10,11... | collective-permute-start | bytes 737288 | tf_op jit(solution)/shard_map/ppermute | solution.py:629
  19.9 24.8 %collective-permute-start.2 = (f32[5,112,128]{2,1,0:T(8,128)S(1)}, f32[5,112,128]{2,1,0:T(8,128)S(1)}, u32[]{:S(2)}, u32[]{:S(2)}) collective-permute-start(f32[5,112,128]{2,1,0:T(8,128)S(1)} %pad_maximum_fusion.refs_2_), channel_id=1, source_target_pairs={{1,2},{3,0},{2,1},{0,3},{5,6},{7,4},{6,5},{4,7},{9,10},{11,8},{10,... | collective-permute-start | bytes 860168 | tf_op jit(solution)/shard_map/ppermute | solution.py:631
  37.1 27.6 %all-to-all-start.1 = ((f32[8,16,128]{2,1,0:T(8,128)}), f32[8,16,128]{2,1,0:T(8,128)S(1)}, u32[]{:S(2)}, u32[]{:S(2)}) async-start(f32[8,16,128]{2,1,0:T(8,128)} %reduce_sum.9), calls=%async_computation.1 | async-start | bytes 131072 | tf_op jit(solution)/shard_map/all_to_all | solution.py:602
  44.7 19.9 %collective-permute-start.6 = (f32[5,16,128]{2,1,0:T(8,128)S(1)}, f32[5,16,128]{2,1,0:T(8,128)S(1)}, u32[]{:S(2)}, u32[]{:S(2)}) collective-permute-start(f32[5,16,128]{2,1,0:T(8,128)S(1)} %get-tuple-element.16), channel_id=1, source_target_pairs={{4,0},{8,4},{12,8},{16,12},{20,16},{24,20},{28,24},{5,1},{9,5},{13... | collective-permute-start | bytes 122888 | tf_op jit(solution)/shard_map/ppermute | solution.py:640
  46.0 19.1 %collective-permute-start.5 = (f32[5,16,128]{2,1,0:T(8,128)S(1)}, f32[5,16,128]{2,1,0:T(8,128)S(1)}, u32[]{:S(2)}, u32[]{:S(2)}) collective-permute-start(f32[5,16,128]{2,1,0:T(8,128)S(1)} %get-tuple-element.17), channel_id=1, source_target_pairs={{0,4},{4,8},{8,12},{12,16},{16,20},{20,24},{24,28},{1,5},{5,9},{9,... | collective-permute-start | bytes 122888 | tf_op jit(solution)/shard_map/ppermute | solution.py:639

commit v6 on v5

--- a/solution.py
+++ b/solution.py
@@ -529,28 +529,31 @@
 
     weight = basis_ref[sector + 2 * ROWS :, :]
 
-    def go(ref, spec_ref, slot):
-        for f in range(fields):
-            rows = slice(slot * CYCLES, (slot + 1) * CYCLES)
-            padded[f * CYCLES : (f + 1) * CYCLES, :] = spec_ref[f, rows, :] * weight
+    def go(ref, spec_ref):
+        for slot in range(2):
+            for f in range(fields):
+                rows = slice(slot * CYCLES, (slot + 1) * CYCLES)
+                at = (slot * fields + f) * CYCLES
+                padded[at : at + CYCLES, :] = spec_ref[f, rows, :] * weight
         smooth = lax.dot_general(
             basis_ref[ROWS : ROWS + sector, :], padded[...], (((1,), (1,)), ((), ())),
             precision=HIGHEST, preferred_element_type=jnp.float32,
         )
-        for f in range(fields):
-            inner = smooth if f == 0 else pltpu.roll(smooth, radial - CYCLES * f, 1)
-            out_ref[f, slot, :main, :] = part_ref[f, slot, :main, :] + jnp.where(
-                wide, ref[f, slot], inner[:main]
-            )
-            rest = inner[main:]
-            for g in range(groups):
-                moved = pltpu.roll(ref[f, slot, g * tail : (g + 1) * tail, :], CYCLES * (g + 1), 1)
-                rest = jnp.where(lane // CYCLES == g + 1, moved, rest)
-            out_ref[f, slot, main:, :] = part_ref[f, slot, main:, :] + rest
-
-    for k in range(2):
-        pl.when(step == 0)(lambda k=k: go(low_ref, spec_low, k))
-        pl.when(step == 1)(lambda k=k: go(high_ref, spec_high, k))
+        for slot in range(2):
+            for f in range(fields):
+                k = slot * fields + f
+                inner = smooth if k == 0 else pltpu.roll(smooth, radial - CYCLES * k, 1)
+                out_ref[f, slot, :main, :] = part_ref[f, slot, :main, :] + jnp.where(
+                    wide, ref[f, slot], inner[:main]
+                )
+                rest = inner[main:]
+                for g in range(groups):
+                    moved = pltpu.roll(ref[f, slot, g * tail : (g + 1) * tail, :], CYCLES * (g + 1), 1)
+                    rest = jnp.where(lane // CYCLES == g + 1, moved, rest)
+                out_ref[f, slot, main:, :] = part_ref[f, slot, main:, :] + rest
+
+    pl.when(step == 0)(lambda: go(low_ref, spec_low))
+    pl.when(step == 1)(lambda: go(high_ref, spec_high))
 
 
 def add_edges(section, low, high, spec_low, spec_high, basis, sums, observers):

time: 70.9 us -> 70.5 us (level)
  Pallas kernels: 30.9 us -> 28.8 us
  waiting for transfers between devices: 1.74 us -> 3.02 us
    pallas_call x1, Pallas kernels: 4.38 us -> 2.63 us  [panel_sums(): pl.pallas_call(functools.partial(panel_kernel, lax.axis_size('ax'), lax.a...]
    all_to_all x1, waiting for transfers between devices: 0.01 us -> 1.23 us  [exchanged_sums(): return lax.all_to_all(blocks, 'ax', split_axis=0, concat_axis=0, tiled=True)]
  transfers between devices with their start and end apart: 8 -> 8, of which waited for: 2 -> 3; matrix products, arithmetic and copies ran while one was open for 4% -> 4% of each run, Pallas kernels for 33% -> 30%
where the time goes in v6:
time: 70.5 us; the launch traced here: 69.3 us
  Pallas kernels  28.8 us (41%)
  starting transfers between devices  21.4 us (30%)
  blocking collectives  9.53 us (14%)
  local copies, waits for them, and re-layouts  3.44 us (5%)
  waiting for transfers between devices  3.02 us (4%)
  other arithmetic  1.68 us (2%)
  between operations  1.47 us (2%)
    pallas_call x1, Pallas kernels, local_section(): pl.pallas_call(functools.partial(section_kernel, 2.0 * math.pi / length),...  14.1 us
    all_to_all x1, blocking collectives, exchanged_sums(): lax.all_to_all(blocks, 'az', split_axis=0, concat_axis=0, tiled=True)  9.53 us
    all_to_all x1, starting transfers between devices, exchanged_sums(): return lax.all_to_all(blocks, 'ax', split_axis=0, concat_axis=0, tiled=True)  7.62 us
    ppermute x1, starting transfers between devices, on_device(): spec_low = lax.ppermute(outside[:, :2 * CYCLES], 'ax', up)  4.55 us
    ppermute x1, starting transfers between devices, on_device(): low = lax.ppermute(send_up, 'ax', up)  4.46 us
    pallas_call x1, Pallas kernels, add_edges(): pl.pallas_call(add_kernel, grid_spec=pltpu.PrefetchScalarGridSpec(num_sca...  4.27 us
    pallas_call x1, Pallas kernels, inner_terms(): pl.pallas_call(functools.partial(inner_kernel, 2.0 * math.pi / length), g...  4.22 us
    pallas_call x1, Pallas kernels, edge_terms(): pl.pallas_call(edge_kernel, grid_spec=pltpu.PrefetchScalarGridSpec(num_sc...  3.64 us
  transfers between devices with their start and end apart: 8, of which 3 were waited for; matrix products, arithmetic and copies ran while one was open for 4% of the time, Pallas kernels for 30%

profile of v6, /device:TPU:0, one launch (start us, length us, event | category | flops | bytes accessed | tf_op | source)
XLA Modules:
  0.0 69.3 jit_solution(4540667913675600601)
XLA Ops:
  0.6 0.0 copy-start.5
  0.6 3.6 %edge_terms.1 = (f32[5,2,240,128]{3,2,1,0:T(8,128)}, f32[5,2,240,128]{3,2,1,0:T(8,128)}, f32[5,16,128]{2,1,0:T(8,128)S(1)}) custom-call(s32[1]{0:T(128)} %bitcast.az_ref.refs_0_, f32[5,8,256,128]{3,2,1,0:T(8,128)} %refs_1_.3, f32[5,8,256,128]{3,2,1,0:T(8,128)} %refs_1_.3, f32[5,8,256,128]{3,2,1,0:T(8,128)} %refs_1_.3), custom_call_target="tpu_custom_call" | custom-call | flops 13107200 | bytes 5242880 | tf_op jit(solution)/shard_map/edge_terms/pallas_call | solution.py:120
  4.3 0.5 collective-permute-start
  4.7 4.5 %collective-permute-start.3 = (f32[5,2,240,128]{3,2,1,0:T(8,128)}, f32[5,2,240,128]{3,2,1,0:T(8,128)S(1)}, u32[]{:S(2)}, u32[]{:S(2)}) collective-permute-start(f32[5,2,240,128]{3,2,1,0:T(8,128)} %get-tuple-element.12), channel_id=1, source_target_pairs={{0,4},{4,8},{8,12},{12,16},{16,20},{20,24},{24,28},{1,5},{5,9},{9,... | collective-permute-start | bytes 3686408 | tf_op jit(solution)/shard_map/ppermute | solution.py:624
  9.2 1.3 %collective-permute-start.4 = (f32[5,2,240,128]{3,2,1,0:T(8,128)}, f32[5,2,240,128]{3,2,1,0:T(8,128)S(1)}, u32[]{:S(2)}, u32[]{:S(2)}) collective-permute-start(f32[5,2,240,128]{3,2,1,0:T(8,128)} %get-tuple-element.13), channel_id=1, source_target_pairs={{4,0},{8,4},{12,8},{16,12},{20,16},{24,20},{28,24},{5,1},{9,5},{13... | collective-permute-start | bytes 3686408 | tf_op jit(solution)/shard_map/ppermute | solution.py:625
  10.5 0.9 %constant_dynamic-slice_fusion = f32[272,128]{1,0:T(8,128)S(1)} fusion(f32[1040,128]{1,0:T(8,128)} %constant.16.clone, s32[]{:T(128)S(6)} %select_n.3), kind=kLoop, calls=%fused_computation.3 | loop fusion | bytes 278532 | tf_op jit(solution)/shard_map/dynamic_slice | solution.py:618
  11.4 0.0 copy-done.5
  11.5 0.0 collective-permute-done.refs_4_
  11.5 0.0 copy-start
  11.5 2.5 %copy-done = f32[5,8,256,128]{3,2,1,0:T(8,128)S(1)} copy-done((f32[5,8,256,128]{3,2,1,0:T(8,128)S(1)}, f32[5,8,256,128]{3,2,1,0:T(8,128)}, u32[]{:S(2)}) %copy-start) | copy-done | bytes 5242904
  14.0 4.2 %inner_terms.1 = (f32[5,96,128]{2,1,0:T(8,128)S(1)}, f32[5,16,128]{2,1,0:T(8,128)S(1)}) custom-call(s32[1]{0:T(128)} %bitcast.az_ref.refs_0_, f32[5,8,256,128]{3,2,1,0:T(8,128)S(1)} %copy-done, f32[5,8,256,128]{3,2,1,0:T(8,128)S(1)} %copy-done, f32[280,128]{1,0:T(8,128)S(1)} %pad_maximum_fusion.1.refs_3_.refs_6_.basis_ref, ...), custom_call_target="tpu_custom_call" | custom-call | flops 251658240 | bytes 5242880 | tf_op jit(solution)/shard_map/inner_terms/pallas_call | solution.py:255
  18.2 0.0 copy-start.2
  18.2 0.0 copy-start.3
  18.2 0.0 copy-start.4
  18.2 0.3 collective-permute-start.1
  18.5 1.3 %collective-permute-done.1 = f32[5,96,128]{2,1,0:T(8,128)S(1)} collective-permute-done((f32[5,96,128]{2,1,0:T(8,128)S(1)}, f32[5,96,128]{2,1,0:T(8,128)S(1)}, u32[]{:S(2)}, u32[]{:S(2)}) %collective-permute-start.1) | collective-permute-done | bytes 245792 | tf_op jit(solution)/shard_map/ppermute | solution.py:632
  19.9 1.4 %collective-permute-start.2 = (f32[5,112,128]{2,1,0:T(8,128)S(1)}, f32[5,112,128]{2,1,0:T(8,128)S(1)}, u32[]{:S(2)}, u32[]{:S(2)}) collective-permute-start(f32[5,112,128]{2,1,0:T(8,128)S(1)} %pad_maximum_fusion.refs_2_), channel_id=1, source_target_pairs={{1,2},{3,0},{2,1},{0,3},{5,6},{7,4},{6,5},{4,7},{9,10},{11,8},{10,... | collective-permute-start | bytes 860168 | tf_op jit(solution)/shard_map/ppermute | solution.py:634
  21.9 0.0 copy-done.1
  22.0 2.6 %panel_sums.1 = f32[32,16,128]{2,1,0:T(8,128)S(1)} custom-call(s32[512]{0:T(512)S(1)} %copy-done.4, s32[1]{0:T(128)S(6)} %copy.11.count_ref, s32[1,512]{1,0:T(1,128)S(1)} %bitcast.11, f32[5,2048,128]{2,1,0:T(8,128)S(1)} %bitcast.7, s32[64,512]{1,0:T(8,128)S(1)} %bitcast.9, f32[64,512]{1,0:T(8,128)S(1)} %bitcast.10, f32[5,96,128]{2,1,0:T(8,128)S(1)} %get-tuple-element.10._), custom_call_target="tpu_custom_call" | custom-call | flops 268435456 | bytes 5242880 | tf_op jit(solution)/shard_map/panel_sums/pallas_call | solution.py:352
  24.6 9.5 %all_to_all.10 = f32[4,8,16,128]{3,2,1,0:T(8,128)} all-to-all(f32[4,8,16,128]{3,2,1,0:T(8,128)S(1)} %bitcast.8), channel_id=1, replica_groups=mesh['ax'=8,'az'=4] {'az'}, dimensions={0} | all-to-all | bytes 524288 | tf_op jit(solution)/shard_map/all_to_all | solution.py:604
  34.1 1.6 %reduce_sum.9 = f32[8,16,128]{2,1,0:T(8,128)} reduce(f32[4,8,16,128]{3,2,1,0:T(8,128)} %all_to_all.10, f32[]{:T(128)} %constant.6.clone.1), dimensions={0}, to_apply=%region_0.0 | reduce | flops 49152 | bytes 327684 | tf_op jit(solution)/shard_map/reduce_sum | solution.py:604
  35.7 7.6 %all-to-all-start.1 = ((f32[8,16,128]{2,1,0:T(8,128)}), f32[8,16,128]{2,1,0:T(8,128)S(1)}, u32[]{:S(2)}, u32[]{:S(2)}) async-start(f32[8,16,128]{2,1,0:T(8,128)} %reduce_sum.9), calls=%async_computation.1 | async-start | bytes 131072 | tf_op jit(solution)/shard_map/all_to_all | solution.py:605
  43.4 0.0 collective-permute-done.2.refs_3_.refs_5_
  43.4 1.3 %collective-permute-start.6 = (f32[5,16,128]{2,1,0:T(8,128)S(1)}, f32[5,16,128]{2,1,0:T(8,128)S(1)}, u32[]{:S(2)}, u32[]{:S(2)}) collective-permute-start(f32[5,16,128]{2,1,0:T(8,128)S(1)} %get-tuple-element.16), channel_id=1, source_target_pairs={{4,0},{8,4},{12,8},{16,12},{20,16},{24,20},{28,24},{5,1},{9,5},{13... | collective-permute-start | bytes 122888 | tf_op jit(solution)/shard_map/ppermute | solution.py:643
  44.7 4.5 %collective-permute-start.5 = (f32[5,16,128]{2,1,0:T(8,128)S(1)}, f32[5,16,128]{2,1,0:T(8,128)S(1)}, u32[]{:S(2)}, u32[]{:S(2)}) collective-permute-start(f32[5,16,128]{2,1,0:T(8,128)S(1)} %get-tuple-element.17), channel_id=1, source_target_pairs={{0,4},{4,8},{8,12},{12,16},{16,20},{20,24},{24,28},{1,5},{5,9},{9,... | collective-permute-start | bytes 122888 | tf_op jit(solution)/shard_map/ppermute | solution.py:642
  49.3 14.1 %local_section.1.part_ref = f32[5,8,256,128]{3,2,1,0:T(8,128)} custom-call(s32[1]{0:T(128)} %bitcast.az_ref.refs_0_, f32[5,8,256,128]{3,2,1,0:T(8,128)} %refs_1_.3, f32[5,112,128]{2,1,0:T(8,128)S(1)} %pad_maximum_fusion.refs_2_, f32[5,112,128]{2,1,0:T(8,128)S(1)} %collective-permute-done.2.refs_3_.refs_5_, f32[5,16,128]{2,1,0:T(8,128)S(1)} %collective-permute-done.refs_4_, ...), custom_call_target="tpu_custom_call" | custom-call | flops 157286400 | bytes 52428800 | tf_op jit(solution)/shard_map/local_section/pallas_call | solution.py:477
  63.3 1.2 %all-to-all-done.1.sums_ref = f32[8,16,128]{2,1,0:T(8,128)S(1)} async-done(((f32[8,16,128]{2,1,0:T(8,128)}), f32[8,16,128]{2,1,0:T(8,128)S(1)}, u32[]{:S(2)}, u32[]{:S(2)}) %all-to-all-start.1) | async-done | bytes 65568 | tf_op jit(solution)/shard_map/all_to_all | solution.py:605
  64.6 0.0 collective-permute-done.6.spec_high
  64.6 0.5 collective-permute-done.5.spec_low
  65.1 0.0 collective-permute-done.3.low_ref
  65.1 0.0 collective-permute-done.4.high_ref
  65.1 4.3 %add_edges.1 = (f32[5,8,256,128]{3,2,1,0:T(8,128)}, f32[32,64]{1,0:T(8,128)}) custom-call(f32[5,8,256,128]{3,2,1,0:T(8,128)} %local_section.1.part_ref, f32[5,2,240,128]{3,2,1,0:T(8,128)S(1)} %collective-permute-done.3.low_ref, f32[5,2,240,128]{3,2,1,0:T(8,128)S(1)} %collective-permute-done.4.high_ref, ...), custom_call_target="tpu_custom_call", output_to_operand_aliasing={{0}: (0, {})} | custom-call | flops 1310720 | bytes 7864320 | tf_op jit(solution)/shard_map/add_edges/pallas_call | solution.py:566
  (9 shorter events, 0.1 us)
Async XLA Ops:
  0.6 10.8 %copy-start.5 = (f32[8,128]{1,0:T(8,128)S(1)}, f32[8,128]{1,0:T(8,128)}, u32[]{:S(2)}) copy-start(f32[8,128]{1,0:T(8,128)} %constant.17.clone) | copy-start | bytes 12292
  4.3 7.2 %collective-permute-start = (f32[5,16,128]{2,1,0:T(8,128)S(1)}, f32[5,16,128]{2,1,0:T(8,128)S(1)}, u32[]{:S(2)}, u32[]{:S(2)}) collective-permute-start(f32[5,16,128]{2,1,0:T(8,128)S(1)} %get-tuple-element.9), channel_id=1, source_target_pairs={{0,1},{1,0},{2,3},{3,2},{4,5},{5,4},{6,7},{7,6},{8,9},{9,8},{10,11... | collective-permute-start | bytes 122888 | tf_op jit(solution)/shard_map/ppermute | solution.py:623
  4.7 60.3 %collective-permute-start.3 = (f32[5,2,240,128]{3,2,1,0:T(8,128)}, f32[5,2,240,128]{3,2,1,0:T(8,128)S(1)}, u32[]{:S(2)}, u32[]{:S(2)}) collective-permute-start(f32[5,2,240,128]{3,2,1,0:T(8,128)} %get-tuple-element.12), channel_id=1, source_target_pairs={{0,4},{4,8},{8,12},{12,16},{16,20},{20,24},{24,28},{1,5},{5,9},{9,... | collective-permute-start | bytes 3686408 | tf_op jit(solution)/shard_map/ppermute | solution.py:624
  9.2 55.9 %collective-permute-start.4 = (f32[5,2,240,128]{3,2,1,0:T(8,128)}, f32[5,2,240,128]{3,2,1,0:T(8,128)S(1)}, u32[]{:S(2)}, u32[]{:S(2)}) collective-permute-start(f32[5,2,240,128]{3,2,1,0:T(8,128)} %get-tuple-element.13), channel_id=1, source_target_pairs={{4,0},{8,4},{12,8},{16,12},{20,16},{24,20},{28,24},{5,1},{9,5},{13... | collective-permute-start | bytes 3686408 | tf_op jit(solution)/shard_map/ppermute | solution.py:625
  11.5 2.5 %copy-start = (f32[5,8,256,128]{3,2,1,0:T(8,128)S(1)}, f32[5,8,256,128]{3,2,1,0:T(8,128)}, u32[]{:S(2)}) copy-start(f32[5,8,256,128]{3,2,1,0:T(8,128)} %refs_1_.3) | copy-start | bytes 15728644
  14.0 8.0 %copy-start.1 = (f32[5,8,256,128]{3,2,1,0:T(8,128)S(1)}, f32[5,8,256,128]{3,2,1,0:T(8,128)}, u32[]{:S(2)}) copy-start(f32[5,8,256,128]{3,2,1,0:T(8,128)} %refs_1_.3) | copy-start | bytes 15728644
  18.2 3.8 %copy-start.2 = (s32[512,64]{0,1:T(8,128)S(1)}, s32[512,64]{0,1:T(8,128)}, u32[]{:S(2)}) copy-start(s32[512,64]{0,1:T(8,128)} %param.10) | copy-start | bytes 393220
  18.2 3.8 %copy-start.3 = (f32[512,64]{0,1:T(8,128)S(1)}, f32[512,64]{0,1:T(8,128)}, u32[]{:S(2)}) copy-start(f32[512,64]{0,1:T(8,128)} %param.11) | copy-start | bytes 393220
  18.2 3.7 %copy-start.4 = (s32[512]{0:T(512)S(1)}, s32[512]{0:T(512)}, u32[]{:S(2)}) copy-start(s32[512]{0:T(512)} %cells_ref.1) | copy-start | bytes 6148
  18.2 1.6 %collective-permute-start.1 = (f32[5,96,128]{2,1,0:T(8,128)S(1)}, f32[5,96,128]{2,1,0:T(8,128)S(1)}, u32[]{:S(2)}, u32[]{:S(2)}) collective-permute-start(f32[5,96,128]{2,1,0:T(8,128)S(1)} %get-tuple-element.10._), channel_id=1, source_target_pairs={{0,1},{1,0},{2,3},{3,2},{4,5},{5,4},{6,7},{7,6},{8,9},{9,8},{10,11... | collective-permute-start | bytes 737288 | tf_op jit(solution)/shard_map/ppermute | solution.py:632
  19.9 23.5 %collective-permute-start.2 = (f32[5,112,128]{2,1,0:T(8,128)S(1)}, f32[5,112,128]{2,1,0:T(8,128)S(1)}, u32[]{:S(2)}, u32[]{:S(2)}) collective-permute-start(f32[5,112,128]{2,1,0:T(8,128)S(1)} %pad_maximum_fusion.refs_2_), channel_id=1, source_target_pairs={{1,2},{3,0},{2,1},{0,3},{5,6},{7,4},{6,5},{4,7},{9,10},{11,8},{10,... | collective-permute-start | bytes 860168 | tf_op jit(solution)/shard_map/ppermute | solution.py:634
  35.7 28.8 %all-to-all-start.1 = ((f32[8,16,128]{2,1,0:T(8,128)}), f32[8,16,128]{2,1,0:T(8,128)S(1)}, u32[]{:S(2)}, u32[]{:S(2)}) async-start(f32[8,16,128]{2,1,0:T(8,128)} %reduce_sum.9), calls=%async_computation.1 | async-start | bytes 131072 | tf_op jit(solution)/shard_map/all_to_all | solution.py:605
  43.4 21.2 %collective-permute-start.6 = (f32[5,16,128]{2,1,0:T(8,128)S(1)}, f32[5,16,128]{2,1,0:T(8,128)S(1)}, u32[]{:S(2)}, u32[]{:S(2)}) collective-permute-start(f32[5,16,128]{2,1,0:T(8,128)S(1)} %get-tuple-element.16), channel_id=1, source_target_pairs={{4,0},{8,4},{12,8},{16,12},{20,16},{24,20},{28,24},{5,1},{9,5},{13... | collective-permute-start | bytes 122888 | tf_op jit(solution)/shard_map/ppermute | solution.py:643
  44.7 20.4 %collective-permute-start.5 = (f32[5,16,128]{2,1,0:T(8,128)S(1)}, f32[5,16,128]{2,1,0:T(8,128)S(1)}, u32[]{:S(2)}, u32[]{:S(2)}) collective-permute-start(f32[5,16,128]{2,1,0:T(8,128)S(1)} %get-tuple-element.17), channel_id=1, source_target_pairs={{0,4},{4,8},{8,12},{12,16},{16,20},{20,24},{24,28},{1,5},{5,9},{9,... | collective-permute-start | bytes 122888 | tf_op jit(solution)/shard_map/ppermute | solution.py:642

commit v7 on v6

--- a/solution.py
+++ b/solution.py
@@ -570,8 +570,8 @@
             grid=(2,),
             in_specs=[
                 plane,
-                full(low),
-                full(high),
+                pl.BlockSpec(memory_space=pltpu.VMEM),
+                pl.BlockSpec(memory_space=pltpu.VMEM),
                 full(spec_low),
                 full(spec_high),
                 full(basis),

time: 70.5 us -> 70.5 us (level)
  no operation moved by 1% of the time
where the time goes in v7:
time: 70.5 us; the launch traced here: 69.3 us
  Pallas kernels  28.8 us (41%)
  starting transfers between devices  22 us (31%)
  blocking collectives  9.1 us (13%)
  local copies, waits for them, and re-layouts  3.44 us (5%)
  waiting for transfers between devices  2.85 us (4%)
  other arithmetic  1.68 us (2%)
  between operations  1.47 us (2%)
    pallas_call x1, Pallas kernels, local_section(): pl.pallas_call(functools.partial(section_kernel, 2.0 * math.pi / length),...  14.1 us
    all_to_all x1, blocking collectives, exchanged_sums(): lax.all_to_all(blocks, 'az', split_axis=0, concat_axis=0, tiled=True)  9.1 us
    all_to_all x1, starting transfers between devices, exchanged_sums(): return lax.all_to_all(blocks, 'ax', split_axis=0, concat_axis=0, tiled=True)  8.31 us
    ppermute x1, starting transfers between devices, on_device(): spec_low = lax.ppermute(outside[:, :2 * CYCLES], 'ax', up)  4.55 us
    ppermute x1, starting transfers between devices, on_device(): low = lax.ppermute(send_up, 'ax', up)  4.46 us
    pallas_call x1, Pallas kernels, add_edges(): pl.pallas_call(add_kernel, grid_spec=pltpu.PrefetchScalarGridSpec(num_sca...  4.27 us
    pallas_call x1, Pallas kernels, inner_terms(): pl.pallas_call(functools.partial(inner_kernel, 2.0 * math.pi / length), g...  4.22 us
    pallas_call x1, Pallas kernels, edge_terms(): pl.pallas_call(edge_kernel, grid_spec=pltpu.PrefetchScalarGridSpec(num_sc...  3.64 us
  transfers between devices with their start and end apart: 8, of which 3 were waited for; matrix products, arithmetic and copies ran while one was open for 4% of the time, Pallas kernels for 30%

profile of v7, /device:TPU:0, one launch (start us, length us, event | category | flops | bytes accessed | tf_op | source)
XLA Modules:
  0.0 69.3 jit_solution(4540667913675600601)
XLA Ops:
  0.6 0.0 copy-start.5
  0.6 3.6 %edge_terms.1 = (f32[5,2,240,128]{3,2,1,0:T(8,128)}, f32[5,2,240,128]{3,2,1,0:T(8,128)}, f32[5,16,128]{2,1,0:T(8,128)S(1)}) custom-call(s32[1]{0:T(128)} %bitcast.az_ref.refs_0_, f32[5,8,256,128]{3,2,1,0:T(8,128)} %refs_1_.3, f32[5,8,256,128]{3,2,1,0:T(8,128)} %refs_1_.3, f32[5,8,256,128]{3,2,1,0:T(8,128)} %refs_1_.3), custom_call_target="tpu_custom_call" | custom-call | flops 13107200 | bytes 5242880 | tf_op jit(solution)/shard_map/edge_terms/pallas_call | solution.py:120
  4.3 0.5 collective-permute-start
  4.7 4.5 %collective-permute-start.3 = (f32[5,2,240,128]{3,2,1,0:T(8,128)}, f32[5,2,240,128]{3,2,1,0:T(8,128)S(1)}, u32[]{:S(2)}, u32[]{:S(2)}) collective-permute-start(f32[5,2,240,128]{3,2,1,0:T(8,128)} %get-tuple-element.12), channel_id=1, source_target_pairs={{0,4},{4,8},{8,12},{12,16},{16,20},{20,24},{24,28},{1,5},{5,9},{9,... | collective-permute-start | bytes 3686408 | tf_op jit(solution)/shard_map/ppermute | solution.py:624
  9.2 1.3 %collective-permute-start.4 = (f32[5,2,240,128]{3,2,1,0:T(8,128)}, f32[5,2,240,128]{3,2,1,0:T(8,128)S(1)}, u32[]{:S(2)}, u32[]{:S(2)}) collective-permute-start(f32[5,2,240,128]{3,2,1,0:T(8,128)} %get-tuple-element.13), channel_id=1, source_target_pairs={{4,0},{8,4},{12,8},{16,12},{20,16},{24,20},{28,24},{5,1},{9,5},{13... | collective-permute-start | bytes 3686408 | tf_op jit(solution)/shard_map/ppermute | solution.py:625
  10.5 0.9 %constant_dynamic-slice_fusion = f32[272,128]{1,0:T(8,128)S(1)} fusion(f32[1040,128]{1,0:T(8,128)} %constant.16.clone, s32[]{:T(128)S(6)} %select_n.3), kind=kLoop, calls=%fused_computation.3 | loop fusion | bytes 278532 | tf_op jit(solution)/shard_map/dynamic_slice | solution.py:618
  11.4 0.0 copy-done.5
  11.5 0.0 collective-permute-done.refs_4_
  11.5 0.0 copy-start
  11.5 2.5 %copy-done = f32[5,8,256,128]{3,2,1,0:T(8,128)S(1)} copy-done((f32[5,8,256,128]{3,2,1,0:T(8,128)S(1)}, f32[5,8,256,128]{3,2,1,0:T(8,128)}, u32[]{:S(2)}) %copy-start) | copy-done | bytes 5242904
  14.0 4.2 %inner_terms.1 = (f32[5,96,128]{2,1,0:T(8,128)S(1)}, f32[5,16,128]{2,1,0:T(8,128)S(1)}) custom-call(s32[1]{0:T(128)} %bitcast.az_ref.refs_0_, f32[5,8,256,128]{3,2,1,0:T(8,128)S(1)} %copy-done, f32[5,8,256,128]{3,2,1,0:T(8,128)S(1)} %copy-done, f32[280,128]{1,0:T(8,128)S(1)} %pad_maximum_fusion.1.refs_3_.refs_6_.basis_ref, ...), custom_call_target="tpu_custom_call" | custom-call | flops 251658240 | bytes 5242880 | tf_op jit(solution)/shard_map/inner_terms/pallas_call | solution.py:255
  18.2 0.0 copy-start.2
  18.2 0.0 copy-start.3
  18.2 0.0 copy-start.4
  18.2 0.3 collective-permute-start.1
  18.5 1.3 %collective-permute-done.1 = f32[5,96,128]{2,1,0:T(8,128)S(1)} collective-permute-done((f32[5,96,128]{2,1,0:T(8,128)S(1)}, f32[5,96,128]{2,1,0:T(8,128)S(1)}, u32[]{:S(2)}, u32[]{:S(2)}) %collective-permute-start.1) | collective-permute-done | bytes 245792 | tf_op jit(solution)/shard_map/ppermute | solution.py:632
  19.9 1.4 %collective-permute-start.2 = (f32[5,112,128]{2,1,0:T(8,128)S(1)}, f32[5,112,128]{2,1,0:T(8,128)S(1)}, u32[]{:S(2)}, u32[]{:S(2)}) collective-permute-start(f32[5,112,128]{2,1,0:T(8,128)S(1)} %pad_maximum_fusion.refs_2_), channel_id=1, source_target_pairs={{1,2},{3,0},{2,1},{0,3},{5,6},{7,4},{6,5},{4,7},{9,10},{11,8},{10,... | collective-permute-start | bytes 860168 | tf_op jit(solution)/shard_map/ppermute | solution.py:634
  21.9 0.0 copy-done.1
  22.0 2.5 %panel_sums.1 = f32[32,16,128]{2,1,0:T(8,128)S(1)} custom-call(s32[512]{0:T(512)S(1)} %copy-done.4, s32[1]{0:T(128)S(6)} %copy.11.count_ref, s32[1,512]{1,0:T(1,128)S(1)} %bitcast.11, f32[5,2048,128]{2,1,0:T(8,128)S(1)} %bitcast.7, s32[64,512]{1,0:T(8,128)S(1)} %bitcast.9, f32[64,512]{1,0:T(8,128)S(1)} %bitcast.10, f32[5,96,128]{2,1,0:T(8,128)S(1)} %get-tuple-element.10._), custom_call_target="tpu_custom_call" | custom-call | flops 268435456 | bytes 5242880 | tf_op jit(solution)/shard_map/panel_sums/pallas_call | solution.py:352
  24.5 9.1 %all_to_all.10 = f32[4,8,16,128]{3,2,1,0:T(8,128)} all-to-all(f32[4,8,16,128]{3,2,1,0:T(8,128)S(1)} %bitcast.8), channel_id=1, replica_groups=mesh['ax'=8,'az'=4] {'az'}, dimensions={0} | all-to-all | bytes 524288 | tf_op jit(solution)/shard_map/all_to_all | solution.py:604
  33.6 1.6 %reduce_sum.9 = f32[8,16,128]{2,1,0:T(8,128)} reduce(f32[4,8,16,128]{3,2,1,0:T(8,128)} %all_to_all.10, f32[]{:T(128)} %constant.6.clone.1), dimensions={0}, to_apply=%region_0.0 | reduce | flops 49152 | bytes 327684 | tf_op jit(solution)/shard_map/reduce_sum | solution.py:604
  35.2 8.3 %all-to-all-start.1 = ((f32[8,16,128]{2,1,0:T(8,128)}), f32[8,16,128]{2,1,0:T(8,128)S(1)}, u32[]{:S(2)}, u32[]{:S(2)}) async-start(f32[8,16,128]{2,1,0:T(8,128)} %reduce_sum.9), calls=%async_computation.1 | async-start | bytes 131072 | tf_op jit(solution)/shard_map/all_to_all | solution.py:605
  43.5 0.0 collective-permute-done.2.refs_3_.refs_5_
  43.6 1.3 %collective-permute-start.6 = (f32[5,16,128]{2,1,0:T(8,128)S(1)}, f32[5,16,128]{2,1,0:T(8,128)S(1)}, u32[]{:S(2)}, u32[]{:S(2)}) collective-permute-start(f32[5,16,128]{2,1,0:T(8,128)S(1)} %get-tuple-element.16), channel_id=1, source_target_pairs={{4,0},{8,4},{12,8},{16,12},{20,16},{24,20},{28,24},{5,1},{9,5},{13... | collective-permute-start | bytes 122888 | tf_op jit(solution)/shard_map/ppermute | solution.py:643
  44.9 4.5 %collective-permute-start.5 = (f32[5,16,128]{2,1,0:T(8,128)S(1)}, f32[5,16,128]{2,1,0:T(8,128)S(1)}, u32[]{:S(2)}, u32[]{:S(2)}) collective-permute-start(f32[5,16,128]{2,1,0:T(8,128)S(1)} %get-tuple-element.17), channel_id=1, source_target_pairs={{0,4},{4,8},{8,12},{12,16},{16,20},{20,24},{24,28},{1,5},{5,9},{9,... | collective-permute-start | bytes 122888 | tf_op jit(solution)/shard_map/ppermute | solution.py:642
  49.4 14.1 %local_section.1.part_ref = f32[5,8,256,128]{3,2,1,0:T(8,128)} custom-call(s32[1]{0:T(128)} %bitcast.az_ref.refs_0_, f32[5,8,256,128]{3,2,1,0:T(8,128)} %refs_1_.3, f32[5,112,128]{2,1,0:T(8,128)S(1)} %pad_maximum_fusion.refs_2_, f32[5,112,128]{2,1,0:T(8,128)S(1)} %collective-permute-done.2.refs_3_.refs_5_, f32[5,16,128]{2,1,0:T(8,128)S(1)} %collective-permute-done.refs_4_, ...), custom_call_target="tpu_custom_call" | custom-call | flops 157286400 | bytes 52428800 | tf_op jit(solution)/shard_map/local_section/pallas_call | solution.py:477
  63.5 1.1 %all-to-all-done.1.sums_ref = f32[8,16,128]{2,1,0:T(8,128)S(1)} async-done(((f32[8,16,128]{2,1,0:T(8,128)}), f32[8,16,128]{2,1,0:T(8,128)S(1)}, u32[]{:S(2)}, u32[]{:S(2)}) %all-to-all-start.1) | async-done | bytes 65568 | tf_op jit(solution)/shard_map/all_to_all | solution.py:605
  64.6 0.0 collective-permute-done.6.spec_high
  64.6 0.5 collective-permute-done.5.spec_low
  65.1 0.0 collective-permute-done.3.low_ref
  65.1 0.0 collective-permute-done.4.high_ref
  65.1 4.3 %add_edges.1 = (f32[5,8,256,128]{3,2,1,0:T(8,128)}, f32[32,64]{1,0:T(8,128)}) custom-call(f32[5,8,256,128]{3,2,1,0:T(8,128)} %local_section.1.part_ref, f32[5,2,240,128]{3,2,1,0:T(8,128)S(1)} %collective-permute-done.3.low_ref, f32[5,2,240,128]{3,2,1,0:T(8,128)S(1)} %collective-permute-done.4.high_ref, ...), custom_call_target="tpu_custom_call", output_to_operand_aliasing={{0}: (0, {})} | custom-call | flops 1310720 | bytes 7864320 | tf_op jit(solution)/shard_map/add_edges/pallas_call | solution.py:566
  (9 shorter events, 0.1 us)
Async XLA Ops:
  0.6 10.8 %copy-start.5 = (f32[8,128]{1,0:T(8,128)S(1)}, f32[8,128]{1,0:T(8,128)}, u32[]{:S(2)}) copy-start(f32[8,128]{1,0:T(8,128)} %constant.17.clone) | copy-start | bytes 12292
  4.3 7.2 %collective-permute-start = (f32[5,16,128]{2,1,0:T(8,128)S(1)}, f32[5,16,128]{2,1,0:T(8,128)S(1)}, u32[]{:S(2)}, u32[]{:S(2)}) collective-permute-start(f32[5,16,128]{2,1,0:T(8,128)S(1)} %get-tuple-element.9), channel_id=1, source_target_pairs={{0,1},{1,0},{2,3},{3,2},{4,5},{5,4},{6,7},{7,6},{8,9},{9,8},{10,11... | collective-permute-start | bytes 122888 | tf_op jit(solution)/shard_map/ppermute | solution.py:623
  4.7 60.3 %collective-permute-start.3 = (f32[5,2,240,128]{3,2,1,0:T(8,128)}, f32[5,2,240,128]{3,2,1,0:T(8,128)S(1)}, u32[]{:S(2)}, u32[]{:S(2)}) collective-permute-start(f32[5,2,240,128]{3,2,1,0:T(8,128)} %get-tuple-element.12), channel_id=1, source_target_pairs={{0,4},{4,8},{8,12},{12,16},{16,20},{20,24},{24,28},{1,5},{5,9},{9,... | collective-permute-start | bytes 3686408 | tf_op jit(solution)/shard_map/ppermute | solution.py:624
  9.2 55.9 %collective-permute-start.4 = (f32[5,2,240,128]{3,2,1,0:T(8,128)}, f32[5,2,240,128]{3,2,1,0:T(8,128)S(1)}, u32[]{:S(2)}, u32[]{:S(2)}) collective-permute-start(f32[5,2,240,128]{3,2,1,0:T(8,128)} %get-tuple-element.13), channel_id=1, source_target_pairs={{4,0},{8,4},{12,8},{16,12},{20,16},{24,20},{28,24},{5,1},{9,5},{13... | collective-permute-start | bytes 3686408 | tf_op jit(solution)/shard_map/ppermute | solution.py:625
  11.5 2.5 %copy-start = (f32[5,8,256,128]{3,2,1,0:T(8,128)S(1)}, f32[5,8,256,128]{3,2,1,0:T(8,128)}, u32[]{:S(2)}) copy-start(f32[5,8,256,128]{3,2,1,0:T(8,128)} %refs_1_.3) | copy-start | bytes 15728644
  14.0 8.0 %copy-start.1 = (f32[5,8,256,128]{3,2,1,0:T(8,128)S(1)}, f32[5,8,256,128]{3,2,1,0:T(8,128)}, u32[]{:S(2)}) copy-start(f32[5,8,256,128]{3,2,1,0:T(8,128)} %refs_1_.3) | copy-start | bytes 15728644
  18.2 3.8 %copy-start.2 = (s32[512,64]{0,1:T(8,128)S(1)}, s32[512,64]{0,1:T(8,128)}, u32[]{:S(2)}) copy-start(s32[512,64]{0,1:T(8,128)} %param.10) | copy-start | bytes 393220
  18.2 3.8 %copy-start.3 = (f32[512,64]{0,1:T(8,128)S(1)}, f32[512,64]{0,1:T(8,128)}, u32[]{:S(2)}) copy-start(f32[512,64]{0,1:T(8,128)} %param.11) | copy-start | bytes 393220
  18.2 3.7 %copy-start.4 = (s32[512]{0:T(512)S(1)}, s32[512]{0:T(512)}, u32[]{:S(2)}) copy-start(s32[512]{0:T(512)} %cells_ref.1) | copy-start | bytes 6148
  18.2 1.6 %collective-permute-start.1 = (f32[5,96,128]{2,1,0:T(8,128)S(1)}, f32[5,96,128]{2,1,0:T(8,128)S(1)}, u32[]{:S(2)}, u32[]{:S(2)}) collective-permute-start(f32[5,96,128]{2,1,0:T(8,128)S(1)} %get-tuple-element.10._), channel_id=1, source_target_pairs={{0,1},{1,0},{2,3},{3,2},{4,5},{5,4},{6,7},{7,6},{8,9},{9,8},{10,11... | collective-permute-start | bytes 737288 | tf_op jit(solution)/shard_map/ppermute | solution.py:632
  19.9 23.7 %collective-permute-start.2 = (f32[5,112,128]{2,1,0:T(8,128)S(1)}, f32[5,112,128]{2,1,0:T(8,128)S(1)}, u32[]{:S(2)}, u32[]{:S(2)}) collective-permute-start(f32[5,112,128]{2,1,0:T(8,128)S(1)} %pad_maximum_fusion.refs_2_), channel_id=1, source_target_pairs={{1,2},{3,0},{2,1},{0,3},{5,6},{7,4},{6,5},{4,7},{9,10},{11,8},{10,... | collective-permute-start | bytes 860168 | tf_op jit(solution)/shard_map/ppermute | solution.py:634
  35.2 29.3 %all-to-all-start.1 = ((f32[8,16,128]{2,1,0:T(8,128)}), f32[8,16,128]{2,1,0:T(8,128)S(1)}, u32[]{:S(2)}, u32[]{:S(2)}) async-start(f32[8,16,128]{2,1,0:T(8,128)} %reduce_sum.9), calls=%async_computation.1 | async-start | bytes 131072 | tf_op jit(solution)/shard_map/all_to_all | solution.py:605
  43.6 21.0 %collective-permute-start.6 = (f32[5,16,128]{2,1,0:T(8,128)S(1)}, f32[5,16,128]{2,1,0:T(8,128)S(1)}, u32[]{:S(2)}, u32[]{:S(2)}) collective-permute-start(f32[5,16,128]{2,1,0:T(8,128)S(1)} %get-tuple-element.16), channel_id=1, source_target_pairs={{4,0},{8,4},{12,8},{16,12},{20,16},{24,20},{28,24},{5,1},{9,5},{13... | collective-permute-start | bytes 122888 | tf_op jit(solution)/shard_map/ppermute | solution.py:643
  44.9 20.2 %collective-permute-start.5 = (f32[5,16,128]{2,1,0:T(8,128)S(1)}, f32[5,16,128]{2,1,0:T(8,128)S(1)}, u32[]{:S(2)}, u32[]{:S(2)}) collective-permute-start(f32[5,16,128]{2,1,0:T(8,128)S(1)} %get-tuple-element.17), channel_id=1, source_target_pairs={{0,4},{4,8},{8,12},{12,16},{16,20},{20,24},{24,28},{1,5},{5,9},{9,... | collective-permute-start | bytes 122888 | tf_op jit(solution)/shard_map/ppermute | solution.py:642
